TPU v7x, 32 devices: a whole 2x2x4 slice. The times are simulated.
32 devices in a mesh: section: 2 (over y), expert: 16 (over z, x, core).
Axes of the slice: x: 2, y: 2, z: 4, core: 2. Of those that a mesh axis runs over, the one named last changes fastest.
Arguments:
- front_rows: bfloat16 [2, 512, 1024], P('section', 'expert'), may hold values from -25 to 25
- front_routes: int32 [2, 512, 8], P('section', 'expert'), may hold values from 0 to 15, all different within a row; in each aligned block of 32 rows (0 to 31, 32 to 63, ..., all dimensions but the last counted through in order) at most 17 rows name the same one
- front_weights: float32 [2, 512, 8], P('section', 'expert'), may hold values from 0.1 to 1
- rear_rows: bfloat16 [2, 512, 1024], P('section', 'expert'), may hold values from -25 to 25
- rear_routes: int32 [2, 512, 8], P('section', 'expert'), may hold values from 0 to 15, all different within a row; in each aligned block of 32 rows (0 to 31, 32 to 63, ..., all dimensions but the last counted through in order) at most 17 rows name the same one
- rear_weights: float32 [2, 512, 8], P('section', 'expert'), may hold values from 0.1 to 1
- rear_cotangent: bfloat16 [2, 512, 1024], P('section', 'expert'), may hold values from -6 to 6
- norm_gain: float32 [2, 1024], P('section'), may hold values from 0.25 to 1.75
- gate_weight: bfloat16 [2, 16, 1024, 512], P('section', 'expert'), may hold values from -0.1875 to 0.1875
- up_weight: bfloat16 [2, 16, 1024, 512], P('section', 'expert'), may hold values from -0.1875 to 0.1875
- down_weight: bfloat16 [2, 16, 512, 1024], P('section', 'expert'), may hold values from -0.25 to 0.25
Outputs:
- sent_ahead: bfloat16 [2, 512, 1024], P('section', 'expert')
- sent_behind: bfloat16 [2, 512, 1024], P('section', 'expert')
Inputs may be any that keep to these rules, and one draw needn't show every extreme that they name: `front_routes`: A token's 8 experts differ; within each section's aligned blocks of 32 tokens no expert is chosen by more than 17 tokens, a bound that some block reaches. `rear_routes`: A token's 8 experts differ; within each section's aligned blocks of 32 tokens no expert is chosen by more than 17 tokens, a bound that some block reaches.
All inputs are finite; a program needn't handle non-finite values.
Results may differ from a plain program's by a relative error of at most 0.0065.
Values may be sent and summed in bfloat16 or wider, within the bound.
No kernel may reach another device: no remote copies, remote signals or barrier semaphores. Data moves between devices by JAX's collectives and lax.ppermute only.
A program may use at most 64 MiB of HBM per device.

v0:
```python
import functools

import jax
import jax.numpy as jnp
from jax import lax
from jax.experimental import pallas as pl
from jax.experimental.pallas import tpu as pltpu
from jax.sharding import PartitionSpec as P

epsilon = 1e-06
F32 = jnp.float32
BF16 = jnp.bfloat16
VMEM_LIMIT = 32 * 1024 * 1024


def call(kernel, name, shapes, *operands, scalars=0, flops=0):
    vmem = pl.BlockSpec(memory_space=pltpu.VMEM)
    smem = pl.BlockSpec(memory_space=pltpu.SMEM)
    shapes = [jax.ShapeDtypeStruct(shape, dtype) for shape, dtype in shapes]
    moved = sum(value.size * value.dtype.itemsize for value in [*operands, *shapes])
    return pl.pallas_call(
        kernel,
        out_shape=shapes,
        in_specs=[smem] * scalars + [vmem] * (len(operands) - scalars),
        out_specs=[vmem] * len(shapes),
        compiler_params=pltpu.CompilerParams(vmem_limit_bytes=VMEM_LIMIT),
        cost_estimate=pl.CostEstimate(flops=flops, bytes_accessed=moved, transcendentals=0),
        name=name,
    )(*operands)


def ring_of(experts):
    chips = experts // 2
    return list(range(0, chips, 2)) + list(range(1, chips, 2))[::-1]


def ring_pairs(experts, by):
    ring = ring_of(experts)
    chips = len(ring)
    return [
        (2 * ring[i] + c, 2 * ring[(i + by) % chips] + c) for i in range(chips) for c in range(2)
    ]


def table_lanes(experts):
    return -(-4 * experts // 128) * 128


def pack_kernel(experts, fr, frt, fw, rr, rrt, rw, ct, gain, msg):
    tokens, width = fr.shape
    lanes = table_lanes(experts)
    for j, rows in ((0, fr), (1, rr)):
        wide = rows[...].astype(F32)
        inverse = lax.rsqrt(jnp.mean(wide * wide, axis=-1, keepdims=True) + epsilon)
        msg[:, j * width : (j + 1) * width] = (wide * inverse * gain[...]).astype(BF16)
    msg[:, 2 * width : 3 * width] = ct[...]
    row = lax.broadcasted_iota(jnp.int32, (lanes, tokens), 0)
    table = jnp.zeros((lanes, tokens), F32)
    for group, (routes, weights) in enumerate(((frt, fw), (frt, fw), (rrt, rw), (rrt, rw))):
        for k in range(routes.shape[0]):
            hit = row == routes[k : k + 1, :] + group * experts
            weight = weights[k : k + 1, :]
            high = weight.astype(BF16).astype(F32)
            table = table + jnp.where(hit, high if group % 2 == 0 else weight - high, 0.0)
    msg[:, 3 * width :] = table.T.astype(BF16)


def sigmoid(v):
    return 1.0 / (1.0 + jnp.exp(-v))


def expert_kernel(experts, me, *refs):
    *parts, gate, up, down, gain, own, other = refs
    width = gate.shape[0]
    lanes = table_lanes(experts)
    expert = me[0]
    rows = jnp.concatenate([part[:, : 3 * width] for part in parts], axis=0)
    table = jnp.concatenate([part[:, 3 * width :] for part in parts], axis=0).astype(F32)
    lane = lax.broadcasted_iota(jnp.int32, table.shape, 1)
    mixing = []
    for j in range(2):
        hit = (lane == expert + 2 * j * experts) | (lane == expert + (2 * j + 1) * experts)
        mixing.append(jnp.sum(jnp.where(hit, table, 0.0), axis=-1, keepdims=True))
    across = (((1,), (1,)), ((), ()))

    def dot(a, b):
        return jnp.dot(a, b, preferred_element_type=F32)

    def dot_t(a, b):
        return lax.dot_general(a, b, across, preferred_element_type=F32)

    half = rows.shape[0] // 2

    def put(at, value):
        own[:, at : at + width] = value[:half].astype(own.dtype)
        other[:, at : at + width] = value[half:].astype(other.dtype)

    front, rear, cotangent = (rows[:, j * width : (j + 1) * width] for j in range(3))
    gate_value = dot(front, gate[...])
    up_value = dot(front, up[...])
    hidden = (gate_value * sigmoid(gate_value) * up_value).astype(BF16)
    put(0, dot(hidden, down[...]) * mixing[0])
    gate_value = dot(rear, gate[...])
    up_value = dot(rear, up[...])
    hidden_grad = dot_t(cotangent, down[...]) * mixing[1]
    g = sigmoid(gate_value)
    gate_grad = (hidden_grad * up_value * g * (1.0 + gate_value * (1.0 - g))).astype(BF16)
    up_grad = (hidden_grad * gate_value * g).astype(BF16)
    put(width, (dot_t(gate_grad, gate[...]) + dot_t(up_grad, up[...])) * gain[...])


def home_kernel(own, other, fr, rr, ct, out):
    width = fr.shape[1]
    total = own[...] + other[...].astype(F32)
    out[:, :width] = (fr[...].astype(F32) + total[:, :width]).astype(BF16)
    out[:, width : 2 * width] = total[:, width:].astype(BF16)
    out[:, 2 * width : 3 * width] = rr[...]
    out[:, 3 * width :] = ct[...]


def finish_kernel(home, below, above, front, rear):
    width = front.shape[1]
    total = home[:, : 2 * width].astype(F32) + below[...].astype(F32) + above[...].astype(F32)
    front[...] = total[:, :width].astype(BF16)
    wide = home[:, 2 * width : 3 * width].astype(F32)
    inverse = lax.rsqrt(jnp.mean(wide * wide, axis=-1, keepdims=True) + epsilon)
    grad = total[:, width:]
    along = jnp.mean(wide * grad, axis=-1, keepdims=True)
    cubed = inverse * inverse * inverse
    cotangent = home[:, 3 * width :].astype(F32)
    rear[...] = (cotangent + inverse * grad - wide * cubed * along).astype(BF16)


def shards(
    front_rows,
    front_routes,
    front_weights,
    rear_rows,
    rear_routes,
    rear_weights,
    rear_cotangent,
    norm_gain,
    gate_weight,
    up_weight,
    down_weight,
):
    experts = lax.axis_size("expert")
    sections = lax.axis_size("section")
    tokens, width = front_rows.shape[1:]
    half = tokens // 2
    reach = experts // 4
    lanes = table_lanes(experts)
    up_pairs, down_pairs = ring_pairs(experts, 1), ring_pairs(experts, -1)
    twin_pairs = [(i, i ^ 1) for i in range(experts)]

    def twin(value):
        return lax.ppermute(value, "expert", twin_pairs)

    def both(upward, downward):
        return (
            lax.ppermute(upward, "expert", up_pairs),
            lax.ppermute(downward, "expert", down_pairs),
        )

    def across(value, pairs):
        def shifted(part, by):
            moves = [
                (s * experts + a, (s + by) % sections * experts + b)
                for s in range(sections)
                for a, b in pairs
            ]
            return lax.ppermute(part, ("section", "expert"), moves)

        if sections == 2:
            return shifted(value, 1)
        parts = [shifted(value[:, :width], 1), shifted(value[:, width:], -1)]
        return jnp.concatenate(parts, axis=1)

    (message,) = call(
        functools.partial(pack_kernel, experts),
        "pack",
        [((tokens, 3 * width + lanes), BF16)],
        front_rows[0],
        front_routes[0].T,
        front_weights[0].T,
        rear_rows[0],
        rear_routes[0].T,
        rear_weights[0].T,
        rear_cotangent[0],
        norm_gain,
    )
    me = lax.axis_index("expert").reshape(1)

    def expert_of(*mine):
        rows = sum(part.shape[0] for part in mine)
        own, other = call(
            functools.partial(expert_kernel, experts),
            "expert",
            [((rows, 2 * width), F32), ((rows, 2 * width), BF16)],
            me,
            *mine,
            *[twin(part) for part in mine],
            gate_weight[0, 0],
            up_weight[0, 0],
            down_weight[0, 0],
            norm_gain,
            scalars=1,
            flops=2 * 2 * rows * 8 * gate_weight[0, 0].size,
        )
        return own, twin(other)

    below, above = message, message
    results = [expert_of(message)]
    for step in range(1, reach):
        below, above = both(below, above)
        results.append(expert_of(below, above))
    far_below, far_above = both(below[:half], above[half:])
    results.append(expert_of(far_below, far_above))

    def total(step):
        own, other = results[step]
        return own + other.astype(F32)

    (home,) = call(
        home_kernel,
        "home",
        [((tokens, 4 * width), BF16)],
        *results[0],
        front_rows[0],
        rear_rows[0],
        rear_cotangent[0],
    )
    home = across(home, [(i, i) for i in range(experts)])
    far = total(reach).astype(BF16)
    from_below, from_above = both(far[:half], far[half:])
    for step in range(reach - 1, 0, -1):
        one = total(step)
        to_below, to_above = one[:tokens], one[tokens:]
        if step == reach - 1:
            to_above = jnp.concatenate(
                [to_above[:half] + from_below.astype(F32), to_above[half:]], axis=0
            )
            to_below = jnp.concatenate(
                [to_below[:half], to_below[half:] + from_above.astype(F32)], axis=0
            )
        else:
            to_above = to_above + from_below.astype(F32)
            to_below = to_below + from_above.astype(F32)
        to_below, to_above = to_below.astype(BF16), to_above.astype(BF16)
        if step > 1:
            from_below, from_above = both(to_above, to_below)
    from_below, from_above = across(to_above, up_pairs), across(to_below, down_pairs)
    front, rear = call(
        finish_kernel, "finish", [((tokens, width), BF16)] * 2, home, from_below, from_above
    )
    return (front[None], rear[None])


def solution(mesh):
    rows = P("section", "expert", None)
    weights = P("section", "expert", None, None)
    placed = (rows,) * 7 + (P("section", None),) + (weights,) * 3
    return jax.shard_map(
        shards, mesh=mesh, in_specs=placed, out_specs=(rows, rows), check_vma=False
    )
```

profile of v0, /device:TPU:0, one launch (start us, length us, event | category | flops | bytes accessed | tf_op | source)
XLA Modules:
  0.0 78.0 jit_solution(3052871220750504213)
XLA Ops:
  5.6 3.1 %collective-permute-start.3 = (bf16[32,3200]{1,0:T(8,128)(2,1)S(1)}, bf16[32,3200]{1,0:T(8,128)(2,1)S(1)}, u32[]{:S(2)}, u32[]{:S(2)}) collective-permute-start(bf16[32,3200]{1,0:T(8,128)(2,1)S(1)} %pack.1.refs_0_), channel_id=1, source_target_pairs={{0,4},{1,5},{4,8},{5,9},{8,12},{9,13},{12,14},{13,15},{14,10},{15,... | collective-permute-start | bytes 614408 | tf_op jit(solution)/shard_map/ppermute | solution.py:161
  8.7 5.0 %collective-permute-done.3.refs_0_ = bf16[32,3200]{1,0:T(8,128)(2,1)S(1)} collective-permute-done((bf16[32,3200]{1,0:T(8,128)(2,1)S(1)}, bf16[32,3200]{1,0:T(8,128)(2,1)S(1)}, u32[]{:S(2)}, u32[]{:S(2)}) %collective-permute-start.3) | collective-permute-done | bytes 204832 | tf_op jit(solution)/shard_map/ppermute | solution.py:161
  13.7 1.8 %collective-permute-start.8 = (bf16[32,3200]{1,0:T(8,128)(2,1)S(1)}, bf16[32,3200]{1,0:T(8,128)(2,1)S(1)}, u32[]{:S(2)}, u32[]{:S(2)}) collective-permute-start(bf16[32,3200]{1,0:T(8,128)(2,1)S(1)} %collective-permute-done.3.refs_0_), channel_id=1, source_target_pairs={{0,4},{1,5},{4,8},{5,9},{8,12},{9,13},{12,14},{13,15},{14,10},{15,... | collective-permute-start | bytes 614408 | tf_op jit(solution)/shard_map/ppermute | solution.py:161
  15.7 4.2 %collective-permute-done.8.refs_0_ = bf16[32,3200]{1,0:T(8,128)(2,1)S(1)} collective-permute-done((bf16[32,3200]{1,0:T(8,128)(2,1)S(1)}, bf16[32,3200]{1,0:T(8,128)(2,1)S(1)}, u32[]{:S(2)}, u32[]{:S(2)}) %collective-permute-start.8) | collective-permute-done | bytes 204832 | tf_op jit(solution)/shard_map/ppermute | solution.py:161
  19.9 1.5 %collective-permute-start.13 = (bf16[32,3200]{1,0:T(8,128)(2,1)S(1)}, bf16[32,3200]{1,0:T(8,128)(2,1)S(1)}, u32[]{:S(2)}, u32[]{:S(2)}) collective-permute-start(bf16[32,3200]{1,0:T(8,128)(2,1)S(1)} %collective-permute-done.8.refs_0_), channel_id=1, source_target_pairs={{0,4},{1,5},{4,8},{5,9},{8,12},{9,13},{12,14},{13,15},{14,10},{15,... | collective-permute-start | bytes 614408 | tf_op jit(solution)/shard_map/ppermute | solution.py:161
  22.5 3.3 %collective-permute-done.13.refs_0_ = bf16[32,3200]{1,0:T(8,128)(2,1)S(1)} collective-permute-done((bf16[32,3200]{1,0:T(8,128)(2,1)S(1)}, bf16[32,3200]{1,0:T(8,128)(2,1)S(1)}, u32[]{:S(2)}, u32[]{:S(2)}) %collective-permute-start.13) | collective-permute-done | bytes 204832 | tf_op jit(solution)/shard_map/ppermute | solution.py:161
  25.8 1.8 %collective-permute-start.18 = (bf16[16,3200]{1,0:T(8,128)(2,1)S(1)}, bf16[16,3200]{1,0:T(8,128)(2,1)S(1)}, u32[]{:S(2)}, u32[]{:S(2)}) collective-permute-start(bf16[16,3200]{1,0:T(8,128)(2,1)S(1)} %slice.59), channel_id=1, source_target_pairs={{0,4},{1,5},{4,8},{5,9},{8,12},{9,13},{12,14},{13,15},{14,10},{15,... | collective-permute-start | bytes 307208 | tf_op jit(solution)/shard_map/ppermute | solution.py:161
  31.2 2.1 %expert.5 = (f32[32,2048]{1,0:T(8,128)S(1)}, bf16[32,2048]{1,0:T(8,128)(2,1)S(1)}) custom-call(s32[1]{0:T(128)} %bitcast.me, bf16[32,3200]{1,0:T(8,128)(2,1)S(1)} %pack.1.refs_0_, bf16[32,3200]{1,0:T(8,128)(2,1)S(1)} %collective-permute-done.refs_1_, bf16[1024,512]{1,0:T(8,128)(2,1)S(1)} %bitcast.21, bf16[1024,512]{1,0:T(8,128)(2,1)S(1)} %bitcast.26, ...), custom_call_target="tpu_custom_call" | custom-call | flops 536870912 | bytes 3952644 | tf_op jit(solution)/shard_map/expert/pallas_call | solution.py:21
  35.3 3.5 %collective-permute-done.19.refs_1_ = bf16[16,3200]{1,0:T(8,128)(2,1)S(1)} collective-permute-done((bf16[16,3200]{1,0:T(8,128)(2,1)S(1)}, bf16[16,3200]{1,0:T(8,128)(2,1)S(1)}, u32[]{:S(2)}, u32[]{:S(2)}) %collective-permute-start.19) | collective-permute-done | bytes 102432 | tf_op jit(solution)/shard_map/ppermute | solution.py:162
  39.5 2.0 %expert.6 = (f32[64,2048]{1,0:T(8,128)S(1)}, bf16[64,2048]{1,0:T(8,128)(2,1)S(1)}) custom-call(s32[1]{0:T(128)} %bitcast.me, bf16[32,3200]{1,0:T(8,128)(2,1)S(1)} %collective-permute-done.3.refs_0_, bf16[32,3200]{1,0:T(8,128)(2,1)S(1)} %collective-permute-done.4.refs_1_, bf16[32,3200]{1,0:T(8,128)(2,1)S(1)} %collective-permute-done.5.refs_2_, ...), custom_call_target="tpu_custom_call" | custom-call | flops 1073741824 | bytes 4755460 | tf_op jit(solution)/shard_map/expert/pallas_call | solution.py:21
  41.6 1.6 %collective-permute-start.2 = (bf16[32,4096]{1,0:T(8,128)(2,1)S(1)}, bf16[32,4096]{1,0:T(8,128)(2,1)S(1)}, u32[]{:S(2)}, u32[]{:S(2)}) collective-permute-start(bf16[32,4096]{1,0:T(8,128)(2,1)S(1)} %home.1), channel_id=1, source_target_pairs={{0,16},{1,17},{2,18},{3,19},{4,20},{5,21},{6,22},{7,23},{8,24},{9,... | collective-permute-start | bytes 786440 | tf_op jit(solution)/shard_map/ppermute | solution.py:172
  43.2 2.1 %expert.9 = (f32[32,2048]{1,0:T(8,128)S(1)}, bf16[32,2048]{1,0:T(8,128)(2,1)S(1)}) custom-call(s32[1]{0:T(128)} %bitcast.me, bf16[16,3200]{1,0:T(8,128)(2,1)S(1)} %collective-permute-done.18.refs_0_, bf16[16,3200]{1,0:T(8,128)(2,1)S(1)} %collective-permute-done.19.refs_1_, bf16[16,3200]{1,0:T(8,128)(2,1)S(1)} %collective-permute-done.20.refs_2_, ...), custom_call_target="tpu_custom_call" | custom-call | flops 536870912 | bytes 3952644 | tf_op jit(solution)/shard_map/expert/pallas_call | solution.py:21
  45.9 2.0 %expert.7 = (f32[64,2048]{1,0:T(8,128)S(1)}, bf16[64,2048]{1,0:T(8,128)(2,1)S(1)}) custom-call(s32[1]{0:T(128)} %bitcast.me, bf16[32,3200]{1,0:T(8,128)(2,1)S(1)} %collective-permute-done.8.refs_0_, bf16[32,3200]{1,0:T(8,128)(2,1)S(1)} %collective-permute-done.9.refs_1_, bf16[32,3200]{1,0:T(8,128)(2,1)S(1)} %collective-permute-done.10.refs_2_, ...), custom_call_target="tpu_custom_call" | custom-call | flops 1073741824 | bytes 4755460 | tf_op jit(solution)/shard_map/expert/pallas_call | solution.py:21
  48.1 2.0 %expert.8 = (f32[64,2048]{1,0:T(8,128)S(1)}, bf16[64,2048]{1,0:T(8,128)(2,1)S(1)}) custom-call(s32[1]{0:T(128)} %bitcast.me, bf16[32,3200]{1,0:T(8,128)(2,1)S(1)} %collective-permute-done.13.refs_0_, bf16[32,3200]{1,0:T(8,128)(2,1)S(1)} %collective-permute-done.14.refs_1_, bf16[32,3200]{1,0:T(8,128)(2,1)S(1)} %collective-permute-done.15.refs_2_, ...), custom_call_target="tpu_custom_call" | custom-call | flops 1073741824 | bytes 4755460 | tf_op jit(solution)/shard_map/expert/pallas_call | solution.py:21
  50.6 1.6 %collective-permute-start.23 = (bf16[16,2048]{1,0:T(8,128)(2,1)S(1)}, bf16[16,2048]{1,0:T(8,128)(2,1)S(1)}, u32[]{:S(2)}, u32[]{:S(2)}) collective-permute-start(bf16[16,2048]{1,0:T(8,128)(2,1)S(1)} %get-tuple-element.37), channel_id=1, source_target_pairs={{0,4},{1,5},{4,8},{5,9},{8,12},{9,13},{12,14},{13,15},{14,10},{15,... | collective-permute-start | bytes 196616 | tf_op jit(solution)/shard_map/ppermute | solution.py:161
  52.8 2.2 %collective-permute-done.23 = bf16[16,2048]{1,0:T(8,128)(2,1)S(1)} collective-permute-done((bf16[16,2048]{1,0:T(8,128)(2,1)S(1)}, bf16[16,2048]{1,0:T(8,128)(2,1)S(1)}, u32[]{:S(2)}, u32[]{:S(2)}) %collective-permute-start.23) | collective-permute-done | bytes 65568 | tf_op jit(solution)/shard_map/ppermute | solution.py:161
  54.9 1.6 %collective-permute-done.27 = bf16[16,2048]{1,0:T(8,128)(2,1)S(1)} collective-permute-done((bf16[16,2048]{1,0:T(8,128)(2,1)S(1)}, bf16[16,2048]{1,0:T(8,128)(2,1)S(1)}, u32[]{:S(2)}, u32[]{:S(2)}) %collective-permute-start.27) | collective-permute-done | bytes 65568 | tf_op jit(solution)/shard_map/ppermute | solution.py:162
  56.6 1.6 %collective-permute-start.24 = (bf16[32,2048]{1,0:T(8,128)(2,1)S(1)}, bf16[32,2048]{1,0:T(8,128)(2,1)S(1)}, u32[]{:S(2)}, u32[]{:S(2)}) collective-permute-start(bf16[32,2048]{1,0:T(8,128)(2,1)S(1)} %pad_maximum_fusion), channel_id=1, source_target_pairs={{0,4},{1,5},{4,8},{5,9},{8,12},{9,13},{12,14},{13,15},{14,10},{15,... | collective-permute-start | bytes 393224 | tf_op jit(solution)/shard_map/ppermute | solution.py:161
  58.8 2.8 %collective-permute-done.24 = bf16[32,2048]{1,0:T(8,128)(2,1)S(1)} collective-permute-done((bf16[32,2048]{1,0:T(8,128)(2,1)S(1)}, bf16[32,2048]{1,0:T(8,128)(2,1)S(1)}, u32[]{:S(2)}, u32[]{:S(2)}) %collective-permute-start.24) | collective-permute-done | bytes 131104 | tf_op jit(solution)/shard_map/ppermute | solution.py:161
  61.6 1.6 %collective-permute-done.28 = bf16[32,2048]{1,0:T(8,128)(2,1)S(1)} collective-permute-done((bf16[32,2048]{1,0:T(8,128)(2,1)S(1)}, bf16[32,2048]{1,0:T(8,128)(2,1)S(1)}, u32[]{:S(2)}, u32[]{:S(2)}) %collective-permute-start.28) | collective-permute-done | bytes 131104 | tf_op jit(solution)/shard_map/ppermute | solution.py:162
  63.3 1.5 %collective-permute-start.25 = (bf16[32,2048]{1,0:T(8,128)(2,1)S(1)}, bf16[32,2048]{1,0:T(8,128)(2,1)S(1)}, u32[]{:S(2)}, u32[]{:S(2)}) collective-permute-start(bf16[32,2048]{1,0:T(8,128)(2,1)S(1)} %get-tuple-element.31), channel_id=1, source_target_pairs={{0,4},{1,5},{4,8},{5,9},{8,12},{9,13},{12,14},{13,15},{14,10},{15,... | collective-permute-start | bytes 393224 | tf_op jit(solution)/shard_map/ppermute | solution.py:161
  65.4 2.9 %collective-permute-done.25 = bf16[32,2048]{1,0:T(8,128)(2,1)S(1)} collective-permute-done((bf16[32,2048]{1,0:T(8,128)(2,1)S(1)}, bf16[32,2048]{1,0:T(8,128)(2,1)S(1)}, u32[]{:S(2)}, u32[]{:S(2)}) %collective-permute-start.25) | collective-permute-done | bytes 131104 | tf_op jit(solution)/shard_map/ppermute | solution.py:161
  71.0 1.8 %collective-permute-start.30 = (bf16[32,2048]{1,0:T(8,128)(2,1)S(1)}, bf16[32,2048]{1,0:T(8,128)(2,1)S(1)}, u32[]{:S(2)}, u32[]{:S(2)}) collective-permute-start(bf16[32,2048]{1,0:T(8,128)(2,1)S(1)} %get-tuple-element.28), channel_id=1, source_target_pairs={{0,18},{1,19},{4,16},{5,17},{8,20},{9,21},{12,24},{13,25},{14,28},... | collective-permute-start | bytes 393224 | tf_op jit(solution)/shard_map/ppermute | solution.py:172
  72.9 3.2 %collective-permute-done.26.below = bf16[32,2048]{1,0:T(8,128)(2,1)S(1)} collective-permute-done((bf16[32,2048]{1,0:T(8,128)(2,1)S(1)}, bf16[32,2048]{1,0:T(8,128)(2,1)S(1)}, u32[]{:S(2)}, u32[]{:S(2)}) %collective-permute-start.26) | collective-permute-done | bytes 131104 | tf_op jit(solution)/shard_map/ppermute | solution.py:172
  (93 shorter events, 20.1 us)
Async XLA Ops:
  5.6 8.0 %collective-permute-start.3 = (bf16[32,3200]{1,0:T(8,128)(2,1)S(1)}, bf16[32,3200]{1,0:T(8,128)(2,1)S(1)}, u32[]{:S(2)}, u32[]{:S(2)}) collective-permute-start(bf16[32,3200]{1,0:T(8,128)(2,1)S(1)} %pack.1.refs_0_), channel_id=1, source_target_pairs={{0,4},{1,5},{4,8},{5,9},{8,12},{9,13},{12,14},{13,15},{14,10},{15,... | collective-permute-start | bytes 614408 | tf_op jit(solution)/shard_map/ppermute | solution.py:161
  8.7 6.8 %collective-permute-start.4 = (bf16[32,3200]{1,0:T(8,128)(2,1)S(1)}, bf16[32,3200]{1,0:T(8,128)(2,1)S(1)}, u32[]{:S(2)}, u32[]{:S(2)}) collective-permute-start(bf16[32,3200]{1,0:T(8,128)(2,1)S(1)} %pack.1.refs_0_), channel_id=1, source_target_pairs={{0,2},{1,3},{4,0},{5,1},{8,4},{9,5},{12,8},{13,9},{14,12},{15,13},... | collective-permute-start | bytes 614408 | tf_op jit(solution)/shard_map/ppermute | solution.py:162
  13.7 6.3 %collective-permute-start.8 = (bf16[32,3200]{1,0:T(8,128)(2,1)S(1)}, bf16[32,3200]{1,0:T(8,128)(2,1)S(1)}, u32[]{:S(2)}, u32[]{:S(2)}) collective-permute-start(bf16[32,3200]{1,0:T(8,128)(2,1)S(1)} %collective-permute-done.3.refs_0_), channel_id=1, source_target_pairs={{0,4},{1,5},{4,8},{5,9},{8,12},{9,13},{12,14},{13,15},{14,10},{15,... | collective-permute-start | bytes 614408 | tf_op jit(solution)/shard_map/ppermute | solution.py:161
  15.5 5.9 %collective-permute-start.9 = (bf16[32,3200]{1,0:T(8,128)(2,1)S(1)}, bf16[32,3200]{1,0:T(8,128)(2,1)S(1)}, u32[]{:S(2)}, u32[]{:S(2)}) collective-permute-start(bf16[32,3200]{1,0:T(8,128)(2,1)S(1)} %collective-permute-done.4.refs_1_), channel_id=1, source_target_pairs={{0,2},{1,3},{4,0},{5,1},{8,4},{9,5},{12,8},{13,9},{14,12},{15,13},... | collective-permute-start | bytes 614408 | tf_op jit(solution)/shard_map/ppermute | solution.py:162
  19.9 5.8 %collective-permute-start.13 = (bf16[32,3200]{1,0:T(8,128)(2,1)S(1)}, bf16[32,3200]{1,0:T(8,128)(2,1)S(1)}, u32[]{:S(2)}, u32[]{:S(2)}) collective-permute-start(bf16[32,3200]{1,0:T(8,128)(2,1)S(1)} %collective-permute-done.8.refs_0_), channel_id=1, source_target_pairs={{0,4},{1,5},{4,8},{5,9},{8,12},{9,13},{12,14},{13,15},{14,10},{15,... | collective-permute-start | bytes 614408 | tf_op jit(solution)/shard_map/ppermute | solution.py:161
  21.5 6.1 %collective-permute-start = (bf16[32,3200]{1,0:T(8,128)(2,1)S(1)}, bf16[32,3200]{1,0:T(8,128)(2,1)S(1)}, u32[]{:S(2)}, u32[]{:S(2)}) collective-permute-start(bf16[32,3200]{1,0:T(8,128)(2,1)S(1)} %pack.1.refs_0_), channel_id=1, source_target_pairs={{0,1},{1,0},{2,3},{3,2},{4,5},{5,4},{6,7},{7,6},{8,9},{9,8},{10,11... | collective-permute-start | bytes 614408 | tf_op jit(solution)/shard_map/ppermute | solution.py:157
  21.5 12.0 %collective-permute-start.14 = (bf16[32,3200]{1,0:T(8,128)(2,1)S(1)}, bf16[32,3200]{1,0:T(8,128)(2,1)S(1)}, u32[]{:S(2)}, u32[]{:S(2)}) collective-permute-start(bf16[32,3200]{1,0:T(8,128)(2,1)S(1)} %collective-permute-done.9.refs_1_), channel_id=1, source_target_pairs={{0,2},{1,3},{4,0},{5,1},{8,4},{9,5},{12,8},{13,9},{14,12},{15,13},... | collective-permute-start | bytes 614408 | tf_op jit(solution)/shard_map/ppermute | solution.py:162
  22.0 12.9 %collective-permute-start.5 = (bf16[32,3200]{1,0:T(8,128)(2,1)S(1)}, bf16[32,3200]{1,0:T(8,128)(2,1)S(1)}, u32[]{:S(2)}, u32[]{:S(2)}) collective-permute-start(bf16[32,3200]{1,0:T(8,128)(2,1)S(1)} %collective-permute-done.3.refs_0_), channel_id=1, source_target_pairs={{0,1},{1,0},{2,3},{3,2},{4,5},{5,4},{6,7},{7,6},{8,9},{9,8},{10,11... | collective-permute-start | bytes 614408 | tf_op jit(solution)/shard_map/ppermute | solution.py:157
  22.2 16.6 %collective-permute-start.6 = (bf16[32,3200]{1,0:T(8,128)(2,1)S(1)}, bf16[32,3200]{1,0:T(8,128)(2,1)S(1)}, u32[]{:S(2)}, u32[]{:S(2)}) collective-permute-start(bf16[32,3200]{1,0:T(8,128)(2,1)S(1)} %collective-permute-done.4.refs_1_), channel_id=1, source_target_pairs={{0,1},{1,0},{2,3},{3,2},{4,5},{5,4},{6,7},{7,6},{8,9},{9,8},{10,11... | collective-permute-start | bytes 614408 | tf_op jit(solution)/shard_map/ppermute | solution.py:157
  25.8 8.0 %collective-permute-start.18 = (bf16[16,3200]{1,0:T(8,128)(2,1)S(1)}, bf16[16,3200]{1,0:T(8,128)(2,1)S(1)}, u32[]{:S(2)}, u32[]{:S(2)}) collective-permute-start(bf16[16,3200]{1,0:T(8,128)(2,1)S(1)} %slice.59), channel_id=1, source_target_pairs={{0,4},{1,5},{4,8},{5,9},{8,12},{9,13},{12,14},{13,15},{14,10},{15,... | collective-permute-start | bytes 307208 | tf_op jit(solution)/shard_map/ppermute | solution.py:161
  33.4 5.3 %collective-permute-start.19 = (bf16[16,3200]{1,0:T(8,128)(2,1)S(1)}, bf16[16,3200]{1,0:T(8,128)(2,1)S(1)}, u32[]{:S(2)}, u32[]{:S(2)}) collective-permute-start(bf16[16,3200]{1,0:T(8,128)(2,1)S(1)} %slice.60), channel_id=1, source_target_pairs={{0,2},{1,3},{4,0},{5,1},{8,4},{9,5},{12,8},{13,9},{14,12},{15,13},... | collective-permute-start | bytes 307208 | tf_op jit(solution)/shard_map/ppermute | solution.py:162
  33.8 5.6 %collective-permute-start.20 = (bf16[16,3200]{1,0:T(8,128)(2,1)S(1)}, bf16[16,3200]{1,0:T(8,128)(2,1)S(1)}, u32[]{:S(2)}, u32[]{:S(2)}) collective-permute-start(bf16[16,3200]{1,0:T(8,128)(2,1)S(1)} %collective-permute-done.18.refs_0_), channel_id=1, source_target_pairs={{0,1},{1,0},{2,3},{3,2},{4,5},{5,4},{6,7},{7,6},{8,9},{9,8},{10,11... | collective-permute-start | bytes 307208 | tf_op jit(solution)/shard_map/ppermute | solution.py:157
  34.8 10.5 %collective-permute-start.10 = (bf16[32,3200]{1,0:T(8,128)(2,1)S(1)}, bf16[32,3200]{1,0:T(8,128)(2,1)S(1)}, u32[]{:S(2)}, u32[]{:S(2)}) collective-permute-start(bf16[32,3200]{1,0:T(8,128)(2,1)S(1)} %collective-permute-done.8.refs_0_), channel_id=1, source_target_pairs={{0,1},{1,0},{2,3},{3,2},{4,5},{5,4},{6,7},{7,6},{8,9},{9,8},{10,11... | collective-permute-start | bytes 614408 | tf_op jit(solution)/shard_map/ppermute | solution.py:157
  34.9 10.6 %collective-permute-start.11 = (bf16[32,3200]{1,0:T(8,128)(2,1)S(1)}, bf16[32,3200]{1,0:T(8,128)(2,1)S(1)}, u32[]{:S(2)}, u32[]{:S(2)}) collective-permute-start(bf16[32,3200]{1,0:T(8,128)(2,1)S(1)} %collective-permute-done.9.refs_1_), channel_id=1, source_target_pairs={{0,1},{1,0},{2,3},{3,2},{4,5},{5,4},{6,7},{7,6},{8,9},{9,8},{10,11... | collective-permute-start | bytes 614408 | tf_op jit(solution)/shard_map/ppermute | solution.py:157
  38.8 9.1 %collective-permute-start.15 = (bf16[32,3200]{1,0:T(8,128)(2,1)S(1)}, bf16[32,3200]{1,0:T(8,128)(2,1)S(1)}, u32[]{:S(2)}, u32[]{:S(2)}) collective-permute-start(bf16[32,3200]{1,0:T(8,128)(2,1)S(1)} %collective-permute-done.13.refs_0_), channel_id=1, source_target_pairs={{0,1},{1,0},{2,3},{3,2},{4,5},{5,4},{6,7},{7,6},{8,9},{9,8},{10,11... | collective-permute-start | bytes 614408 | tf_op jit(solution)/shard_map/ppermute | solution.py:157
  39.4 8.7 %collective-permute-start.16 = (bf16[32,3200]{1,0:T(8,128)(2,1)S(1)}, bf16[32,3200]{1,0:T(8,128)(2,1)S(1)}, u32[]{:S(2)}, u32[]{:S(2)}) collective-permute-start(bf16[32,3200]{1,0:T(8,128)(2,1)S(1)} %collective-permute-done.14.refs_1_), channel_id=1, source_target_pairs={{0,1},{1,0},{2,3},{3,2},{4,5},{5,4},{6,7},{7,6},{8,9},{9,8},{10,11... | collective-permute-start | bytes 614408 | tf_op jit(solution)/shard_map/ppermute | solution.py:157
  41.6 31.3 %collective-permute-start.2 = (bf16[32,4096]{1,0:T(8,128)(2,1)S(1)}, bf16[32,4096]{1,0:T(8,128)(2,1)S(1)}, u32[]{:S(2)}, u32[]{:S(2)}) collective-permute-start(bf16[32,4096]{1,0:T(8,128)(2,1)S(1)} %home.1), channel_id=1, source_target_pairs={{0,16},{1,17},{2,18},{3,19},{4,20},{5,21},{6,22},{7,23},{8,24},{9,... | collective-permute-start | bytes 786440 | tf_op jit(solution)/shard_map/ppermute | solution.py:172
  45.3 20.1 %collective-permute-start.7 = (bf16[64,2048]{1,0:T(8,128)(2,1)S(1)}, bf16[64,2048]{1,0:T(8,128)(2,1)S(1)}, u32[]{:S(2)}, u32[]{:S(2)}) collective-permute-start(bf16[64,2048]{1,0:T(8,128)(2,1)S(1)} %get-tuple-element.17), channel_id=1, source_target_pairs={{0,1},{1,0},{2,3},{3,2},{4,5},{5,4},{6,7},{7,6},{8,9},{9,8},{10,11... | collective-permute-start | bytes 786440 | tf_op jit(solution)/shard_map/ppermute | solution.py:157
  45.5 5.1 %collective-permute-start.22 = (bf16[32,2048]{1,0:T(8,128)(2,1)S(1)}, bf16[32,2048]{1,0:T(8,128)(2,1)S(1)}, u32[]{:S(2)}, u32[]{:S(2)}) collective-permute-start(bf16[32,2048]{1,0:T(8,128)(2,1)S(1)} %get-tuple-element.23), channel_id=1, source_target_pairs={{0,1},{1,0},{2,3},{3,2},{4,5},{5,4},{6,7},{7,6},{8,9},{9,8},{10,11... | collective-permute-start | bytes 393224 | tf_op jit(solution)/shard_map/ppermute | solution.py:157
  47.9 10.8 %collective-permute-start.12 = (bf16[64,2048]{1,0:T(8,128)(2,1)S(1)}, bf16[64,2048]{1,0:T(8,128)(2,1)S(1)}, u32[]{:S(2)}, u32[]{:S(2)}) collective-permute-start(bf16[64,2048]{1,0:T(8,128)(2,1)S(1)} %get-tuple-element.19), channel_id=1, source_target_pairs={{0,1},{1,0},{2,3},{3,2},{4,5},{5,4},{6,7},{7,6},{8,9},{9,8},{10,11... | collective-permute-start | bytes 786440 | tf_op jit(solution)/shard_map/ppermute | solution.py:157
  56.6 5.0 %collective-permute-start.24 = (bf16[32,2048]{1,0:T(8,128)(2,1)S(1)}, bf16[32,2048]{1,0:T(8,128)(2,1)S(1)}, u32[]{:S(2)}, u32[]{:S(2)}) collective-permute-start(bf16[32,2048]{1,0:T(8,128)(2,1)S(1)} %pad_maximum_fusion), channel_id=1, source_target_pairs={{0,4},{1,5},{4,8},{5,9},{8,12},{9,13},{12,14},{13,15},{14,10},{15,... | collective-permute-start | bytes 393224 | tf_op jit(solution)/shard_map/ppermute | solution.py:161
  58.2 5.0 %collective-permute-start.28 = (bf16[32,2048]{1,0:T(8,128)(2,1)S(1)}, bf16[32,2048]{1,0:T(8,128)(2,1)S(1)}, u32[]{:S(2)}, u32[]{:S(2)}) collective-permute-start(bf16[32,2048]{1,0:T(8,128)(2,1)S(1)} %pad_maximum_fusion.1), channel_id=1, source_target_pairs={{0,2},{1,3},{4,0},{5,1},{8,4},{9,5},{12,8},{13,9},{14,12},{15,13},... | collective-permute-start | bytes 393224 | tf_op jit(solution)/shard_map/ppermute | solution.py:162
  69.9 6.2 %collective-permute-start.26 = (bf16[32,2048]{1,0:T(8,128)(2,1)S(1)}, bf16[32,2048]{1,0:T(8,128)(2,1)S(1)}, u32[]{:S(2)}, u32[]{:S(2)}) collective-permute-start(bf16[32,2048]{1,0:T(8,128)(2,1)S(1)} %get-tuple-element.29), channel_id=1, source_target_pairs={{0,20},{1,21},{4,24},{5,25},{8,28},{9,29},{12,30},{13,31},{14,26},... | collective-permute-start | bytes 393224 | tf_op jit(solution)/shard_map/ppermute | solution.py:172
  71.0 6.2 %collective-permute-start.30 = (bf16[32,2048]{1,0:T(8,128)(2,1)S(1)}, bf16[32,2048]{1,0:T(8,128)(2,1)S(1)}, u32[]{:S(2)}, u32[]{:S(2)}) collective-permute-start(bf16[32,2048]{1,0:T(8,128)(2,1)S(1)} %get-tuple-element.28), channel_id=1, source_target_pairs={{0,18},{1,19},{4,16},{5,17},{8,20},{9,21},{12,24},{13,25},{14,28},... | collective-permute-start | bytes 393224 | tf_op jit(solution)/shard_map/ppermute | solution.py:172
  (24 other events, 79.9 us)
where the time goes:
time: 78.4 us; the launch traced here: 78 us
  waiting for transfers between devices  33.6 us (43%)
  starting transfers between devices  23.3 us (30%)
  Pallas kernels  11.5 us (15%)
  local copies, waits for them, and re-layouts  8.32 us (11%)
  between operations  0.87 us (1%)
    ppermute x7, waiting for transfers between devices, both(): lax.ppermute(upward, 'expert', up_pairs)  20.4 us
    ppermute x7, starting transfers between devices, both(): lax.ppermute(upward, 'expert', up_pairs)  12.9 us
    pallas_call x8, Pallas kernels, call(): pl.pallas_call(kernel, out_shape=shapes, in_specs=[smem] * scalars + [vme...  11.5 us
    unnamed x34, local copies, waits for them, and re-layouts  8.28 us
    ppermute x7, waiting for transfers between devices, both(): lax.ppermute(downward, 'expert', down_pairs)  8.23 us
    ppermute x3, starting transfers between devices, shifted(): return lax.ppermute(part, ('section', 'expert'), moves)  4.57 us
    ppermute x3, waiting for transfers between devices, shifted(): return lax.ppermute(part, ('section', 'expert'), moves)  4.34 us
    ppermute x14, starting transfers between devices, twin(): return lax.ppermute(value, 'expert', twin_pairs)  3.18 us
  transfers between devices with their start and end apart: 31, of which 13 were waited for; matrix products, arithmetic and copies ran while one was open for 0% of the time, Pallas kernels for 13%

commit v1 on v0

v1 whole, which is shorter than its diff:
```python
import functools

import jax
import jax.numpy as jnp
from jax import lax
from jax.experimental import pallas as pl
from jax.experimental.pallas import tpu as pltpu
from jax.sharding import PartitionSpec as P

epsilon = 1e-06
F32 = jnp.float32
BF16 = jnp.bfloat16
VMEM_LIMIT = 16 * 1024 * 1024
PACK_LIMIT = 60 * 1024 * 1024
HOLD_LIMIT = 50 * 1024 * 1024


def call(kernel, name, shapes, *operands, scalars=0, flops=0, limit=VMEM_LIMIT, scratch=(), anywhere=()):
    vmem = pl.BlockSpec(memory_space=pltpu.VMEM)
    smem = pl.BlockSpec(memory_space=pltpu.SMEM)
    places = [smem] * scalars + [vmem] * (len(operands) - scalars)
    for at in anywhere:
        places[at] = pl.BlockSpec(memory_space=pltpu.HBM)
    shapes = [jax.ShapeDtypeStruct(shape, dtype) for shape, dtype in shapes]
    moved = sum(value.size * value.dtype.itemsize for value in [*operands, *shapes])
    return pl.pallas_call(
        kernel,
        out_shape=shapes,
        in_specs=places,
        out_specs=[vmem] * len(shapes),
        scratch_shapes=scratch,
        compiler_params=pltpu.CompilerParams(vmem_limit_bytes=limit),
        cost_estimate=pl.CostEstimate(flops=flops, bytes_accessed=moved, transcendentals=0),
        name=name,
    )(*operands)


def ring_of(experts):
    chips = experts // 2
    return list(range(0, chips, 2)) + list(range(1, chips, 2))[::-1]


def ring_pairs(experts, by):
    ring = ring_of(experts)
    chips = len(ring)
    return [
        (2 * ring[i] + c, 2 * ring[(i + by) % chips] + c) for i in range(chips) for c in range(2)
    ]


def table_lanes(experts):
    return -(-4 * experts // 128) * 128


def pack_kernel(experts, fr, frt, fw, rr, rrt, rw, ct, gain, msg, rest):
    tokens, width = fr.shape
    lanes = table_lanes(experts)
    for j, rows in ((0, fr), (1, rr)):
        wide = rows[...].astype(F32)
        inverse = lax.rsqrt(jnp.mean(wide * wide, axis=-1, keepdims=True) + epsilon)
        msg[:, j * width : (j + 1) * width] = (wide * inverse * gain[...]).astype(BF16)
    msg[:, 2 * width : 3 * width] = ct[...]
    for j, rows in enumerate((fr, rr, ct)):
        rest[:, j * width : (j + 1) * width] = rows[...]
    row = lax.broadcasted_iota(jnp.int32, (lanes, tokens), 0)
    table = jnp.zeros((lanes, tokens), F32)
    for group, (routes, weights) in enumerate(((frt, fw), (frt, fw), (rrt, rw), (rrt, rw))):
        for k in range(routes.shape[0]):
            hit = row == routes[k : k + 1, :] + group * experts
            weight = weights[k : k + 1, :]
            high = weight.astype(BF16).astype(F32)
            table = table + jnp.where(hit, high if group % 2 == 0 else weight - high, 0.0)
    msg[:, 3 * width :] = table.T.astype(BF16)


def sigmoid(v):
    return 1.0 / (1.0 + jnp.exp(-v))


def hold_kernel(*refs):
    *refs, sems = refs
    count = len(refs) // 2
    copies = [
        pltpu.make_async_copy(refs[i], refs[count + i], sems.at[i]) for i in range(count)
    ]
    for copy in copies:
        copy.start()
    for copy in copies:
        copy.wait()


def expert_kernel(experts, *refs):
    *parts, gate, up, down, gate_twin, up_twin, down_twin, gain, out = refs
    width = gate.shape[0]
    rows = jnp.concatenate([part[:, : 3 * width] for part in parts], axis=0)
    table = jnp.concatenate([part[:, 3 * width :] for part in parts], axis=0).astype(F32)
    lane = lax.broadcasted_iota(jnp.int32, table.shape, 1)
    count = rows.shape[0]
    across = (((1,), (1,)), ((), ()))

    def mixing(expert, group):
        hit = (lane == expert + group * experts) | (lane == expert + (group + 1) * experts)
        return jnp.sum(jnp.where(hit, table, 0.0), axis=-1, keepdims=True)

    def dot(a, b):
        return jnp.dot(a, b, preferred_element_type=F32)

    def dot_t(a, b):
        return lax.dot_general(a, b, across, preferred_element_type=F32)

    both_rows = jnp.concatenate([rows[:, :width], rows[:, width : 2 * width]], axis=0)
    cotangent = rows[:, 2 * width :]
    me = lax.axis_index("expert")
    front = rear = 0.0
    for expert, gate, up, down in (
        (me, gate, up, down),
        (me ^ 1, gate_twin, up_twin, down_twin),
    ):
        gate_value = dot(both_rows, gate[...])
        up_value = dot(both_rows, up[...])
        g = sigmoid(gate_value)
        silu = gate_value * g
        hidden = (silu[:count] * up_value[:count]).astype(BF16)
        front = front + dot(hidden, down[...]) * mixing(expert, 0)
        gate_value, up_value, g, silu = (v[count:] for v in (gate_value, up_value, g, silu))
        hidden_grad = dot_t(cotangent, down[...]) * mixing(expert, 2)
        gate_grad = (hidden_grad * up_value * g * (1.0 + gate_value * (1.0 - g))).astype(BF16)
        up_grad = (hidden_grad * silu).astype(BF16)
        rear = rear + dot_t(gate_grad, gate[...]) + dot_t(up_grad, up[...])
    out[:, :width] = front
    out[:, width:] = rear * gain[...]


def finish_kernel(rest, home, far, below, above, front, rear):
    width = front.shape[1]
    total = home[...].astype(F32) + far[...].astype(F32)
    total = total + below[...].astype(F32) + above[...].astype(F32)
    front[...] = (rest[:, :width].astype(F32) + total[:, :width]).astype(BF16)
    wide = rest[:, width : 2 * width].astype(F32)
    inverse = lax.rsqrt(jnp.mean(wide * wide, axis=-1, keepdims=True) + epsilon)
    grad = total[:, width:]
    along = jnp.mean(wide * grad, axis=-1, keepdims=True)
    cubed = inverse * inverse * inverse
    cotangent = rest[:, 2 * width :].astype(F32)
    rear[...] = (cotangent + inverse * grad - wide * cubed * along).astype(BF16)


def shards(
    front_rows,
    front_routes,
    front_weights,
    rear_rows,
    rear_routes,
    rear_weights,
    rear_cotangent,
    norm_gain,
    gate_weight,
    up_weight,
    down_weight,
):
    experts = lax.axis_size("expert")
    sections = lax.axis_size("section")
    tokens, width = front_rows.shape[1:]
    half = tokens // 2
    reach = experts // 4
    lanes = table_lanes(experts)
    up_pairs, down_pairs = ring_pairs(experts, 1), ring_pairs(experts, -1)
    twin_pairs = [(i, i ^ 1) for i in range(experts)]

    def both(upward, downward):
        return (
            lax.ppermute(upward, "expert", up_pairs),
            lax.ppermute(downward, "expert", down_pairs),
        )

    def across(value, pairs):
        def shifted(part, by):
            moves = [
                (s * experts + a, (s + by) % sections * experts + b)
                for s in range(sections)
                for a, b in pairs
            ]
            return lax.ppermute(part, ("section", "expert"), moves)

        if sections == 2:
            return shifted(value, 1)
        parts = [shifted(value[:, :width], 1), shifted(value[:, width:], -1)]
        return jnp.concatenate(parts, axis=1)

    message, rest = call(
        functools.partial(pack_kernel, experts),
        "pack",
        [((tokens, 3 * width + lanes), BF16), ((tokens, 3 * width), BF16)],
        front_rows[0],
        front_routes[0].T,
        front_weights[0].T,
        rear_rows[0],
        rear_routes[0].T,
        rear_weights[0].T,
        rear_cotangent[0],
        norm_gain,
        limit=PACK_LIMIT,
    )
    def after(value, *first):
        return lax.optimization_barrier((value, *first))[0]

    weights = [gate_weight[0, 0], up_weight[0, 0], down_weight[0, 0]]
    held = call(
        hold_kernel,
        "hold",
        [(weight.shape, weight.dtype) for weight in weights],
        *[after(weight, message) for weight in weights],
        limit=HOLD_LIMIT,
        scratch=[pltpu.SemaphoreType.DMA((len(weights),))],
        anywhere=range(len(weights)),
    )
    moved = [lax.ppermute(after(weight, message), "expert", twin_pairs) for weight in weights]
    held = [*held, *moved]

    def expert_of(*parts):
        rows = sum(part.shape[0] for part in parts)
        return call(
            functools.partial(expert_kernel, experts),
            "expert",
            [((rows, 2 * width), F32)],
            *parts,
            *held,
            norm_gain,
            flops=2 * 2 * rows * 8 * weights[0].size,
        )[0]

    below, above = both(message, message)
    here = [(i, i) for i in range(experts)]
    rest = across(after(rest, *held[: len(weights)]), here)
    results = []
    for step in range(1, reach):
        below = after(below, *(results[-1:] or held[: len(weights)]))
        above = after(above, below)
        mine = (below, above)
        if step == reach - 2:
            mine = (after(below, rest), above)
        if step == reach - 1:
            mine = (after(below, home), above)
        if step < reach - 1:
            below, above = both(below, above)
        else:
            below, above = both(below[:half], above[half:])
        results.append(expert_of(*mine, *([message] if step == 1 else [])))
        if step == 1:
            home = across(results[0][2 * tokens :].astype(BF16), here)
    from_below = from_above = None
    for step in range(reach - 1, 0, -1):
        to_above = results[step - 1][tokens : 2 * tokens]
        to_below = results[step - 1][:tokens]
        if step < reach - 1:
            to_above = to_above + from_below.astype(F32)
        to_above = to_above.astype(BF16)
        if step == reach - 2:
            to_above = after(to_above, far)
        if step < reach - 1:
            from_above = after(from_above, to_above)
            to_below = to_below + from_above.astype(F32)
        to_below = to_below.astype(BF16)
        if step == reach - 1:
            far = expert_of(after(below, to_above, to_below), above).astype(BF16)
        if step == reach - 2:
            far = across(after(far, to_below), ring_pairs(experts, reach))
        if step > 1:
            from_below, from_above = both(to_above, to_below)
    from_below, from_above = across(to_above, up_pairs), across(to_below, down_pairs)
    front, rear = call(
        finish_kernel, "finish", [((tokens, width), BF16)] * 2, rest, home, far, from_below, from_above
    )
    return (front[None], rear[None])


def solution(mesh):
    rows = P("section", "expert", None)
    weights = P("section", "expert", None, None)
    placed = (rows,) * 7 + (P("section", None),) + (weights,) * 3
    return jax.shard_map(
        shards, mesh=mesh, in_specs=placed, out_specs=(rows, rows), check_vma=False
    )
```

time: 78.4 us -> 54.6 us (0.70)
  waiting for transfers between devices: 33.6 us -> 11.5 us
  local copies, waits for them, and re-layouts: 8.32 us -> 0.06 us
  Pallas kernels: 11.5 us -> 18 us
    ppermute x7 -> x6, waiting for transfers between devices: 20.4 us -> 5.1 us  [both(): lax.ppermute(upward, 'expert', up_pairs)]
    unnamed x34 -> x6, local copies, waits for them, and re-layouts: 8.28 us -> 0.01 us
    pallas_call x8 -> x7, Pallas kernels: 11.5 us -> 18 us  [call(): pl.pallas_call(kernel, out_shape=shapes, in_specs=places, out_specs=[vmem...]
    ppermute x7 -> x6, waiting for transfers between devices: 8.23 us -> 2.11 us  [both(): lax.ppermute(downward, 'expert', down_pairs)]
    ppermute x3 -> x5, starting transfers between devices: 4.57 us -> 9.97 us  [shifted(): return lax.ppermute(part, ('section', 'expert'), moves)]
    ppermute x14 -> x3, starting transfers between devices: 3.18 us -> 0.96 us  [shards(): lax.ppermute(after(weight, message), 'expert', twin_pairs)]
    ppermute x7 -> x6, starting transfers between devices: 12.9 us -> 10.9 us  [both(): lax.ppermute(upward, 'expert', up_pairs)]
    ppermute x7 -> x6, starting transfers between devices: 2.58 us -> 2.12 us  [both(): lax.ppermute(downward, 'expert', down_pairs)]
  transfers between devices with their start and end apart: 31 -> 20, of which waited for: 13 -> 6; matrix products, arithmetic and copies ran while one was open for 0% -> 0% of each run, Pallas kernels for 13% -> 28%
where the time goes in v1:
time: 54.6 us; the launch traced here: 54.4 us
  starting transfers between devices  23.9 us (44%)
  Pallas kernels  18 us (33%)
  waiting for transfers between devices  11.5 us (21%)
  between operations  0.76 us (1%)
    pallas_call x7, Pallas kernels, call(): pl.pallas_call(kernel, out_shape=shapes, in_specs=places, out_specs=[vmem...  18 us
    ppermute x6, starting transfers between devices, both(): lax.ppermute(upward, 'expert', up_pairs)  10.9 us
    ppermute x5, starting transfers between devices, shifted(): return lax.ppermute(part, ('section', 'expert'), moves)  9.97 us
    ppermute x6, waiting for transfers between devices, both(): lax.ppermute(upward, 'expert', up_pairs)  5.1 us
    ppermute x5, waiting for transfers between devices, shifted(): return lax.ppermute(part, ('section', 'expert'), moves)  4.25 us
    ppermute x6, starting transfers between devices, both(): lax.ppermute(downward, 'expert', down_pairs)  2.12 us
    ppermute x6, waiting for transfers between devices, both(): lax.ppermute(downward, 'expert', down_pairs)  2.11 us
  transfers between devices with their start and end apart: 20, of which 6 were waited for; matrix products, arithmetic and copies ran while one was open for 0% of the time, Pallas kernels for 28%

profile of v1, /device:TPU:0, one launch (start us, length us, event | category | flops | bytes accessed | tf_op | source)
XLA Modules:
  0.0 54.4 jit_solution(236935493337513394)
XLA Ops:
  0.6 2.1 %pack.1 = (bf16[32,3200]{1,0:T(8,128)(2,1)}, bf16[32,3072]{1,0:T(8,128)(2,1)}) custom-call(bf16[32,1024]{1,0:T(8,128)(2,1)} %bitcast.26, s32[8,32]{1,0:T(8,128)} %bitcast.29, f32[8,32]{1,0:T(8,128)} %bitcast.30, bf16[32,1024]{1,0:T(8,128)(2,1)} %bitcast.27, s32[8,32]{1,0:T(8,128)} %bitcast.31, f32[8,32]{1,0:T(8,128)} %bitcast.32, bf16[32,1024]{1,0:T(8,128)(2,1)} %bitcast.28, ...), custom_call_target="tpu_custom_call" | custom-call | bytes 606208 | tf_op jit(solution)/shard_map/pack/pallas_call | solution.py:26
  3.7 2.6 %collective-permute-start.1 = (bf16[32,3200]{1,0:T(8,128)(2,1)}, bf16[32,3200]{1,0:T(8,128)(2,1)S(1)}, u32[]{:S(2)}, u32[]{:S(2)}) collective-permute-start(bf16[32,3200]{1,0:T(8,128)(2,1)} %get-tuple-element.27.refs_2_), channel_id=1, source_target_pairs={{0,4},{1,5},{4,8},{5,9},{8,12},{9,13},{12,14},{13,15},{14,10},{15,... | collective-permute-start | bytes 614408 | tf_op jit(solution)/shard_map/ppermute | solution.py:172
  6.2 1.9 %hold.1 = (bf16[1024,512]{1,0:T(8,128)(2,1)S(1)}, bf16[1024,512]{1,0:T(8,128)(2,1)S(1)}, bf16[512,1024]{1,0:T(8,128)(2,1)S(1)}) custom-call(bf16[1024,512]{1,0:T(8,128)(2,1)} %bitcast.21, bf16[1024,512]{1,0:T(8,128)(2,1)} %bitcast.23, bf16[512,1024]{1,0:T(8,128)(2,1)} %bitcast.25), custom_call_target="tpu_custom_call" | custom-call | bytes 6291456 | tf_op jit(solution)/shard_map/hold/pallas_call | solution.py:26
  8.1 4.0 %collective-permute-done.1.refs_0_ = bf16[32,3200]{1,0:T(8,128)(2,1)S(1)} collective-permute-done((bf16[32,3200]{1,0:T(8,128)(2,1)}, bf16[32,3200]{1,0:T(8,128)(2,1)S(1)}, u32[]{:S(2)}, u32[]{:S(2)}) %collective-permute-start.1) | collective-permute-done | bytes 204832 | tf_op jit(solution)/shard_map/ppermute | solution.py:172
  12.1 1.8 %collective-permute-start.7 = (bf16[32,3200]{1,0:T(8,128)(2,1)S(1)}, bf16[32,3200]{1,0:T(8,128)(2,1)S(1)}, u32[]{:S(2)}, u32[]{:S(2)}) collective-permute-start(bf16[32,3200]{1,0:T(8,128)(2,1)S(1)} %collective-permute-done.1.refs_0_), channel_id=1, source_target_pairs={{0,4},{1,5},{4,8},{5,9},{8,12},{9,13},{12,14},{13,15},{14,10},{15,... | collective-permute-start | bytes 614408 | tf_op jit(solution)/shard_map/ppermute | solution.py:172
  14.1 1.8 %collective-permute-start = (bf16[32,3072]{1,0:T(8,128)(2,1)S(1)}, bf16[32,3072]{1,0:T(8,128)(2,1)S(1)}, u32[]{:S(2)}, u32[]{:S(2)}) collective-permute-start(bf16[32,3072]{1,0:T(8,128)(2,1)S(1)} %copy-done.2), channel_id=1, source_target_pairs={{0,16},{1,17},{2,18},{3,19},{4,20},{5,21},{6,22},{7,23},{8,24},{9,... | collective-permute-start | bytes 589832 | tf_op jit(solution)/shard_map/ppermute | solution.py:183
  15.9 3.5 %expert.4 = f32[96,2048]{1,0:T(8,128)S(1)} custom-call(bf16[32,3200]{1,0:T(8,128)(2,1)S(1)} %collective-permute-done.1.refs_0_, bf16[32,3200]{1,0:T(8,128)(2,1)S(1)} %collective-permute-done.2.refs_1_, bf16[32,3200]{1,0:T(8,128)(2,1)S(1)} %copy-done, bf16[1024,512]{1,0:T(8,128)(2,1)S(1)} %get-tuple-element.31.refs_3_.refs_2_, ...), custom_call_target="tpu_custom_call" | custom-call | flops 1610612736 | bytes 7696384 | tf_op jit(solution)/shard_map/expert/pallas_call | solution.py:26
  19.5 1.6 %collective-permute-start.8 = (bf16[32,3200]{1,0:T(8,128)(2,1)S(1)}, bf16[32,3200]{1,0:T(8,128)(2,1)S(1)}, u32[]{:S(2)}, u32[]{:S(2)}) collective-permute-start(bf16[32,3200]{1,0:T(8,128)(2,1)S(1)} %collective-permute-done.7.refs_0_), channel_id=1, source_target_pairs={{0,4},{1,5},{4,8},{5,9},{8,12},{9,13},{12,14},{13,15},{14,10},{15,... | collective-permute-start | bytes 614408 | tf_op jit(solution)/shard_map/ppermute | solution.py:172
  21.6 1.1 %collective-permute-start.6 = (bf16[32,2048]{1,0:T(8,128)(2,1)S(1)}, bf16[32,2048]{1,0:T(8,128)(2,1)S(1)}, u32[]{:S(2)}, u32[]{:S(2)}) collective-permute-start(bf16[32,2048]{1,0:T(8,128)(2,1)S(1)} %slice.59), channel_id=1, source_target_pairs={{0,16},{1,17},{2,18},{3,19},{4,20},{5,21},{6,22},{7,23},{8,24},{9,... | collective-permute-start | bytes 393224 | tf_op jit(solution)/shard_map/ppermute | solution.py:183
  22.7 3.3 %expert.5 = f32[64,2048]{1,0:T(8,128)S(1)} custom-call(bf16[32,3200]{1,0:T(8,128)(2,1)S(1)} %collective-permute-done.7.refs_0_, bf16[32,3200]{1,0:T(8,128)(2,1)S(1)} %collective-permute-done.9.refs_1_, bf16[1024,512]{1,0:T(8,128)(2,1)S(1)} %get-tuple-element.31.refs_3_.refs_2_, bf16[1024,512]{1,0:T(8,128)(2,1)S(1)} %get-tuple-element.32.refs_4_.refs_3_, ...), custom_call_target="tpu_custom_call" | custom-call | flops 1073741824 | bytes 7229440 | tf_op jit(solution)/shard_map/expert/pallas_call | solution.py:26
  26.0 1.6 %collective-permute-start.10 = (bf16[16,3200]{1,0:T(8,128)(2,1)S(1)}, bf16[16,3200]{1,0:T(8,128)(2,1)S(1)}, u32[]{:S(2)}, u32[]{:S(2)}) collective-permute-start(bf16[16,3200]{1,0:T(8,128)(2,1)S(1)} %slice.31), channel_id=1, source_target_pairs={{0,4},{1,5},{4,8},{5,9},{8,12},{9,13},{12,14},{13,15},{14,10},{15,... | collective-permute-start | bytes 307208 | tf_op jit(solution)/shard_map/ppermute | solution.py:172
  27.6 3.3 %expert.6 = f32[64,2048]{1,0:T(8,128)S(1)} custom-call(bf16[32,3200]{1,0:T(8,128)(2,1)S(1)} %collective-permute-done.8.refs_0_, bf16[32,3200]{1,0:T(8,128)(2,1)S(1)} %collective-permute-done.11.refs_1_, bf16[1024,512]{1,0:T(8,128)(2,1)S(1)} %get-tuple-element.31.refs_3_.refs_2_, bf16[1024,512]{1,0:T(8,128)(2,1)S(1)} %get-tuple-element.32.refs_4_.refs_3_, ...), custom_call_target="tpu_custom_call" | custom-call | flops 1073741824 | bytes 7229440 | tf_op jit(solution)/shard_map/expert/pallas_call | solution.py:26
  30.9 0.5 collective-permute-start.12
  31.5 1.6 %collective-permute-start.14 = (bf16[32,2048]{1,0:T(8,128)(2,1)S(1)}, bf16[32,2048]{1,0:T(8,128)(2,1)S(1)}, u32[]{:S(2)}, u32[]{:S(2)}) collective-permute-start(bf16[32,2048]{1,0:T(8,128)(2,1)S(1)} %get-tuple-element.51), channel_id=1, source_target_pairs={{0,4},{1,5},{4,8},{5,9},{8,12},{9,13},{12,14},{13,15},{14,10},{15,... | collective-permute-start | bytes 393224 | tf_op jit(solution)/shard_map/ppermute | solution.py:172
  33.5 2.1 %collective-permute-done.12.refs_1_ = bf16[16,3200]{1,0:T(8,128)(2,1)S(1)} collective-permute-done((bf16[16,3200]{1,0:T(8,128)(2,1)S(1)}, bf16[16,3200]{1,0:T(8,128)(2,1)S(1)}, u32[]{:S(2)}, u32[]{:S(2)}) %collective-permute-start.12) | collective-permute-done | bytes 102432 | tf_op jit(solution)/shard_map/ppermute | solution.py:173
  35.6 3.3 %expert.7 = f32[32,2048]{1,0:T(8,128)S(1)} custom-call(bf16[16,3200]{1,0:T(8,128)(2,1)S(1)} %collective-permute-done.10.refs_0_, bf16[16,3200]{1,0:T(8,128)(2,1)S(1)} %collective-permute-done.12.refs_1_, bf16[1024,512]{1,0:T(8,128)(2,1)S(1)} %get-tuple-element.31.refs_3_.refs_2_, bf16[1024,512]{1,0:T(8,128)(2,1)S(1)} %get-tuple-element.32.refs_4_.refs_3_, ...), custom_call_target="tpu_custom_call" | custom-call | flops 536870912 | bytes 6762496 | tf_op jit(solution)/shard_map/expert/pallas_call | solution.py:26
  39.0 1.6 %collective-permute-start.16 = (bf16[32,2048]{1,0:T(8,128)(2,1)S(1)}, bf16[32,2048]{1,0:T(8,128)(2,1)S(1)}, u32[]{:S(2)}, u32[]{:S(2)}) collective-permute-start(bf16[32,2048]{1,0:T(8,128)(2,1)S(1)} %fusion.2), channel_id=1, source_target_pairs={{0,4},{1,5},{4,8},{5,9},{8,12},{9,13},{12,14},{13,15},{14,10},{15,... | collective-permute-start | bytes 393224 | tf_op jit(solution)/shard_map/ppermute | solution.py:172
  41.2 4.0 %collective-permute-start.15 = (bf16[32,2048]{1,0:T(8,128)(2,1)S(1)}, bf16[32,2048]{1,0:T(8,128)(2,1)S(1)}, u32[]{:S(2)}, u32[]{:S(2)}) collective-permute-start(bf16[32,2048]{1,0:T(8,128)(2,1)S(1)} %convert_element_type.30), channel_id=1, source_target_pairs={{0,30},{1,31},{4,26},{5,27},{8,22},{9,23},{12,18},{13,19},{14,16},... | collective-permute-start | bytes 393224 | tf_op jit(solution)/shard_map/ppermute | solution.py:183
  45.2 1.1 %collective-permute-done.16 = bf16[32,2048]{1,0:T(8,128)(2,1)S(1)} collective-permute-done((bf16[32,2048]{1,0:T(8,128)(2,1)S(1)}, bf16[32,2048]{1,0:T(8,128)(2,1)S(1)}, u32[]{:S(2)}, u32[]{:S(2)}) %collective-permute-start.16) | collective-permute-done | bytes 131104 | tf_op jit(solution)/shard_map/ppermute | solution.py:172
  46.3 1.1 %collective-permute-start.17 = (bf16[32,2048]{1,0:T(8,128)(2,1)S(1)}, bf16[32,2048]{1,0:T(8,128)(2,1)S(1)}, u32[]{:S(2)}, u32[]{:S(2)}) collective-permute-start(bf16[32,2048]{1,0:T(8,128)(2,1)S(1)} %fusion.1), channel_id=1, source_target_pairs={{0,20},{1,21},{4,24},{5,25},{8,28},{9,29},{12,30},{13,31},{14,26},... | collective-permute-start | bytes 393224 | tf_op jit(solution)/shard_map/ppermute | solution.py:183
  47.5 1.9 %collective-permute-start.19 = (bf16[32,2048]{1,0:T(8,128)(2,1)S(1)}, bf16[32,2048]{1,0:T(8,128)(2,1)S(1)}, u32[]{:S(2)}, u32[]{:S(2)}) collective-permute-start(bf16[32,2048]{1,0:T(8,128)(2,1)S(1)} %fusion), channel_id=1, source_target_pairs={{0,18},{1,19},{4,16},{5,17},{8,20},{9,21},{12,24},{13,25},{14,28},... | collective-permute-start | bytes 393224 | tf_op jit(solution)/shard_map/ppermute | solution.py:183
  49.8 2.7 %collective-permute-done.17.below = bf16[32,2048]{1,0:T(8,128)(2,1)S(1)} collective-permute-done((bf16[32,2048]{1,0:T(8,128)(2,1)S(1)}, bf16[32,2048]{1,0:T(8,128)(2,1)S(1)}, u32[]{:S(2)}, u32[]{:S(2)}) %collective-permute-start.17) | collective-permute-done | bytes 131104 | tf_op jit(solution)/shard_map/ppermute | solution.py:183
  52.5 1.1 %collective-permute-done.19.above = bf16[32,2048]{1,0:T(8,128)(2,1)S(1)} collective-permute-done((bf16[32,2048]{1,0:T(8,128)(2,1)S(1)}, bf16[32,2048]{1,0:T(8,128)(2,1)S(1)}, u32[]{:S(2)}, u32[]{:S(2)}) %collective-permute-start.19) | collective-permute-done | bytes 131104 | tf_op jit(solution)/shard_map/ppermute | solution.py:183
  53.7 0.8 %finish.1 = (bf16[32,1024]{1,0:T(8,128)(2,1)}, bf16[32,1024]{1,0:T(8,128)(2,1)}) custom-call(bf16[32,3072]{1,0:T(8,128)(2,1)S(1)} %collective-permute-done.rest, bf16[32,2048]{1,0:T(8,128)(2,1)S(1)} %collective-permute-done.6.home, bf16[32,2048]{1,0:T(8,128)(2,1)S(1)} %collective-permute-done.15.far, bf16[32,2048]{1,0:T(8,128)(2,1)S(1)} %collective-permute-done.17.below, ...), custom_call_target="tpu_custom_call" | custom-call | bytes 851968 | tf_op jit(solution)/shard_map/finish/pallas_call | solution.py:26
  (39 shorter events, 3.3 us)
Async XLA Ops:
  2.7 11.4 %collective-permute-start.3 = (bf16[1024,512]{1,0:T(8,128)(2,1)}, bf16[1024,512]{1,0:T(8,128)(2,1)S(1)}, u32[]{:S(2)}, u32[]{:S(2)}) collective-permute-start(bf16[1024,512]{1,0:T(8,128)(2,1)} %bitcast.20), channel_id=1, source_target_pairs={{0,1},{1,0},{2,3},{3,2},{4,5},{5,4},{6,7},{7,6},{8,9},{9,8},{10,11... | collective-permute-start | bytes 3145736 | tf_op jit(solution)/shard_map/ppermute | solution.py:217
  3.1 12.8 %collective-permute-start.4 = (bf16[1024,512]{1,0:T(8,128)(2,1)}, bf16[1024,512]{1,0:T(8,128)(2,1)S(1)}, u32[]{:S(2)}, u32[]{:S(2)}) collective-permute-start(bf16[1024,512]{1,0:T(8,128)(2,1)} %bitcast.22), channel_id=1, source_target_pairs={{0,1},{1,0},{2,3},{3,2},{4,5},{5,4},{6,7},{7,6},{8,9},{9,8},{10,11... | collective-permute-start | bytes 3145736 | tf_op jit(solution)/shard_map/ppermute | solution.py:217
  3.2 10.9 %copy-start.2 = (bf16[32,3072]{1,0:T(8,128)(2,1)S(1)}, bf16[32,3072]{1,0:T(8,128)(2,1)}, u32[]{:S(2)}) copy-start(bf16[32,3072]{1,0:T(8,128)(2,1)} %get-tuple-element.34) | copy-start | bytes 589828
  3.2 12.7 %copy-start = (bf16[32,3200]{1,0:T(8,128)(2,1)S(1)}, bf16[32,3200]{1,0:T(8,128)(2,1)}, u32[]{:S(2)}) copy-start(bf16[32,3200]{1,0:T(8,128)(2,1)} %get-tuple-element.27.refs_2_) | copy-start | bytes 614404
  3.2 12.7 %collective-permute-start.5 = (bf16[512,1024]{1,0:T(8,128)(2,1)}, bf16[512,1024]{1,0:T(8,128)(2,1)S(1)}, u32[]{:S(2)}, u32[]{:S(2)}) collective-permute-start(bf16[512,1024]{1,0:T(8,128)(2,1)} %bitcast.24), channel_id=1, source_target_pairs={{0,1},{1,0},{2,3},{3,2},{4,5},{5,4},{6,7},{7,6},{8,9},{9,8},{10,11... | collective-permute-start | bytes 3145736 | tf_op jit(solution)/shard_map/ppermute | solution.py:217
  3.7 8.4 %collective-permute-start.1 = (bf16[32,3200]{1,0:T(8,128)(2,1)}, bf16[32,3200]{1,0:T(8,128)(2,1)S(1)}, u32[]{:S(2)}, u32[]{:S(2)}) collective-permute-start(bf16[32,3200]{1,0:T(8,128)(2,1)} %get-tuple-element.27.refs_2_), channel_id=1, source_target_pairs={{0,4},{1,5},{4,8},{5,9},{8,12},{9,13},{12,14},{13,15},{14,10},{15,... | collective-permute-start | bytes 614408 | tf_op jit(solution)/shard_map/ppermute | solution.py:172
  6.2 7.7 %collective-permute-start.2 = (bf16[32,3200]{1,0:T(8,128)(2,1)}, bf16[32,3200]{1,0:T(8,128)(2,1)S(1)}, u32[]{:S(2)}, u32[]{:S(2)}) collective-permute-start(bf16[32,3200]{1,0:T(8,128)(2,1)} %get-tuple-element.27.refs_2_), channel_id=1, source_target_pairs={{0,2},{1,3},{4,0},{5,1},{8,4},{9,5},{12,8},{13,9},{14,12},{15,13},... | collective-permute-start | bytes 614408 | tf_op jit(solution)/shard_map/ppermute | solution.py:173
  8.1 7.8 %copy-start.1 = (f32[1,1024]{1,0:T(1,128)S(1)}, f32[1,1024]{1,0:T(1,128)}, u32[]{:S(2)}) copy-start(f32[1,1024]{1,0:T(1,128)} %refs_8_.5) | copy-start | bytes 12292
  12.1 7.3 %collective-permute-start.7 = (bf16[32,3200]{1,0:T(8,128)(2,1)S(1)}, bf16[32,3200]{1,0:T(8,128)(2,1)S(1)}, u32[]{:S(2)}, u32[]{:S(2)}) collective-permute-start(bf16[32,3200]{1,0:T(8,128)(2,1)S(1)} %collective-permute-done.1.refs_0_), channel_id=1, source_target_pairs={{0,4},{1,5},{4,8},{5,9},{8,12},{9,13},{12,14},{13,15},{14,10},{15,... | collective-permute-start | bytes 614408 | tf_op jit(solution)/shard_map/ppermute | solution.py:172
  13.9 7.2 %collective-permute-start.9 = (bf16[32,3200]{1,0:T(8,128)(2,1)S(1)}, bf16[32,3200]{1,0:T(8,128)(2,1)S(1)}, u32[]{:S(2)}, u32[]{:S(2)}) collective-permute-start(bf16[32,3200]{1,0:T(8,128)(2,1)S(1)} %collective-permute-done.2.refs_1_), channel_id=1, source_target_pairs={{0,2},{1,3},{4,0},{5,1},{8,4},{9,5},{12,8},{13,9},{14,12},{15,13},... | collective-permute-start | bytes 614408 | tf_op jit(solution)/shard_map/ppermute | solution.py:173
  14.1 8.6 %collective-permute-start = (bf16[32,3072]{1,0:T(8,128)(2,1)S(1)}, bf16[32,3072]{1,0:T(8,128)(2,1)S(1)}, u32[]{:S(2)}, u32[]{:S(2)}) collective-permute-start(bf16[32,3072]{1,0:T(8,128)(2,1)S(1)} %copy-done.2), channel_id=1, source_target_pairs={{0,16},{1,17},{2,18},{3,19},{4,20},{5,21},{6,22},{7,23},{8,24},{9,... | collective-permute-start | bytes 589832 | tf_op jit(solution)/shard_map/ppermute | solution.py:183
  19.5 6.5 %collective-permute-start.8 = (bf16[32,3200]{1,0:T(8,128)(2,1)S(1)}, bf16[32,3200]{1,0:T(8,128)(2,1)S(1)}, u32[]{:S(2)}, u32[]{:S(2)}) collective-permute-start(bf16[32,3200]{1,0:T(8,128)(2,1)S(1)} %collective-permute-done.7.refs_0_), channel_id=1, source_target_pairs={{0,4},{1,5},{4,8},{5,9},{8,12},{9,13},{12,14},{13,15},{14,10},{15,... | collective-permute-start | bytes 614408 | tf_op jit(solution)/shard_map/ppermute | solution.py:172
  21.1 6.5 %collective-permute-start.11 = (bf16[32,3200]{1,0:T(8,128)(2,1)S(1)}, bf16[32,3200]{1,0:T(8,128)(2,1)S(1)}, u32[]{:S(2)}, u32[]{:S(2)}) collective-permute-start(bf16[32,3200]{1,0:T(8,128)(2,1)S(1)} %collective-permute-done.9.refs_1_), channel_id=1, source_target_pairs={{0,2},{1,3},{4,0},{5,1},{8,4},{9,5},{12,8},{13,9},{14,12},{15,13},... | collective-permute-start | bytes 614408 | tf_op jit(solution)/shard_map/ppermute | solution.py:173
  21.6 6.1 %collective-permute-start.6 = (bf16[32,2048]{1,0:T(8,128)(2,1)S(1)}, bf16[32,2048]{1,0:T(8,128)(2,1)S(1)}, u32[]{:S(2)}, u32[]{:S(2)}) collective-permute-start(bf16[32,2048]{1,0:T(8,128)(2,1)S(1)} %slice.59), channel_id=1, source_target_pairs={{0,16},{1,17},{2,18},{3,19},{4,20},{5,21},{6,22},{7,23},{8,24},{9,... | collective-permute-start | bytes 393224 | tf_op jit(solution)/shard_map/ppermute | solution.py:183
  26.0 7.5 %collective-permute-start.10 = (bf16[16,3200]{1,0:T(8,128)(2,1)S(1)}, bf16[16,3200]{1,0:T(8,128)(2,1)S(1)}, u32[]{:S(2)}, u32[]{:S(2)}) collective-permute-start(bf16[16,3200]{1,0:T(8,128)(2,1)S(1)} %slice.31), channel_id=1, source_target_pairs={{0,4},{1,5},{4,8},{5,9},{8,12},{9,13},{12,14},{13,15},{14,10},{15,... | collective-permute-start | bytes 307208 | tf_op jit(solution)/shard_map/ppermute | solution.py:172
  30.9 4.7 %collective-permute-start.12 = (bf16[16,3200]{1,0:T(8,128)(2,1)S(1)}, bf16[16,3200]{1,0:T(8,128)(2,1)S(1)}, u32[]{:S(2)}, u32[]{:S(2)}) collective-permute-start(bf16[16,3200]{1,0:T(8,128)(2,1)S(1)} %slice.34), channel_id=1, source_target_pairs={{0,2},{1,3},{4,0},{5,1},{8,4},{9,5},{12,8},{13,9},{14,12},{15,13},... | collective-permute-start | bytes 307208 | tf_op jit(solution)/shard_map/ppermute | solution.py:173
  31.5 7.5 %collective-permute-start.14 = (bf16[32,2048]{1,0:T(8,128)(2,1)S(1)}, bf16[32,2048]{1,0:T(8,128)(2,1)S(1)}, u32[]{:S(2)}, u32[]{:S(2)}) collective-permute-start(bf16[32,2048]{1,0:T(8,128)(2,1)S(1)} %get-tuple-element.51), channel_id=1, source_target_pairs={{0,4},{1,5},{4,8},{5,9},{8,12},{9,13},{12,14},{13,15},{14,10},{15,... | collective-permute-start | bytes 393224 | tf_op jit(solution)/shard_map/ppermute | solution.py:172
  33.1 7.5 %collective-permute-start.13 = (bf16[32,2048]{1,0:T(8,128)(2,1)S(1)}, bf16[32,2048]{1,0:T(8,128)(2,1)S(1)}, u32[]{:S(2)}, u32[]{:S(2)}) collective-permute-start(bf16[32,2048]{1,0:T(8,128)(2,1)S(1)} %get-tuple-element.50), channel_id=1, source_target_pairs={{0,2},{1,3},{4,0},{5,1},{8,4},{9,5},{12,8},{13,9},{14,12},{15,13},... | collective-permute-start | bytes 393224 | tf_op jit(solution)/shard_map/ppermute | solution.py:173
  39.0 7.3 %collective-permute-start.16 = (bf16[32,2048]{1,0:T(8,128)(2,1)S(1)}, bf16[32,2048]{1,0:T(8,128)(2,1)S(1)}, u32[]{:S(2)}, u32[]{:S(2)}) collective-permute-start(bf16[32,2048]{1,0:T(8,128)(2,1)S(1)} %fusion.2), channel_id=1, source_target_pairs={{0,4},{1,5},{4,8},{5,9},{8,12},{9,13},{12,14},{13,15},{14,10},{15,... | collective-permute-start | bytes 393224 | tf_op jit(solution)/shard_map/ppermute | solution.py:172
  40.6 6.8 %collective-permute-start.18 = (bf16[32,2048]{1,0:T(8,128)(2,1)S(1)}, bf16[32,2048]{1,0:T(8,128)(2,1)S(1)}, u32[]{:S(2)}, u32[]{:S(2)}) collective-permute-start(bf16[32,2048]{1,0:T(8,128)(2,1)S(1)} %fusion.3), channel_id=1, source_target_pairs={{0,2},{1,3},{4,0},{5,1},{8,4},{9,5},{12,8},{13,9},{14,12},{15,13},... | collective-permute-start | bytes 393224 | tf_op jit(solution)/shard_map/ppermute | solution.py:173
  41.2 8.7 %collective-permute-start.15 = (bf16[32,2048]{1,0:T(8,128)(2,1)S(1)}, bf16[32,2048]{1,0:T(8,128)(2,1)S(1)}, u32[]{:S(2)}, u32[]{:S(2)}) collective-permute-start(bf16[32,2048]{1,0:T(8,128)(2,1)S(1)} %convert_element_type.30), channel_id=1, source_target_pairs={{0,30},{1,31},{4,26},{5,27},{8,22},{9,23},{12,18},{13,19},{14,16},... | collective-permute-start | bytes 393224 | tf_op jit(solution)/shard_map/ppermute | solution.py:183
  46.3 6.2 %collective-permute-start.17 = (bf16[32,2048]{1,0:T(8,128)(2,1)S(1)}, bf16[32,2048]{1,0:T(8,128)(2,1)S(1)}, u32[]{:S(2)}, u32[]{:S(2)}) collective-permute-start(bf16[32,2048]{1,0:T(8,128)(2,1)S(1)} %fusion.1), channel_id=1, source_target_pairs={{0,20},{1,21},{4,24},{5,25},{8,28},{9,29},{12,30},{13,31},{14,26},... | collective-permute-start | bytes 393224 | tf_op jit(solution)/shard_map/ppermute | solution.py:183
  47.5 6.2 %collective-permute-start.19 = (bf16[32,2048]{1,0:T(8,128)(2,1)S(1)}, bf16[32,2048]{1,0:T(8,128)(2,1)S(1)}, u32[]{:S(2)}, u32[]{:S(2)}) collective-permute-start(bf16[32,2048]{1,0:T(8,128)(2,1)S(1)} %fusion), channel_id=1, source_target_pairs={{0,18},{1,19},{4,16},{5,17},{8,20},{9,21},{12,24},{13,25},{14,28},... | collective-permute-start | bytes 393224 | tf_op jit(solution)/shard_map/ppermute | solution.py:183

commit v2 on v1

--- a/solution.py
+++ b/solution.py
@@ -52,7 +52,7 @@
     return -(-4 * experts // 128) * 128
 
 
-def pack_kernel(experts, fr, frt, fw, rr, rrt, rw, ct, gain, msg, rest):
+def pack_kernel(experts, fr, frt, fw, rr, rrt, rw, ct, gain, msg):
     tokens, width = fr.shape
     lanes = table_lanes(experts)
     for j, rows in ((0, fr), (1, rr)):
@@ -60,8 +60,6 @@
         inverse = lax.rsqrt(jnp.mean(wide * wide, axis=-1, keepdims=True) + epsilon)
         msg[:, j * width : (j + 1) * width] = (wide * inverse * gain[...]).astype(BF16)
     msg[:, 2 * width : 3 * width] = ct[...]
-    for j, rows in enumerate((fr, rr, ct)):
-        rest[:, j * width : (j + 1) * width] = rows[...]
     row = lax.broadcasted_iota(jnp.int32, (lanes, tokens), 0)
     table = jnp.zeros((lanes, tokens), F32)
     for group, (routes, weights) in enumerate(((frt, fw), (frt, fw), (rrt, rw), (rrt, rw))):
@@ -131,18 +129,18 @@
     out[:, width:] = rear * gain[...]
 
 
-def finish_kernel(rest, home, far, below, above, front, rear):
+def finish_kernel(home, far, below, above, front, rear):
     width = front.shape[1]
-    total = home[...].astype(F32) + far[...].astype(F32)
-    total = total + below[...].astype(F32) + above[...].astype(F32)
-    front[...] = (rest[:, :width].astype(F32) + total[:, :width]).astype(BF16)
-    wide = rest[:, width : 2 * width].astype(F32)
-    inverse = lax.rsqrt(jnp.mean(wide * wide, axis=-1, keepdims=True) + epsilon)
-    grad = total[:, width:]
-    along = jnp.mean(wide * grad, axis=-1, keepdims=True)
+    own, rows, own_grad, rear_rows, cotangent = (
+        home[:, j * width : (j + 1) * width].astype(F32) for j in range(5)
+    )
+    total = far[...].astype(F32) + below[...].astype(F32) + above[...].astype(F32)
+    front[...] = (rows + (own + total[:, :width])).astype(BF16)
+    inverse = lax.rsqrt(jnp.mean(rear_rows * rear_rows, axis=-1, keepdims=True) + epsilon)
+    grad = own_grad + total[:, width:]
+    along = jnp.mean(rear_rows * grad, axis=-1, keepdims=True)
     cubed = inverse * inverse * inverse
-    cotangent = rest[:, 2 * width :].astype(F32)
-    rear[...] = (cotangent + inverse * grad - wide * cubed * along).astype(BF16)
+    rear[...] = (cotangent + inverse * grad - rear_rows * cubed * along).astype(BF16)
 
 
 def shards(
@@ -161,7 +159,6 @@
     experts = lax.axis_size("expert")
     sections = lax.axis_size("section")
     tokens, width = front_rows.shape[1:]
-    half = tokens // 2
     reach = experts // 4
     lanes = table_lanes(experts)
     up_pairs, down_pairs = ring_pairs(experts, 1), ring_pairs(experts, -1)
@@ -173,7 +170,7 @@
             lax.ppermute(downward, "expert", down_pairs),
         )
 
-    def across(value, pairs):
+    def across(value, pairs, ahead):
         def shifted(part, by):
             moves = [
                 (s * experts + a, (s + by) % sections * experts + b)
@@ -184,13 +181,13 @@
 
         if sections == 2:
             return shifted(value, 1)
-        parts = [shifted(value[:, :width], 1), shifted(value[:, width:], -1)]
+        parts = [shifted(value[:, :ahead], 1), shifted(value[:, ahead:], -1)]
         return jnp.concatenate(parts, axis=1)
 
-    message, rest = call(
+    (message,) = call(
         functools.partial(pack_kernel, experts),
         "pack",
-        [((tokens, 3 * width + lanes), BF16), ((tokens, 3 * width), BF16)],
+        [((tokens, 3 * width + lanes), BF16)],
         front_rows[0],
         front_routes[0].T,
         front_weights[0].T,
@@ -205,14 +202,16 @@
         return lax.optimization_barrier((value, *first))[0]
 
     weights = [gate_weight[0, 0], up_weight[0, 0], down_weight[0, 0]]
-    held = call(
+    kept = [*weights, front_rows[0], rear_rows[0], rear_cotangent[0]]
+    *held, rows, rear, cotangent = call(
         hold_kernel,
         "hold",
-        [(weight.shape, weight.dtype) for weight in weights],
-        *[after(weight, message) for weight in weights],
+        [(value.shape, value.dtype) for value in kept],
+        *[after(value, message) for value in kept],
         limit=HOLD_LIMIT,
-        scratch=[pltpu.SemaphoreType.DMA((len(weights),))],
-        anywhere=range(len(weights)),
+        flops=20000000000,
+        scratch=[pltpu.SemaphoreType.DMA((len(kept),))],
+        anywhere=range(len(kept)),
     )
     moved = [lax.ppermute(after(weight, message), "expert", twin_pairs) for weight in weights]
     held = [*held, *moved]
@@ -231,23 +230,20 @@
 
     below, above = both(message, message)
     here = [(i, i) for i in range(experts)]
-    rest = across(after(rest, *held[: len(weights)]), here)
     results = []
     for step in range(1, reach):
         below = after(below, *(results[-1:] or held[: len(weights)]))
         above = after(above, below)
         mine = (below, above)
-        if step == reach - 2:
-            mine = (after(below, rest), above)
-        if step == reach - 1:
-            mine = (after(below, home), above)
         if step < reach - 1:
             below, above = both(below, above)
         else:
-            below, above = both(below[:half], above[half:])
+            below = lax.ppermute(below, "expert", up_pairs)
         results.append(expert_of(*mine, *([message] if step == 1 else [])))
         if step == 1:
-            home = across(results[0][2 * tokens :].astype(BF16), here)
+            home = results[0][2 * tokens :].astype(BF16)
+            home = [home[:, :width], rows, home[:, width:], rear, cotangent]
+            home = across(jnp.concatenate(home, axis=1), here, 2 * width)
     from_below = from_above = None
     for step in range(reach - 1, 0, -1):
         to_above = results[step - 1][tokens : 2 * tokens]
@@ -255,6 +251,8 @@
         if step < reach - 1:
             to_above = to_above + from_below.astype(F32)
         to_above = to_above.astype(BF16)
+        if step == reach - 1:
+            to_above = after(to_above, home)
         if step == reach - 2:
             to_above = after(to_above, far)
         if step < reach - 1:
@@ -262,14 +260,14 @@
             to_below = to_below + from_above.astype(F32)
         to_below = to_below.astype(BF16)
         if step == reach - 1:
-            far = expert_of(after(below, to_above, to_below), above).astype(BF16)
+            far = expert_of(after(below, to_above, to_below)).astype(BF16)
         if step == reach - 2:
-            far = across(after(far, to_below), ring_pairs(experts, reach))
+            far = across(after(far, to_below), ring_pairs(experts, reach), width)
         if step > 1:
             from_below, from_above = both(to_above, to_below)
-    from_below, from_above = across(to_above, up_pairs), across(to_below, down_pairs)
+    from_below, from_above = across(to_above, up_pairs, width), across(to_below, down_pairs, width)
     front, rear = call(
-        finish_kernel, "finish", [((tokens, width), BF16)] * 2, rest, home, far, from_below, from_above
+        finish_kernel, "finish", [((tokens, width), BF16)] * 2, home, far, from_below, from_above
     )
     return (front[None], rear[None])
 

time: 54.6 us -> 50.4 us (0.923)
  waiting for transfers between devices: 11.5 us -> 8.73 us
  starting transfers between devices: 23.9 us -> 22.2 us
    ppermute x6 -> x5, waiting for transfers between devices: 5.1 us -> 3.32 us  [both(): lax.ppermute(upward, 'expert', up_pairs)]
    ppermute x6 -> x5, waiting for transfers between devices: 2.11 us -> 0.45 us  [both(): lax.ppermute(downward, 'expert', down_pairs)]
    ppermute x0 -> x1, starting transfers between devices: none -> 1.62 us  [shards(): below = lax.ppermute(below, 'expert', up_pairs)]
    ppermute x6 -> x5, starting transfers between devices: 10.9 us -> 9.64 us  [both(): lax.ppermute(upward, 'expert', up_pairs)]
    ppermute x5 -> x4, starting transfers between devices: 9.97 us -> 8.76 us  [shifted(): return lax.ppermute(part, ('section', 'expert'), moves)]
    ppermute x5 -> x4, waiting for transfers between devices: 4.25 us -> 4.95 us  [shifted(): return lax.ppermute(part, ('section', 'expert'), moves)]
    ppermute x6 -> x5, starting transfers between devices: 2.12 us -> 1.7 us  [both(): lax.ppermute(downward, 'expert', down_pairs)]
  transfers between devices with their start and end apart: 20 -> 18, of which waited for: 6 -> 6; matrix products, arithmetic and copies ran while one was open for 0% -> 1% of each run, Pallas kernels for 28% -> 30%
where the time goes in v2:
time: 50.4 us; the launch traced here: 50.2 us
  starting transfers between devices  22.2 us (44%)
  Pallas kernels  18.1 us (36%)
  waiting for transfers between devices  8.73 us (17%)
  between operations  0.82 us (2%)
    pallas_call x7, Pallas kernels, call(): pl.pallas_call(kernel, out_shape=shapes, in_specs=places, out_specs=[vmem...  18.1 us
    ppermute x5, starting transfers between devices, both(): lax.ppermute(upward, 'expert', up_pairs)  9.64 us
    ppermute x4, starting transfers between devices, shifted(): return lax.ppermute(part, ('section', 'expert'), moves)  8.76 us
    ppermute x4, waiting for transfers between devices, shifted(): return lax.ppermute(part, ('section', 'expert'), moves)  4.95 us
    ppermute x5, waiting for transfers between devices, both(): lax.ppermute(upward, 'expert', up_pairs)  3.32 us
    ppermute x5, starting transfers between devices, both(): lax.ppermute(downward, 'expert', down_pairs)  1.7 us
    ppermute x1, starting transfers between devices, shards(): below = lax.ppermute(below, 'expert', up_pairs)  1.62 us
  transfers between devices with their start and end apart: 18, of which 6 were waited for; matrix products, arithmetic and copies ran while one was open for 1% of the time, Pallas kernels for 30%

profile of v2, /device:TPU:0, one launch (start us, length us, event | category | flops | bytes accessed | tf_op | source)
XLA Modules:
  0.0 50.2 jit_solution(11886278261595380496)
XLA Ops:
  0.7 2.1 %pack.1.refs_2_ = bf16[32,3200]{1,0:T(8,128)(2,1)} custom-call(bf16[32,1024]{1,0:T(8,128)(2,1)} %bitcast.20, s32[8,32]{1,0:T(8,128)} %bitcast.26, f32[8,32]{1,0:T(8,128)} %bitcast.27, bf16[32,1024]{1,0:T(8,128)(2,1)} %bitcast.22, s32[8,32]{1,0:T(8,128)} %bitcast.28, f32[8,32]{1,0:T(8,128)} %bitcast.29, bf16[32,1024]{1,0:T(8,128)(2,1)} %bitcast.24, ...), custom_call_target="tpu_custom_call" | custom-call | bytes 409600 | tf_op jit(solution)/shard_map/pack/pallas_call | solution.py:26
  2.7 3.0 %collective-permute-start = (bf16[32,3200]{1,0:T(8,128)(2,1)}, bf16[32,3200]{1,0:T(8,128)(2,1)S(1)}, u32[]{:S(2)}, u32[]{:S(2)}) collective-permute-start(bf16[32,3200]{1,0:T(8,128)(2,1)} %pack.1.refs_2_), channel_id=1, source_target_pairs={{0,4},{1,5},{4,8},{5,9},{8,12},{9,13},{12,14},{13,15},{14,10},{15,... | collective-permute-start | bytes 614408 | tf_op jit(solution)/shard_map/ppermute | solution.py:169
  5.8 0.5 %collective-permute-start.3 = (bf16[1024,512]{1,0:T(8,128)(2,1)}, bf16[1024,512]{1,0:T(8,128)(2,1)S(1)}, u32[]{:S(2)}, u32[]{:S(2)}) collective-permute-start(bf16[1024,512]{1,0:T(8,128)(2,1)} %bitcast.32), channel_id=1, source_target_pairs={{0,1},{1,0},{2,3},{3,2},{4,5},{5,4},{6,7},{7,6},{8,9},{9,8},{10,11... | collective-permute-start | bytes 3145736 | tf_op jit(solution)/shard_map/ppermute | solution.py:216
  6.3 2.0 %hold.1 = (bf16[1024,512]{1,0:T(8,128)(2,1)S(1)}, bf16[1024,512]{1,0:T(8,128)(2,1)S(1)}, bf16[512,1024]{1,0:T(8,128)(2,1)S(1)}, bf16[32,1024]{1,0:T(8,128)(2,1)S...) custom-call(bf16[1024,512]{1,0:T(8,128)(2,1)} %bitcast.31, bf16[1024,512]{1,0:T(8,128)(2,1)} %bitcast.33, ...), custom_call_target="tpu_custom_call" | custom-call | flops 20000000000 | bytes 6684672 | tf_op jit(solution)/shard_map/hold/pallas_call | solution.py:26
  8.3 2.7 %collective-permute-done.refs_0_ = bf16[32,3200]{1,0:T(8,128)(2,1)S(1)} collective-permute-done((bf16[32,3200]{1,0:T(8,128)(2,1)}, bf16[32,3200]{1,0:T(8,128)(2,1)S(1)}, u32[]{:S(2)}, u32[]{:S(2)}) %collective-permute-start) | collective-permute-done | bytes 204832 | tf_op jit(solution)/shard_map/ppermute | solution.py:169
  11.0 1.8 %collective-permute-start.6 = (bf16[32,3200]{1,0:T(8,128)(2,1)S(1)}, bf16[32,3200]{1,0:T(8,128)(2,1)S(1)}, u32[]{:S(2)}, u32[]{:S(2)}) collective-permute-start(bf16[32,3200]{1,0:T(8,128)(2,1)S(1)} %collective-permute-done.refs_0_), channel_id=1, source_target_pairs={{0,4},{1,5},{4,8},{5,9},{8,12},{9,13},{12,14},{13,15},{14,10},{15,... | collective-permute-start | bytes 614408 | tf_op jit(solution)/shard_map/ppermute | solution.py:169
  13.0 3.5 %expert.4 = f32[96,2048]{1,0:T(8,128)S(1)} custom-call(bf16[32,3200]{1,0:T(8,128)(2,1)S(1)} %collective-permute-done.refs_0_, bf16[32,3200]{1,0:T(8,128)(2,1)S(1)} %collective-permute-done.1.refs_1_, bf16[32,3200]{1,0:T(8,128)(2,1)S(1)} %copy-done, bf16[1024,512]{1,0:T(8,128)(2,1)S(1)} %get-tuple-element.34.refs_3_.refs_2_.refs_1_, ...), custom_call_target="tpu_custom_call" | custom-call | flops 1610612736 | bytes 7696384 | tf_op jit(solution)/shard_map/expert/pallas_call | solution.py:26
  16.6 0.6 %collective-permute-done.6.refs_0_ = bf16[32,3200]{1,0:T(8,128)(2,1)S(1)} collective-permute-done((bf16[32,3200]{1,0:T(8,128)(2,1)S(1)}, bf16[32,3200]{1,0:T(8,128)(2,1)S(1)}, u32[]{:S(2)}, u32[]{:S(2)}) %collective-permute-start.6) | collective-permute-done | bytes 204832 | tf_op jit(solution)/shard_map/ppermute | solution.py:169
  17.2 1.5 %collective-permute-start.7 = (bf16[32,3200]{1,0:T(8,128)(2,1)S(1)}, bf16[32,3200]{1,0:T(8,128)(2,1)S(1)}, u32[]{:S(2)}, u32[]{:S(2)}) collective-permute-start(bf16[32,3200]{1,0:T(8,128)(2,1)S(1)} %collective-permute-done.6.refs_0_), channel_id=1, source_target_pairs={{0,4},{1,5},{4,8},{5,9},{8,12},{9,13},{12,14},{13,15},{14,10},{15,... | collective-permute-start | bytes 614408 | tf_op jit(solution)/shard_map/ppermute | solution.py:169
  18.8 0.6 %collective-permute-start.10 = (bf16[32,3200]{1,0:T(8,128)(2,1)S(1)}, bf16[32,3200]{1,0:T(8,128)(2,1)S(1)}, u32[]{:S(2)}, u32[]{:S(2)}) collective-permute-start(bf16[32,3200]{1,0:T(8,128)(2,1)S(1)} %collective-permute-done.8.refs_1_), channel_id=1, source_target_pairs={{0,2},{1,3},{4,0},{5,1},{8,4},{9,5},{12,8},{13,9},{14,12},{15,13},... | collective-permute-start | bytes 614408 | tf_op jit(solution)/shard_map/ppermute | solution.py:170
  19.4 1.5 %collective-permute-start.5 = (bf16[32,5120]{1,0:T(8,128)(2,1)S(1)}, bf16[32,5120]{1,0:T(8,128)(2,1)S(1)}, u32[]{:S(2)}, u32[]{:S(2)}) collective-permute-start(bf16[32,5120]{1,0:T(8,128)(2,1)S(1)} %constant_dynamic-update-slice_fusion), channel_id=1, source_target_pairs={{0,16},{1,17},{2,18},{3,19},{4,20},{5,21},{6,22},{7,23},{8,24},{9,... | collective-permute-start | bytes 983048 | tf_op jit(solution)/shard_map/ppermute | solution.py:180
  20.9 3.3 %expert.5 = f32[64,2048]{1,0:T(8,128)S(1)} custom-call(bf16[32,3200]{1,0:T(8,128)(2,1)S(1)} %collective-permute-done.6.refs_0_, bf16[32,3200]{1,0:T(8,128)(2,1)S(1)} %collective-permute-done.8.refs_1_, bf16[1024,512]{1,0:T(8,128)(2,1)S(1)} %get-tuple-element.34.refs_3_.refs_2_.refs_1_, bf16[1024,512]{1,0:T(8,128)(2,1)S(1)} %get-tuple-element.35.refs_4_.refs_3_.refs_2_, ...), custom_call_target="tpu_custom_call" | custom-call | flops 1073741824 | bytes 7229440 | tf_op jit(solution)/shard_map/expert/pallas_call | solution.py:26
  24.1 1.6 %collective-permute-start.9 = (bf16[32,3200]{1,0:T(8,128)(2,1)S(1)}, bf16[32,3200]{1,0:T(8,128)(2,1)S(1)}, u32[]{:S(2)}, u32[]{:S(2)}) collective-permute-start(bf16[32,3200]{1,0:T(8,128)(2,1)S(1)} %collective-permute-done.7.refs_0_), channel_id=1, source_target_pairs={{0,4},{1,5},{4,8},{5,9},{8,12},{9,13},{12,14},{13,15},{14,10},{15,... | collective-permute-start | bytes 614408 | tf_op jit(solution)/shard_map/ppermute | solution.py:241
  25.8 3.2 %expert.6 = f32[64,2048]{1,0:T(8,128)S(1)} custom-call(bf16[32,3200]{1,0:T(8,128)(2,1)S(1)} %collective-permute-done.7.refs_0_, bf16[32,3200]{1,0:T(8,128)(2,1)S(1)} %collective-permute-done.10.refs_1_, bf16[1024,512]{1,0:T(8,128)(2,1)S(1)} %get-tuple-element.34.refs_3_.refs_2_.refs_1_, bf16[1024,512]{1,0:T(8,128)(2,1)S(1)} %get-tuple-element.35.refs_4_.refs_3_.refs_2_, ...), custom_call_target="tpu_custom_call" | custom-call | flops 1073741824 | bytes 7229440 | tf_op jit(solution)/shard_map/expert/pallas_call | solution.py:26
  29.1 1.6 %collective-permute-start.12 = (bf16[32,2048]{1,0:T(8,128)(2,1)S(1)}, bf16[32,2048]{1,0:T(8,128)(2,1)S(1)}, u32[]{:S(2)}, u32[]{:S(2)}) collective-permute-start(bf16[32,2048]{1,0:T(8,128)(2,1)S(1)} %get-tuple-element.46), channel_id=1, source_target_pairs={{0,4},{1,5},{4,8},{5,9},{8,12},{9,13},{12,14},{13,15},{14,10},{15,... | collective-permute-start | bytes 393224 | tf_op jit(solution)/shard_map/ppermute | solution.py:169
  31.2 3.3 %expert.7 = f32[32,2048]{1,0:T(8,128)S(1)} custom-call(bf16[32,3200]{1,0:T(8,128)(2,1)S(1)} %collective-permute-done.9.refs_0_, bf16[1024,512]{1,0:T(8,128)(2,1)S(1)} %get-tuple-element.34.refs_3_.refs_2_.refs_1_, bf16[1024,512]{1,0:T(8,128)(2,1)S(1)} %get-tuple-element.35.refs_4_.refs_3_.refs_2_, ...), custom_call_target="tpu_custom_call" | custom-call | flops 536870912 | bytes 6762496 | tf_op jit(solution)/shard_map/expert/pallas_call | solution.py:26
  34.5 1.6 %collective-permute-start.14 = (bf16[32,2048]{1,0:T(8,128)(2,1)S(1)}, bf16[32,2048]{1,0:T(8,128)(2,1)S(1)}, u32[]{:S(2)}, u32[]{:S(2)}) collective-permute-start(bf16[32,2048]{1,0:T(8,128)(2,1)S(1)} %fusion.2), channel_id=1, source_target_pairs={{0,4},{1,5},{4,8},{5,9},{8,12},{9,13},{12,14},{13,15},{14,10},{15,... | collective-permute-start | bytes 393224 | tf_op jit(solution)/shard_map/ppermute | solution.py:169
  36.7 4.7 %collective-permute-start.13 = (bf16[32,2048]{1,0:T(8,128)(2,1)S(1)}, bf16[32,2048]{1,0:T(8,128)(2,1)S(1)}, u32[]{:S(2)}, u32[]{:S(2)}) collective-permute-start(bf16[32,2048]{1,0:T(8,128)(2,1)S(1)} %convert_element_type.30), channel_id=1, source_target_pairs={{0,30},{1,31},{4,26},{5,27},{8,22},{9,23},{12,18},{13,19},{14,16},... | collective-permute-start | bytes 393224 | tf_op jit(solution)/shard_map/ppermute | solution.py:180
  41.4 1.4 %collective-permute-start.15 = (bf16[32,2048]{1,0:T(8,128)(2,1)S(1)}, bf16[32,2048]{1,0:T(8,128)(2,1)S(1)}, u32[]{:S(2)}, u32[]{:S(2)}) collective-permute-start(bf16[32,2048]{1,0:T(8,128)(2,1)S(1)} %fusion.1), channel_id=1, source_target_pairs={{0,20},{1,21},{4,24},{5,25},{8,28},{9,29},{12,30},{13,31},{14,26},... | collective-permute-start | bytes 393224 | tf_op jit(solution)/shard_map/ppermute | solution.py:180
  43.3 1.2 %collective-permute-start.17 = (bf16[32,2048]{1,0:T(8,128)(2,1)S(1)}, bf16[32,2048]{1,0:T(8,128)(2,1)S(1)}, u32[]{:S(2)}, u32[]{:S(2)}) collective-permute-start(bf16[32,2048]{1,0:T(8,128)(2,1)S(1)} %fusion), channel_id=1, source_target_pairs={{0,18},{1,19},{4,16},{5,17},{8,20},{9,21},{12,24},{13,25},{14,28},... | collective-permute-start | bytes 393224 | tf_op jit(solution)/shard_map/ppermute | solution.py:180
  44.5 1.1 %collective-permute-done.13.far = bf16[32,2048]{1,0:T(8,128)(2,1)S(1)} collective-permute-done((bf16[32,2048]{1,0:T(8,128)(2,1)S(1)}, bf16[32,2048]{1,0:T(8,128)(2,1)S(1)}, u32[]{:S(2)}, u32[]{:S(2)}) %collective-permute-start.13) | collective-permute-done | bytes 131104 | tf_op jit(solution)/shard_map/ppermute | solution.py:180
  45.5 1.8 %collective-permute-done.15.below = bf16[32,2048]{1,0:T(8,128)(2,1)S(1)} collective-permute-done((bf16[32,2048]{1,0:T(8,128)(2,1)S(1)}, bf16[32,2048]{1,0:T(8,128)(2,1)S(1)}, u32[]{:S(2)}, u32[]{:S(2)}) %collective-permute-start.15) | collective-permute-done | bytes 131104 | tf_op jit(solution)/shard_map/ppermute | solution.py:180
  47.3 2.1 %collective-permute-done.17.above = bf16[32,2048]{1,0:T(8,128)(2,1)S(1)} collective-permute-done((bf16[32,2048]{1,0:T(8,128)(2,1)S(1)}, bf16[32,2048]{1,0:T(8,128)(2,1)S(1)}, u32[]{:S(2)}, u32[]{:S(2)}) %collective-permute-start.17) | collective-permute-done | bytes 131104 | tf_op jit(solution)/shard_map/ppermute | solution.py:180
  49.4 0.8 %finish.1 = (bf16[32,1024]{1,0:T(8,128)(2,1)}, bf16[32,1024]{1,0:T(8,128)(2,1)}) custom-call(bf16[32,5120]{1,0:T(8,128)(2,1)S(1)} %collective-permute-done.5.home, bf16[32,2048]{1,0:T(8,128)(2,1)S(1)} %collective-permute-done.13.far, bf16[32,2048]{1,0:T(8,128)(2,1)S(1)} %collective-permute-done.15.below, bf16[32,2048]{1,0:T(8,128)(2,1)S(1)} %collective-permute-done.17.above), custom_call_target="tpu_custom_call" | custom-call | bytes 851968 | tf_op jit(solution)/shard_map/finish/pallas_call | solution.py:26
  (42 shorter events, 1.9 us)
Async XLA Ops:
  0.6 5.7 %copy-start.2 = (bf16[1,32,1024]{2,1,0:T(8,128)(2,1)S(1)}, bf16[1,32,1024]{2,1,0:T(8,128)(2,1)}, u32[]{:S(2)}) copy-start(bf16[1,32,1024]{2,1,0:T(8,128)(2,1)} %param.11) | copy-start | bytes 196612
  0.6 5.7 %copy-start.3 = (bf16[1,32,1024]{2,1,0:T(8,128)(2,1)S(1)}, bf16[1,32,1024]{2,1,0:T(8,128)(2,1)}, u32[]{:S(2)}) copy-start(bf16[1,32,1024]{2,1,0:T(8,128)(2,1)} %param.14) | copy-start | bytes 196612
  0.7 5.7 %copy-start.4 = (bf16[1,32,1024]{2,1,0:T(8,128)(2,1)S(1)}, bf16[1,32,1024]{2,1,0:T(8,128)(2,1)}, u32[]{:S(2)}) copy-start(bf16[1,32,1024]{2,1,0:T(8,128)(2,1)} %param.17) | copy-start | bytes 196612
  2.7 8.2 %collective-permute-start = (bf16[32,3200]{1,0:T(8,128)(2,1)}, bf16[32,3200]{1,0:T(8,128)(2,1)S(1)}, u32[]{:S(2)}, u32[]{:S(2)}) collective-permute-start(bf16[32,3200]{1,0:T(8,128)(2,1)} %pack.1.refs_2_), channel_id=1, source_target_pairs={{0,4},{1,5},{4,8},{5,9},{8,12},{9,13},{12,14},{13,15},{14,10},{15,... | collective-permute-start | bytes 614408 | tf_op jit(solution)/shard_map/ppermute | solution.py:169
  5.8 7.0 %collective-permute-start.1 = (bf16[32,3200]{1,0:T(8,128)(2,1)}, bf16[32,3200]{1,0:T(8,128)(2,1)S(1)}, u32[]{:S(2)}, u32[]{:S(2)}) collective-permute-start(bf16[32,3200]{1,0:T(8,128)(2,1)} %pack.1.refs_2_), channel_id=1, source_target_pairs={{0,2},{1,3},{4,0},{5,1},{8,4},{9,5},{12,8},{13,9},{14,12},{15,13},... | collective-permute-start | bytes 614408 | tf_op jit(solution)/shard_map/ppermute | solution.py:170
  5.8 7.2 %collective-permute-start.2 = (bf16[1024,512]{1,0:T(8,128)(2,1)}, bf16[1024,512]{1,0:T(8,128)(2,1)S(1)}, u32[]{:S(2)}, u32[]{:S(2)}) collective-permute-start(bf16[1024,512]{1,0:T(8,128)(2,1)} %bitcast.30), channel_id=1, source_target_pairs={{0,1},{1,0},{2,3},{3,2},{4,5},{5,4},{6,7},{7,6},{8,9},{9,8},{10,11... | collective-permute-start | bytes 3145736 | tf_op jit(solution)/shard_map/ppermute | solution.py:216
  5.8 7.2 %collective-permute-start.3 = (bf16[1024,512]{1,0:T(8,128)(2,1)}, bf16[1024,512]{1,0:T(8,128)(2,1)S(1)}, u32[]{:S(2)}, u32[]{:S(2)}) collective-permute-start(bf16[1024,512]{1,0:T(8,128)(2,1)} %bitcast.32), channel_id=1, source_target_pairs={{0,1},{1,0},{2,3},{3,2},{4,5},{5,4},{6,7},{7,6},{8,9},{9,8},{10,11... | collective-permute-start | bytes 3145736 | tf_op jit(solution)/shard_map/ppermute | solution.py:216
  6.3 6.7 %copy-start = (bf16[32,3200]{1,0:T(8,128)(2,1)S(1)}, bf16[32,3200]{1,0:T(8,128)(2,1)}, u32[]{:S(2)}) copy-start(bf16[32,3200]{1,0:T(8,128)(2,1)} %pack.1.refs_2_) | copy-start | bytes 614404
  6.3 6.7 %collective-permute-start.4 = (bf16[512,1024]{1,0:T(8,128)(2,1)}, bf16[512,1024]{1,0:T(8,128)(2,1)S(1)}, u32[]{:S(2)}, u32[]{:S(2)}) collective-permute-start(bf16[512,1024]{1,0:T(8,128)(2,1)} %bitcast.34), channel_id=1, source_target_pairs={{0,1},{1,0},{2,3},{3,2},{4,5},{5,4},{6,7},{7,6},{8,9},{9,8},{10,11... | collective-permute-start | bytes 3145736 | tf_op jit(solution)/shard_map/ppermute | solution.py:216
  8.3 4.8 %copy-start.1 = (f32[1,1024]{1,0:T(1,128)S(1)}, f32[1,1024]{1,0:T(1,128)}, u32[]{:S(2)}) copy-start(f32[1,1024]{1,0:T(1,128)} %refs_7_.1) | copy-start | bytes 12292
  11.0 6.3 %collective-permute-start.6 = (bf16[32,3200]{1,0:T(8,128)(2,1)S(1)}, bf16[32,3200]{1,0:T(8,128)(2,1)S(1)}, u32[]{:S(2)}, u32[]{:S(2)}) collective-permute-start(bf16[32,3200]{1,0:T(8,128)(2,1)S(1)} %collective-permute-done.refs_0_), channel_id=1, source_target_pairs={{0,4},{1,5},{4,8},{5,9},{8,12},{9,13},{12,14},{13,15},{14,10},{15,... | collective-permute-start | bytes 614408 | tf_op jit(solution)/shard_map/ppermute | solution.py:169
  12.8 6.0 %collective-permute-start.8 = (bf16[32,3200]{1,0:T(8,128)(2,1)S(1)}, bf16[32,3200]{1,0:T(8,128)(2,1)S(1)}, u32[]{:S(2)}, u32[]{:S(2)}) collective-permute-start(bf16[32,3200]{1,0:T(8,128)(2,1)S(1)} %collective-permute-done.1.refs_1_), channel_id=1, source_target_pairs={{0,2},{1,3},{4,0},{5,1},{8,4},{9,5},{12,8},{13,9},{14,12},{15,13},... | collective-permute-start | bytes 614408 | tf_op jit(solution)/shard_map/ppermute | solution.py:170
  17.2 6.9 %collective-permute-start.7 = (bf16[32,3200]{1,0:T(8,128)(2,1)S(1)}, bf16[32,3200]{1,0:T(8,128)(2,1)S(1)}, u32[]{:S(2)}, u32[]{:S(2)}) collective-permute-start(bf16[32,3200]{1,0:T(8,128)(2,1)S(1)} %collective-permute-done.6.refs_0_), channel_id=1, source_target_pairs={{0,4},{1,5},{4,8},{5,9},{8,12},{9,13},{12,14},{13,15},{14,10},{15,... | collective-permute-start | bytes 614408 | tf_op jit(solution)/shard_map/ppermute | solution.py:169
  18.8 7.0 %collective-permute-start.10 = (bf16[32,3200]{1,0:T(8,128)(2,1)S(1)}, bf16[32,3200]{1,0:T(8,128)(2,1)S(1)}, u32[]{:S(2)}, u32[]{:S(2)}) collective-permute-start(bf16[32,3200]{1,0:T(8,128)(2,1)S(1)} %collective-permute-done.8.refs_1_), channel_id=1, source_target_pairs={{0,2},{1,3},{4,0},{5,1},{8,4},{9,5},{12,8},{13,9},{14,12},{15,13},... | collective-permute-start | bytes 614408 | tf_op jit(solution)/shard_map/ppermute | solution.py:170
  19.4 9.7 %collective-permute-start.5 = (bf16[32,5120]{1,0:T(8,128)(2,1)S(1)}, bf16[32,5120]{1,0:T(8,128)(2,1)S(1)}, u32[]{:S(2)}, u32[]{:S(2)}) collective-permute-start(bf16[32,5120]{1,0:T(8,128)(2,1)S(1)} %constant_dynamic-update-slice_fusion), channel_id=1, source_target_pairs={{0,16},{1,17},{2,18},{3,19},{4,20},{5,21},{6,22},{7,23},{8,24},{9,... | collective-permute-start | bytes 983048 | tf_op jit(solution)/shard_map/ppermute | solution.py:180
  24.1 7.0 %collective-permute-start.9 = (bf16[32,3200]{1,0:T(8,128)(2,1)S(1)}, bf16[32,3200]{1,0:T(8,128)(2,1)S(1)}, u32[]{:S(2)}, u32[]{:S(2)}) collective-permute-start(bf16[32,3200]{1,0:T(8,128)(2,1)S(1)} %collective-permute-done.7.refs_0_), channel_id=1, source_target_pairs={{0,4},{1,5},{4,8},{5,9},{8,12},{9,13},{12,14},{13,15},{14,10},{15,... | collective-permute-start | bytes 614408 | tf_op jit(solution)/shard_map/ppermute | solution.py:241
  29.1 5.4 %collective-permute-start.12 = (bf16[32,2048]{1,0:T(8,128)(2,1)S(1)}, bf16[32,2048]{1,0:T(8,128)(2,1)S(1)}, u32[]{:S(2)}, u32[]{:S(2)}) collective-permute-start(bf16[32,2048]{1,0:T(8,128)(2,1)S(1)} %get-tuple-element.46), channel_id=1, source_target_pairs={{0,4},{1,5},{4,8},{5,9},{8,12},{9,13},{12,14},{13,15},{14,10},{15,... | collective-permute-start | bytes 393224 | tf_op jit(solution)/shard_map/ppermute | solution.py:169
  30.7 5.4 %collective-permute-start.11 = (bf16[32,2048]{1,0:T(8,128)(2,1)S(1)}, bf16[32,2048]{1,0:T(8,128)(2,1)S(1)}, u32[]{:S(2)}, u32[]{:S(2)}) collective-permute-start(bf16[32,2048]{1,0:T(8,128)(2,1)S(1)} %get-tuple-element.54), channel_id=1, source_target_pairs={{0,2},{1,3},{4,0},{5,1},{8,4},{9,5},{12,8},{13,9},{14,12},{15,13},... | collective-permute-start | bytes 393224 | tf_op jit(solution)/shard_map/ppermute | solution.py:170
  34.5 6.8 %collective-permute-start.14 = (bf16[32,2048]{1,0:T(8,128)(2,1)S(1)}, bf16[32,2048]{1,0:T(8,128)(2,1)S(1)}, u32[]{:S(2)}, u32[]{:S(2)}) collective-permute-start(bf16[32,2048]{1,0:T(8,128)(2,1)S(1)} %fusion.2), channel_id=1, source_target_pairs={{0,4},{1,5},{4,8},{5,9},{8,12},{9,13},{12,14},{13,15},{14,10},{15,... | collective-permute-start | bytes 393224 | tf_op jit(solution)/shard_map/ppermute | solution.py:169
  36.2 7.0 %collective-permute-start.16 = (bf16[32,2048]{1,0:T(8,128)(2,1)S(1)}, bf16[32,2048]{1,0:T(8,128)(2,1)S(1)}, u32[]{:S(2)}, u32[]{:S(2)}) collective-permute-start(bf16[32,2048]{1,0:T(8,128)(2,1)S(1)} %fusion.3), channel_id=1, source_target_pairs={{0,2},{1,3},{4,0},{5,1},{8,4},{9,5},{12,8},{13,9},{14,12},{15,13},... | collective-permute-start | bytes 393224 | tf_op jit(solution)/shard_map/ppermute | solution.py:170
  36.7 8.8 %collective-permute-start.13 = (bf16[32,2048]{1,0:T(8,128)(2,1)S(1)}, bf16[32,2048]{1,0:T(8,128)(2,1)S(1)}, u32[]{:S(2)}, u32[]{:S(2)}) collective-permute-start(bf16[32,2048]{1,0:T(8,128)(2,1)S(1)} %convert_element_type.30), channel_id=1, source_target_pairs={{0,30},{1,31},{4,26},{5,27},{8,22},{9,23},{12,18},{13,19},{14,16},... | collective-permute-start | bytes 393224 | tf_op jit(solution)/shard_map/ppermute | solution.py:180
  41.4 5.9 %collective-permute-start.15 = (bf16[32,2048]{1,0:T(8,128)(2,1)S(1)}, bf16[32,2048]{1,0:T(8,128)(2,1)S(1)}, u32[]{:S(2)}, u32[]{:S(2)}) collective-permute-start(bf16[32,2048]{1,0:T(8,128)(2,1)S(1)} %fusion.1), channel_id=1, source_target_pairs={{0,20},{1,21},{4,24},{5,25},{8,28},{9,29},{12,30},{13,31},{14,26},... | collective-permute-start | bytes 393224 | tf_op jit(solution)/shard_map/ppermute | solution.py:180
  43.3 6.1 %collective-permute-start.17 = (bf16[32,2048]{1,0:T(8,128)(2,1)S(1)}, bf16[32,2048]{1,0:T(8,128)(2,1)S(1)}, u32[]{:S(2)}, u32[]{:S(2)}) collective-permute-start(bf16[32,2048]{1,0:T(8,128)(2,1)S(1)} %fusion), channel_id=1, source_target_pairs={{0,18},{1,19},{4,16},{5,17},{8,20},{9,21},{12,24},{13,25},{14,28},... | collective-permute-start | bytes 393224 | tf_op jit(solution)/shard_map/ppermute | solution.py:180

commit v3 on v2

--- a/solution.py
+++ b/solution.py
@@ -12,7 +12,7 @@
 BF16 = jnp.bfloat16
 VMEM_LIMIT = 16 * 1024 * 1024
 PACK_LIMIT = 60 * 1024 * 1024
-HOLD_LIMIT = 50 * 1024 * 1024
+HOLD_LIMIT = 47 * 1024 * 1024
 
 
 def call(kernel, name, shapes, *operands, scalars=0, flops=0, limit=VMEM_LIMIT, scratch=(), anywhere=()):
@@ -75,26 +75,35 @@
     return 1.0 / (1.0 + jnp.exp(-v))
 
 
-def hold_kernel(*refs):
+def hold_kernel(count, *refs):
     *refs, sems = refs
-    count = len(refs) // 2
     copies = [
         pltpu.make_async_copy(refs[i], refs[count + i], sems.at[i]) for i in range(count)
     ]
     for copy in copies:
         copy.start()
-    for copy in copies:
+    for i, copy in enumerate(copies):
         copy.wait()
+        if 2 * count + i < len(refs):
+            refs[2 * count + i][...] = refs[count + i][...].T
+
+
+def first_kernel(experts, *refs):
+    *refs, gain, out, gate_twin_t, up_twin_t, down_twin_t = refs
+    turned = (gate_twin_t, up_twin_t, down_twin_t)
+    for source, target in zip(refs[-3:], turned):
+        target[...] = source[...].T
+    expert_kernel(experts, *refs, *turned, gain, out)
 
 
 def expert_kernel(experts, *refs):
-    *parts, gate, up, down, gate_twin, up_twin, down_twin, gain, out = refs
+    *parts, gate, up, down, gate_t, up_t, down_t = refs[:-8]
+    gate_twin, up_twin, down_twin, gate_twin_t, up_twin_t, down_twin_t, gain, out = refs[-8:]
     width = gate.shape[0]
     rows = jnp.concatenate([part[:, : 3 * width] for part in parts], axis=0)
     table = jnp.concatenate([part[:, 3 * width :] for part in parts], axis=0).astype(F32)
     lane = lax.broadcasted_iota(jnp.int32, table.shape, 1)
     count = rows.shape[0]
-    across = (((1,), (1,)), ((), ()))
 
     def mixing(expert, group):
         hit = (lane == expert + group * experts) | (lane == expert + (group + 1) * experts)
@@ -102,17 +111,14 @@
 
     def dot(a, b):
         return jnp.dot(a, b, preferred_element_type=F32)
-
-    def dot_t(a, b):
-        return lax.dot_general(a, b, across, preferred_element_type=F32)
 
     both_rows = jnp.concatenate([rows[:, :width], rows[:, width : 2 * width]], axis=0)
     cotangent = rows[:, 2 * width :]
     me = lax.axis_index("expert")
     front = rear = 0.0
-    for expert, gate, up, down in (
-        (me, gate, up, down),
-        (me ^ 1, gate_twin, up_twin, down_twin),
+    for expert, gate, up, down, turned in (
+        (me, gate, up, down, (gate_t, up_t, down_t)),
+        (me ^ 1, gate_twin, up_twin, down_twin, (gate_twin_t, up_twin_t, down_twin_t)),
     ):
         gate_value = dot(both_rows, gate[...])
         up_value = dot(both_rows, up[...])
@@ -121,10 +127,10 @@
         hidden = (silu[:count] * up_value[:count]).astype(BF16)
         front = front + dot(hidden, down[...]) * mixing(expert, 0)
         gate_value, up_value, g, silu = (v[count:] for v in (gate_value, up_value, g, silu))
-        hidden_grad = dot_t(cotangent, down[...]) * mixing(expert, 2)
+        hidden_grad = dot(cotangent, turned[2][...]) * mixing(expert, 2)
         gate_grad = (hidden_grad * up_value * g * (1.0 + gate_value * (1.0 - g))).astype(BF16)
         up_grad = (hidden_grad * silu).astype(BF16)
-        rear = rear + dot_t(gate_grad, gate[...]) + dot_t(up_grad, up[...])
+        rear = rear + dot(gate_grad, turned[0][...]) + dot(up_grad, turned[1][...])
     out[:, :width] = front
     out[:, width:] = rear * gain[...]
 
@@ -203,36 +209,44 @@
 
     weights = [gate_weight[0, 0], up_weight[0, 0], down_weight[0, 0]]
     kept = [*weights, front_rows[0], rear_rows[0], rear_cotangent[0]]
-    *held, rows, rear, cotangent = call(
-        hold_kernel,
+    held = call(
+        functools.partial(hold_kernel, len(kept)),
         "hold",
-        [(value.shape, value.dtype) for value in kept],
+        [(value.shape, value.dtype) for value in kept]
+        + [(weight.shape[::-1], weight.dtype) for weight in weights],
         *[after(value, message) for value in kept],
         limit=HOLD_LIMIT,
         flops=20000000000,
         scratch=[pltpu.SemaphoreType.DMA((len(kept),))],
         anywhere=range(len(kept)),
     )
+    rows, rear, cotangent = held[3:6]
+    held = [*held[:3], *held[6:]]
     moved = [lax.ppermute(after(weight, message), "expert", twin_pairs) for weight in weights]
     held = [*held, *moved]
 
     def expert_of(*parts):
         rows = sum(part.shape[0] for part in parts)
-        return call(
-            functools.partial(expert_kernel, experts),
+        first = len(held) < 4 * len(weights)
+        kernel = first_kernel if first else expert_kernel
+        turned = [(weight.shape[::-1], weight.dtype) for weight in weights]
+        result, *new = call(
+            functools.partial(kernel, experts),
             "expert",
-            [((rows, 2 * width), F32)],
+            [((rows, 2 * width), F32)] + (turned if first else []),
             *parts,
             *held,
             norm_gain,
             flops=2 * 2 * rows * 8 * weights[0].size,
-        )[0]
+        )
+        held.extend(new)
+        return result
 
     below, above = both(message, message)
     here = [(i, i) for i in range(experts)]
     results = []
     for step in range(1, reach):
-        below = after(below, *(results[-1:] or held[: len(weights)]))
+        below = after(below, *(results[-1:] or held[: 2 * len(weights)]))
         above = after(above, below)
         mine = (below, above)
         if step < reach - 1:

time: 50.4 us -> 49 us (0.972)
  Pallas kernels: 18.1 us -> 15.7 us
  waiting for transfers between devices: 8.73 us -> 9.46 us
    pallas_call x7, Pallas kernels: 18.1 us -> 15.7 us  [call(): pl.pallas_call(kernel, out_shape=shapes, in_specs=places, out_specs=[vmem...]
    ppermute x1, waiting for transfers between devices: 0.01 us -> 0.88 us  [shards(): below = lax.ppermute(below, 'expert', up_pairs)]
    ppermute x5, waiting for transfers between devices: 3.32 us -> 4.01 us  [both(): lax.ppermute(upward, 'expert', up_pairs)]
  transfers between devices with their start and end apart: 18 -> 18, of which waited for: 6 -> 7; matrix products, arithmetic and copies ran while one was open for 1% -> 1% of each run, Pallas kernels for 30% -> 26%
where the time goes in v3:
time: 49 us; the launch traced here: 48.8 us
  starting transfers between devices  22.5 us (46%)
  Pallas kernels  15.7 us (32%)
  waiting for transfers between devices  9.46 us (19%)
  between operations  0.82 us (2%)
    pallas_call x7, Pallas kernels, call(): pl.pallas_call(kernel, out_shape=shapes, in_specs=places, out_specs=[vmem...  15.7 us
    ppermute x5, starting transfers between devices, both(): lax.ppermute(upward, 'expert', up_pairs)  9.61 us
    ppermute x4, starting transfers between devices, shifted(): return lax.ppermute(part, ('section', 'expert'), moves)  9.02 us
    ppermute x4, waiting for transfers between devices, shifted(): return lax.ppermute(part, ('section', 'expert'), moves)  4.55 us
    ppermute x5, waiting for transfers between devices, both(): lax.ppermute(upward, 'expert', up_pairs)  4.01 us
    ppermute x5, starting transfers between devices, both(): lax.ppermute(downward, 'expert', down_pairs)  1.73 us
    ppermute x1, starting transfers between devices, shards(): below = lax.ppermute(below, 'expert', up_pairs)  1.62 us
  transfers between devices with their start and end apart: 18, of which 7 were waited for; matrix products, arithmetic and copies ran while one was open for 1% of the time, Pallas kernels for 26%

profile of v3, /device:TPU:0, one launch (start us, length us, event | category | flops | bytes accessed | tf_op | source)
XLA Modules:
  0.0 48.8 jit_solution(10538609527018995622)
XLA Ops:
  0.7 2.1 %pack.1.refs_2_ = bf16[32,3200]{1,0:T(8,128)(2,1)} custom-call(bf16[32,1024]{1,0:T(8,128)(2,1)} %bitcast.20, s32[8,32]{1,0:T(8,128)} %bitcast.26, f32[8,32]{1,0:T(8,128)} %bitcast.27, bf16[32,1024]{1,0:T(8,128)(2,1)} %bitcast.22, s32[8,32]{1,0:T(8,128)} %bitcast.28, f32[8,32]{1,0:T(8,128)} %bitcast.29, bf16[32,1024]{1,0:T(8,128)(2,1)} %bitcast.24, ...), custom_call_target="tpu_custom_call" | custom-call | bytes 409600 | tf_op jit(solution)/shard_map/pack/pallas_call | solution.py:26
  2.8 3.0 %collective-permute-start = (bf16[32,3200]{1,0:T(8,128)(2,1)}, bf16[32,3200]{1,0:T(8,128)(2,1)S(1)}, u32[]{:S(2)}, u32[]{:S(2)}) collective-permute-start(bf16[32,3200]{1,0:T(8,128)(2,1)} %pack.1.refs_2_), channel_id=1, source_target_pairs={{0,4},{1,5},{4,8},{5,9},{8,12},{9,13},{12,14},{13,15},{14,10},{15,... | collective-permute-start | bytes 614408 | tf_op jit(solution)/shard_map/ppermute | solution.py:175
  6.3 2.3 %hold.1 = (bf16[1024,512]{1,0:T(8,128)(2,1)S(1)}, bf16[1024,512]{1,0:T(8,128)(2,1)S(1)}, bf16[512,1024]{1,0:T(8,128)(2,1)S(1)}, bf16[32,1024]{1,0:T(8,128)(2,1)S...) custom-call(bf16[1024,512]{1,0:T(8,128)(2,1)} %bitcast.31, ...), custom_call_target="tpu_custom_call" | custom-call | flops 20000000000 | bytes 9830400 | tf_op jit(solution)/shard_map/hold/pallas_call | solution.py:26
  8.7 2.3 %collective-permute-done.refs_0_ = bf16[32,3200]{1,0:T(8,128)(2,1)S(1)} collective-permute-done((bf16[32,3200]{1,0:T(8,128)(2,1)}, bf16[32,3200]{1,0:T(8,128)(2,1)S(1)}, u32[]{:S(2)}, u32[]{:S(2)}) %collective-permute-start) | collective-permute-done | bytes 204832 | tf_op jit(solution)/shard_map/ppermute | solution.py:175
  11.0 1.8 %collective-permute-start.6 = (bf16[32,3200]{1,0:T(8,128)(2,1)S(1)}, bf16[32,3200]{1,0:T(8,128)(2,1)S(1)}, u32[]{:S(2)}, u32[]{:S(2)}) collective-permute-start(bf16[32,3200]{1,0:T(8,128)(2,1)S(1)} %collective-permute-done.refs_0_), channel_id=1, source_target_pairs={{0,4},{1,5},{4,8},{5,9},{8,12},{9,13},{12,14},{13,15},{14,10},{15,... | collective-permute-start | bytes 614408 | tf_op jit(solution)/shard_map/ppermute | solution.py:175
  13.0 2.8 %expert.4 = (f32[96,2048]{1,0:T(8,128)S(1)}, bf16[512,1024]{1,0:T(8,128)(2,1)S(1)}, bf16[512,1024]{1,0:T(8,128)(2,1)S(1)}, bf16[1024,512]{1,0:T(8,128)(2,1)S(1)}) custom-call(bf16[32,3200]{1,0:T(8,128)(2,1)S(1)} %collective-permute-done.refs_0_, bf16[32,3200]{1,0:T(8,128)(2,1)S(1)} %collective-permute-done.1.refs_1_, bf16[32,3200]{1,0:T(8,128)(2,1)S(1)} %copy-done, ...), custom_call_target="tpu_custom_call" | custom-call | flops 1610612736 | bytes 13987840 | tf_op jit(solution)/shard_map/expert/pallas_call | solution.py:26
  15.9 1.4 %collective-permute-done.6.refs_0_ = bf16[32,3200]{1,0:T(8,128)(2,1)S(1)} collective-permute-done((bf16[32,3200]{1,0:T(8,128)(2,1)S(1)}, bf16[32,3200]{1,0:T(8,128)(2,1)S(1)}, u32[]{:S(2)}, u32[]{:S(2)}) %collective-permute-start.6) | collective-permute-done | bytes 204832 | tf_op jit(solution)/shard_map/ppermute | solution.py:175
  17.2 1.5 %collective-permute-start.7 = (bf16[32,3200]{1,0:T(8,128)(2,1)S(1)}, bf16[32,3200]{1,0:T(8,128)(2,1)S(1)}, u32[]{:S(2)}, u32[]{:S(2)}) collective-permute-start(bf16[32,3200]{1,0:T(8,128)(2,1)S(1)} %collective-permute-done.6.refs_0_), channel_id=1, source_target_pairs={{0,4},{1,5},{4,8},{5,9},{8,12},{9,13},{12,14},{13,15},{14,10},{15,... | collective-permute-start | bytes 614408 | tf_op jit(solution)/shard_map/ppermute | solution.py:175
  18.8 0.6 %collective-permute-start.10 = (bf16[32,3200]{1,0:T(8,128)(2,1)S(1)}, bf16[32,3200]{1,0:T(8,128)(2,1)S(1)}, u32[]{:S(2)}, u32[]{:S(2)}) collective-permute-start(bf16[32,3200]{1,0:T(8,128)(2,1)S(1)} %collective-permute-done.8.refs_1_), channel_id=1, source_target_pairs={{0,2},{1,3},{4,0},{5,1},{8,4},{9,5},{12,8},{13,9},{14,12},{15,13},... | collective-permute-start | bytes 614408 | tf_op jit(solution)/shard_map/ppermute | solution.py:176
  19.4 1.5 %collective-permute-start.5 = (bf16[32,5120]{1,0:T(8,128)(2,1)S(1)}, bf16[32,5120]{1,0:T(8,128)(2,1)S(1)}, u32[]{:S(2)}, u32[]{:S(2)}) collective-permute-start(bf16[32,5120]{1,0:T(8,128)(2,1)S(1)} %constant_dynamic-update-slice_fusion), channel_id=1, source_target_pairs={{0,16},{1,17},{2,18},{3,19},{4,20},{5,21},{6,22},{7,23},{8,24},{9,... | collective-permute-start | bytes 983048 | tf_op jit(solution)/shard_map/ppermute | solution.py:186
  20.9 2.6 %expert.5 = f32[64,2048]{1,0:T(8,128)S(1)} custom-call(bf16[32,3200]{1,0:T(8,128)(2,1)S(1)} %collective-permute-done.6.refs_0_, bf16[32,3200]{1,0:T(8,128)(2,1)S(1)} %collective-permute-done.8.refs_1_, bf16[1024,512]{1,0:T(8,128)(2,1)S(1)} %get-tuple-element.41.refs_3_.refs_2_.refs_1_, bf16[1024,512]{1,0:T(8,128)(2,1)S(1)} %get-tuple-element.42.refs_4_.refs_3_.refs_2_, ...), custom_call_target="tpu_custom_call" | custom-call | flops 1073741824 | bytes 13520896 | tf_op jit(solution)/shard_map/expert/pallas_call | solution.py:26
  23.5 1.6 %collective-permute-start.9 = (bf16[32,3200]{1,0:T(8,128)(2,1)S(1)}, bf16[32,3200]{1,0:T(8,128)(2,1)S(1)}, u32[]{:S(2)}, u32[]{:S(2)}) collective-permute-start(bf16[32,3200]{1,0:T(8,128)(2,1)S(1)} %collective-permute-done.7.refs_0_), channel_id=1, source_target_pairs={{0,4},{1,5},{4,8},{5,9},{8,12},{9,13},{12,14},{13,15},{14,10},{15,... | collective-permute-start | bytes 614408 | tf_op jit(solution)/shard_map/ppermute | solution.py:255
  25.1 2.6 %expert.6 = f32[64,2048]{1,0:T(8,128)S(1)} custom-call(bf16[32,3200]{1,0:T(8,128)(2,1)S(1)} %collective-permute-done.7.refs_0_, bf16[32,3200]{1,0:T(8,128)(2,1)S(1)} %collective-permute-done.10.refs_1_, bf16[1024,512]{1,0:T(8,128)(2,1)S(1)} %get-tuple-element.41.refs_3_.refs_2_.refs_1_, bf16[1024,512]{1,0:T(8,128)(2,1)S(1)} %get-tuple-element.42.refs_4_.refs_3_.refs_2_, ...), custom_call_target="tpu_custom_call" | custom-call | flops 1073741824 | bytes 13520896 | tf_op jit(solution)/shard_map/expert/pallas_call | solution.py:26
  27.7 1.6 %collective-permute-start.12 = (bf16[32,2048]{1,0:T(8,128)(2,1)S(1)}, bf16[32,2048]{1,0:T(8,128)(2,1)S(1)}, u32[]{:S(2)}, u32[]{:S(2)}) collective-permute-start(bf16[32,2048]{1,0:T(8,128)(2,1)S(1)} %get-tuple-element.60), channel_id=1, source_target_pairs={{0,4},{1,5},{4,8},{5,9},{8,12},{9,13},{12,14},{13,15},{14,10},{15,... | collective-permute-start | bytes 393224 | tf_op jit(solution)/shard_map/ppermute | solution.py:175
  29.8 0.9 %collective-permute-done.9.refs_0_ = bf16[32,3200]{1,0:T(8,128)(2,1)S(1)} collective-permute-done((bf16[32,3200]{1,0:T(8,128)(2,1)S(1)}, bf16[32,3200]{1,0:T(8,128)(2,1)S(1)}, u32[]{:S(2)}, u32[]{:S(2)}) %collective-permute-start.9) | collective-permute-done | bytes 204832 | tf_op jit(solution)/shard_map/ppermute | solution.py:255
  30.7 2.6 %expert.7 = f32[32,2048]{1,0:T(8,128)S(1)} custom-call(bf16[32,3200]{1,0:T(8,128)(2,1)S(1)} %collective-permute-done.9.refs_0_, bf16[1024,512]{1,0:T(8,128)(2,1)S(1)} %get-tuple-element.41.refs_3_.refs_2_.refs_1_, bf16[1024,512]{1,0:T(8,128)(2,1)S(1)} %get-tuple-element.42.refs_4_.refs_3_.refs_2_, ...), custom_call_target="tpu_custom_call" | custom-call | flops 536870912 | bytes 13053952 | tf_op jit(solution)/shard_map/expert/pallas_call | solution.py:26
  33.3 1.6 %collective-permute-start.14 = (bf16[32,2048]{1,0:T(8,128)(2,1)S(1)}, bf16[32,2048]{1,0:T(8,128)(2,1)S(1)}, u32[]{:S(2)}, u32[]{:S(2)}) collective-permute-start(bf16[32,2048]{1,0:T(8,128)(2,1)S(1)} %fusion), channel_id=1, source_target_pairs={{0,4},{1,5},{4,8},{5,9},{8,12},{9,13},{12,14},{13,15},{14,10},{15,... | collective-permute-start | bytes 393224 | tf_op jit(solution)/shard_map/ppermute | solution.py:175
  35.5 4.4 %collective-permute-start.13 = (bf16[32,2048]{1,0:T(8,128)(2,1)S(1)}, bf16[32,2048]{1,0:T(8,128)(2,1)S(1)}, u32[]{:S(2)}, u32[]{:S(2)}) collective-permute-start(bf16[32,2048]{1,0:T(8,128)(2,1)S(1)} %convert_element_type.30), channel_id=1, source_target_pairs={{0,30},{1,31},{4,26},{5,27},{8,22},{9,23},{12,18},{13,19},{14,16},... | collective-permute-start | bytes 393224 | tf_op jit(solution)/shard_map/ppermute | solution.py:186
  40.3 1.7 %collective-permute-start.15 = (bf16[32,2048]{1,0:T(8,128)(2,1)S(1)}, bf16[32,2048]{1,0:T(8,128)(2,1)S(1)}, u32[]{:S(2)}, u32[]{:S(2)}) collective-permute-start(bf16[32,2048]{1,0:T(8,128)(2,1)S(1)} %add_convert_fusion.1), channel_id=1, source_target_pairs={{0,20},{1,21},{4,24},{5,25},{8,28},{9,29},{12,30},{13,31},{14,26},... | collective-permute-start | bytes 393224 | tf_op jit(solution)/shard_map/ppermute | solution.py:186
  42.1 1.4 %collective-permute-start.17 = (bf16[32,2048]{1,0:T(8,128)(2,1)S(1)}, bf16[32,2048]{1,0:T(8,128)(2,1)S(1)}, u32[]{:S(2)}, u32[]{:S(2)}) collective-permute-start(bf16[32,2048]{1,0:T(8,128)(2,1)S(1)} %add_convert_fusion), channel_id=1, source_target_pairs={{0,18},{1,19},{4,16},{5,17},{8,20},{9,21},{12,24},{13,25},{14,28},... | collective-permute-start | bytes 393224 | tf_op jit(solution)/shard_map/ppermute | solution.py:186
  43.4 0.8 %collective-permute-done.13.far = bf16[32,2048]{1,0:T(8,128)(2,1)S(1)} collective-permute-done((bf16[32,2048]{1,0:T(8,128)(2,1)S(1)}, bf16[32,2048]{1,0:T(8,128)(2,1)S(1)}, u32[]{:S(2)}, u32[]{:S(2)}) %collective-permute-start.13) | collective-permute-done | bytes 131104 | tf_op jit(solution)/shard_map/ppermute | solution.py:186
  44.2 2.1 %collective-permute-done.15.below = bf16[32,2048]{1,0:T(8,128)(2,1)S(1)} collective-permute-done((bf16[32,2048]{1,0:T(8,128)(2,1)S(1)}, bf16[32,2048]{1,0:T(8,128)(2,1)S(1)}, u32[]{:S(2)}, u32[]{:S(2)}) %collective-permute-start.15) | collective-permute-done | bytes 131104 | tf_op jit(solution)/shard_map/ppermute | solution.py:186
  46.3 1.7 %collective-permute-done.17.above = bf16[32,2048]{1,0:T(8,128)(2,1)S(1)} collective-permute-done((bf16[32,2048]{1,0:T(8,128)(2,1)S(1)}, bf16[32,2048]{1,0:T(8,128)(2,1)S(1)}, u32[]{:S(2)}, u32[]{:S(2)}) %collective-permute-start.17) | collective-permute-done | bytes 131104 | tf_op jit(solution)/shard_map/ppermute | solution.py:186
  48.0 0.8 %finish.1 = (bf16[32,1024]{1,0:T(8,128)(2,1)}, bf16[32,1024]{1,0:T(8,128)(2,1)}) custom-call(bf16[32,5120]{1,0:T(8,128)(2,1)S(1)} %collective-permute-done.5.home, bf16[32,2048]{1,0:T(8,128)(2,1)S(1)} %collective-permute-done.13.far, bf16[32,2048]{1,0:T(8,128)(2,1)S(1)} %collective-permute-done.15.below, bf16[32,2048]{1,0:T(8,128)(2,1)S(1)} %collective-permute-done.17.above), custom_call_target="tpu_custom_call" | custom-call | bytes 851968 | tf_op jit(solution)/shard_map/finish/pallas_call | solution.py:26
  (42 shorter events, 2.3 us)
Async XLA Ops:
  0.6 5.7 %copy-start.2 = (bf16[1,32,1024]{2,1,0:T(8,128)(2,1)S(1)}, bf16[1,32,1024]{2,1,0:T(8,128)(2,1)}, u32[]{:S(2)}) copy-start(bf16[1,32,1024]{2,1,0:T(8,128)(2,1)} %param.11) | copy-start | bytes 196612
  0.6 5.7 %copy-start.3 = (bf16[1,32,1024]{2,1,0:T(8,128)(2,1)S(1)}, bf16[1,32,1024]{2,1,0:T(8,128)(2,1)}, u32[]{:S(2)}) copy-start(bf16[1,32,1024]{2,1,0:T(8,128)(2,1)} %param.14) | copy-start | bytes 196612
  0.7 5.7 %copy-start.4 = (bf16[1,32,1024]{2,1,0:T(8,128)(2,1)S(1)}, bf16[1,32,1024]{2,1,0:T(8,128)(2,1)}, u32[]{:S(2)}) copy-start(bf16[1,32,1024]{2,1,0:T(8,128)(2,1)} %param.17) | copy-start | bytes 196612
  2.8 8.2 %collective-permute-start = (bf16[32,3200]{1,0:T(8,128)(2,1)}, bf16[32,3200]{1,0:T(8,128)(2,1)S(1)}, u32[]{:S(2)}, u32[]{:S(2)}) collective-permute-start(bf16[32,3200]{1,0:T(8,128)(2,1)} %pack.1.refs_2_), channel_id=1, source_target_pairs={{0,4},{1,5},{4,8},{5,9},{8,12},{9,13},{12,14},{13,15},{14,10},{15,... | collective-permute-start | bytes 614408 | tf_op jit(solution)/shard_map/ppermute | solution.py:175
  5.8 7.0 %collective-permute-start.1 = (bf16[32,3200]{1,0:T(8,128)(2,1)}, bf16[32,3200]{1,0:T(8,128)(2,1)S(1)}, u32[]{:S(2)}, u32[]{:S(2)}) collective-permute-start(bf16[32,3200]{1,0:T(8,128)(2,1)} %pack.1.refs_2_), channel_id=1, source_target_pairs={{0,2},{1,3},{4,0},{5,1},{8,4},{9,5},{12,8},{13,9},{14,12},{15,13},... | collective-permute-start | bytes 614408 | tf_op jit(solution)/shard_map/ppermute | solution.py:176
  5.8 7.2 %collective-permute-start.2 = (bf16[1024,512]{1,0:T(8,128)(2,1)}, bf16[1024,512]{1,0:T(8,128)(2,1)S(1)}, u32[]{:S(2)}, u32[]{:S(2)}) collective-permute-start(bf16[1024,512]{1,0:T(8,128)(2,1)} %bitcast.30), channel_id=1, source_target_pairs={{0,1},{1,0},{2,3},{3,2},{4,5},{5,4},{6,7},{7,6},{8,9},{9,8},{10,11... | collective-permute-start | bytes 3145736 | tf_op jit(solution)/shard_map/ppermute | solution.py:225
  5.8 7.2 %collective-permute-start.3 = (bf16[1024,512]{1,0:T(8,128)(2,1)}, bf16[1024,512]{1,0:T(8,128)(2,1)S(1)}, u32[]{:S(2)}, u32[]{:S(2)}) collective-permute-start(bf16[1024,512]{1,0:T(8,128)(2,1)} %bitcast.32), channel_id=1, source_target_pairs={{0,1},{1,0},{2,3},{3,2},{4,5},{5,4},{6,7},{7,6},{8,9},{9,8},{10,11... | collective-permute-start | bytes 3145736 | tf_op jit(solution)/shard_map/ppermute | solution.py:225
  6.3 6.7 %copy-start = (bf16[32,3200]{1,0:T(8,128)(2,1)S(1)}, bf16[32,3200]{1,0:T(8,128)(2,1)}, u32[]{:S(2)}) copy-start(bf16[32,3200]{1,0:T(8,128)(2,1)} %pack.1.refs_2_) | copy-start | bytes 614404
  6.3 6.7 %collective-permute-start.4 = (bf16[512,1024]{1,0:T(8,128)(2,1)}, bf16[512,1024]{1,0:T(8,128)(2,1)S(1)}, u32[]{:S(2)}, u32[]{:S(2)}) collective-permute-start(bf16[512,1024]{1,0:T(8,128)(2,1)} %bitcast.34), channel_id=1, source_target_pairs={{0,1},{1,0},{2,3},{3,2},{4,5},{5,4},{6,7},{7,6},{8,9},{9,8},{10,11... | collective-permute-start | bytes 3145736 | tf_op jit(solution)/shard_map/ppermute | solution.py:225
  11.0 2.1 %copy-start.1 = (f32[1,1024]{1,0:T(1,128)S(1)}, f32[1,1024]{1,0:T(1,128)}, u32[]{:S(2)}) copy-start(f32[1,1024]{1,0:T(1,128)} %refs_13_.1) | copy-start | bytes 12292
  11.0 6.3 %collective-permute-start.6 = (bf16[32,3200]{1,0:T(8,128)(2,1)S(1)}, bf16[32,3200]{1,0:T(8,128)(2,1)S(1)}, u32[]{:S(2)}, u32[]{:S(2)}) collective-permute-start(bf16[32,3200]{1,0:T(8,128)(2,1)S(1)} %collective-permute-done.refs_0_), channel_id=1, source_target_pairs={{0,4},{1,5},{4,8},{5,9},{8,12},{9,13},{12,14},{13,15},{14,10},{15,... | collective-permute-start | bytes 614408 | tf_op jit(solution)/shard_map/ppermute | solution.py:175
  12.8 6.0 %collective-permute-start.8 = (bf16[32,3200]{1,0:T(8,128)(2,1)S(1)}, bf16[32,3200]{1,0:T(8,128)(2,1)S(1)}, u32[]{:S(2)}, u32[]{:S(2)}) collective-permute-start(bf16[32,3200]{1,0:T(8,128)(2,1)S(1)} %collective-permute-done.1.refs_1_), channel_id=1, source_target_pairs={{0,2},{1,3},{4,0},{5,1},{8,4},{9,5},{12,8},{13,9},{14,12},{15,13},... | collective-permute-start | bytes 614408 | tf_op jit(solution)/shard_map/ppermute | solution.py:176
  17.2 6.2 %collective-permute-start.7 = (bf16[32,3200]{1,0:T(8,128)(2,1)S(1)}, bf16[32,3200]{1,0:T(8,128)(2,1)S(1)}, u32[]{:S(2)}, u32[]{:S(2)}) collective-permute-start(bf16[32,3200]{1,0:T(8,128)(2,1)S(1)} %collective-permute-done.6.refs_0_), channel_id=1, source_target_pairs={{0,4},{1,5},{4,8},{5,9},{8,12},{9,13},{12,14},{13,15},{14,10},{15,... | collective-permute-start | bytes 614408 | tf_op jit(solution)/shard_map/ppermute | solution.py:175
  18.8 6.3 %collective-permute-start.10 = (bf16[32,3200]{1,0:T(8,128)(2,1)S(1)}, bf16[32,3200]{1,0:T(8,128)(2,1)S(1)}, u32[]{:S(2)}, u32[]{:S(2)}) collective-permute-start(bf16[32,3200]{1,0:T(8,128)(2,1)S(1)} %collective-permute-done.8.refs_1_), channel_id=1, source_target_pairs={{0,2},{1,3},{4,0},{5,1},{8,4},{9,5},{12,8},{13,9},{14,12},{15,13},... | collective-permute-start | bytes 614408 | tf_op jit(solution)/shard_map/ppermute | solution.py:176
  19.4 8.3 %collective-permute-start.5 = (bf16[32,5120]{1,0:T(8,128)(2,1)S(1)}, bf16[32,5120]{1,0:T(8,128)(2,1)S(1)}, u32[]{:S(2)}, u32[]{:S(2)}) collective-permute-start(bf16[32,5120]{1,0:T(8,128)(2,1)S(1)} %constant_dynamic-update-slice_fusion), channel_id=1, source_target_pairs={{0,16},{1,17},{2,18},{3,19},{4,20},{5,21},{6,22},{7,23},{8,24},{9,... | collective-permute-start | bytes 983048 | tf_op jit(solution)/shard_map/ppermute | solution.py:186
  23.5 7.2 %collective-permute-start.9 = (bf16[32,3200]{1,0:T(8,128)(2,1)S(1)}, bf16[32,3200]{1,0:T(8,128)(2,1)S(1)}, u32[]{:S(2)}, u32[]{:S(2)}) collective-permute-start(bf16[32,3200]{1,0:T(8,128)(2,1)S(1)} %collective-permute-done.7.refs_0_), channel_id=1, source_target_pairs={{0,4},{1,5},{4,8},{5,9},{8,12},{9,13},{12,14},{13,15},{14,10},{15,... | collective-permute-start | bytes 614408 | tf_op jit(solution)/shard_map/ppermute | solution.py:255
  27.7 5.6 %collective-permute-start.12 = (bf16[32,2048]{1,0:T(8,128)(2,1)S(1)}, bf16[32,2048]{1,0:T(8,128)(2,1)S(1)}, u32[]{:S(2)}, u32[]{:S(2)}) collective-permute-start(bf16[32,2048]{1,0:T(8,128)(2,1)S(1)} %get-tuple-element.60), channel_id=1, source_target_pairs={{0,4},{1,5},{4,8},{5,9},{8,12},{9,13},{12,14},{13,15},{14,10},{15,... | collective-permute-start | bytes 393224 | tf_op jit(solution)/shard_map/ppermute | solution.py:175
  29.3 5.6 %collective-permute-start.11 = (bf16[32,2048]{1,0:T(8,128)(2,1)S(1)}, bf16[32,2048]{1,0:T(8,128)(2,1)S(1)}, u32[]{:S(2)}, u32[]{:S(2)}) collective-permute-start(bf16[32,2048]{1,0:T(8,128)(2,1)S(1)} %get-tuple-element.68), channel_id=1, source_target_pairs={{0,2},{1,3},{4,0},{5,1},{8,4},{9,5},{12,8},{13,9},{14,12},{15,13},... | collective-permute-start | bytes 393224 | tf_op jit(solution)/shard_map/ppermute | solution.py:176
  33.3 7.0 %collective-permute-start.14 = (bf16[32,2048]{1,0:T(8,128)(2,1)S(1)}, bf16[32,2048]{1,0:T(8,128)(2,1)S(1)}, u32[]{:S(2)}, u32[]{:S(2)}) collective-permute-start(bf16[32,2048]{1,0:T(8,128)(2,1)S(1)} %fusion), channel_id=1, source_target_pairs={{0,4},{1,5},{4,8},{5,9},{8,12},{9,13},{12,14},{13,15},{14,10},{15,... | collective-permute-start | bytes 393224 | tf_op jit(solution)/shard_map/ppermute | solution.py:175
  35.0 7.0 %collective-permute-start.16 = (bf16[32,2048]{1,0:T(8,128)(2,1)S(1)}, bf16[32,2048]{1,0:T(8,128)(2,1)S(1)}, u32[]{:S(2)}, u32[]{:S(2)}) collective-permute-start(bf16[32,2048]{1,0:T(8,128)(2,1)S(1)} %fusion.1), channel_id=1, source_target_pairs={{0,2},{1,3},{4,0},{5,1},{8,4},{9,5},{12,8},{13,9},{14,12},{15,13},... | collective-permute-start | bytes 393224 | tf_op jit(solution)/shard_map/ppermute | solution.py:176
  35.5 8.7 %collective-permute-start.13 = (bf16[32,2048]{1,0:T(8,128)(2,1)S(1)}, bf16[32,2048]{1,0:T(8,128)(2,1)S(1)}, u32[]{:S(2)}, u32[]{:S(2)}) collective-permute-start(bf16[32,2048]{1,0:T(8,128)(2,1)S(1)} %convert_element_type.30), channel_id=1, source_target_pairs={{0,30},{1,31},{4,26},{5,27},{8,22},{9,23},{12,18},{13,19},{14,16},... | collective-permute-start | bytes 393224 | tf_op jit(solution)/shard_map/ppermute | solution.py:186
  40.3 5.9 %collective-permute-start.15 = (bf16[32,2048]{1,0:T(8,128)(2,1)S(1)}, bf16[32,2048]{1,0:T(8,128)(2,1)S(1)}, u32[]{:S(2)}, u32[]{:S(2)}) collective-permute-start(bf16[32,2048]{1,0:T(8,128)(2,1)S(1)} %add_convert_fusion.1), channel_id=1, source_target_pairs={{0,20},{1,21},{4,24},{5,25},{8,28},{9,29},{12,30},{13,31},{14,26},... | collective-permute-start | bytes 393224 | tf_op jit(solution)/shard_map/ppermute | solution.py:186
  42.1 5.9 %collective-permute-start.17 = (bf16[32,2048]{1,0:T(8,128)(2,1)S(1)}, bf16[32,2048]{1,0:T(8,128)(2,1)S(1)}, u32[]{:S(2)}, u32[]{:S(2)}) collective-permute-start(bf16[32,2048]{1,0:T(8,128)(2,1)S(1)} %add_convert_fusion), channel_id=1, source_target_pairs={{0,18},{1,19},{4,16},{5,17},{8,20},{9,21},{12,24},{13,25},{14,28},... | collective-permute-start | bytes 393224 | tf_op jit(solution)/shard_map/ppermute | solution.py:186

commit v4 on v3

--- a/solution.py
+++ b/solution.py
@@ -60,14 +60,16 @@
         inverse = lax.rsqrt(jnp.mean(wide * wide, axis=-1, keepdims=True) + epsilon)
         msg[:, j * width : (j + 1) * width] = (wide * inverse * gain[...]).astype(BF16)
     msg[:, 2 * width : 3 * width] = ct[...]
-    row = lax.broadcasted_iota(jnp.int32, (lanes, tokens), 0)
-    table = jnp.zeros((lanes, tokens), F32)
-    for group, (routes, weights) in enumerate(((frt, fw), (frt, fw), (rrt, rw), (rrt, rw))):
+    expert = lax.broadcasted_iota(jnp.int32, (experts, tokens), 0)
+    table = []
+    for routes, weights in ((frt, fw), (rrt, rw)):
+        mixing = jnp.zeros((experts, tokens), F32)
         for k in range(routes.shape[0]):
-            hit = row == routes[k : k + 1, :] + group * experts
-            weight = weights[k : k + 1, :]
-            high = weight.astype(BF16).astype(F32)
-            table = table + jnp.where(hit, high if group % 2 == 0 else weight - high, 0.0)
+            mixing += jnp.where(expert == routes[k : k + 1, :], weights[k : k + 1, :], 0.0)
+        high = mixing.astype(BF16).astype(F32)
+        table += [high, mixing - high]
+    table.append(jnp.zeros((lanes - 4 * experts, tokens), F32))
+    table = jnp.concatenate(table[: 4 if lanes == 4 * experts else 5], axis=0)
     msg[:, 3 * width :] = table.T.astype(BF16)
 
 
@@ -131,8 +133,8 @@
         gate_grad = (hidden_grad * up_value * g * (1.0 + gate_value * (1.0 - g))).astype(BF16)
         up_grad = (hidden_grad * silu).astype(BF16)
         rear = rear + dot(gate_grad, turned[0][...]) + dot(up_grad, turned[1][...])
-    out[:, :width] = front
-    out[:, width:] = rear * gain[...]
+    out[:, :width] = front.astype(out.dtype)
+    out[:, width:] = (rear * gain[...]).astype(out.dtype)
 
 
 def finish_kernel(home, far, below, above, front, rear):
@@ -225,7 +227,7 @@
     moved = [lax.ppermute(after(weight, message), "expert", twin_pairs) for weight in weights]
     held = [*held, *moved]
 
-    def expert_of(*parts):
+    def expert_of(*parts, dtype=F32):
         rows = sum(part.shape[0] for part in parts)
         first = len(held) < 4 * len(weights)
         kernel = first_kernel if first else expert_kernel
@@ -233,7 +235,7 @@
         result, *new = call(
             functools.partial(kernel, experts),
             "expert",
-            [((rows, 2 * width), F32)] + (turned if first else []),
+            [((rows, 2 * width), dtype)] + (turned if first else []),
             *parts,
             *held,
             norm_gain,
@@ -274,7 +276,7 @@
             to_below = to_below + from_above.astype(F32)
         to_below = to_below.astype(BF16)
         if step == reach - 1:
-            far = expert_of(after(below, to_above, to_below)).astype(BF16)
+            far = expert_of(after(below, to_above, to_below), dtype=BF16)
         if step == reach - 2:
             far = across(after(far, to_below), ring_pairs(experts, reach), width)
         if step > 1:

time: 49 us -> 48.7 us (level)
  transfers between devices with their start and end apart: 18 -> 18, of which waited for: 7 -> 7; matrix products, arithmetic and copies ran while one was open for 1% -> 0% of each run, Pallas kernels for 26% -> 26%
where the time goes in v4:
time: 48.7 us; the launch traced here: 48.5 us
  starting transfers between devices  22.7 us (47%)
  Pallas kernels  15.4 us (32%)
  waiting for transfers between devices  9.35 us (19%)
  between operations  0.82 us (2%)
    pallas_call x7, Pallas kernels, call(): pl.pallas_call(kernel, out_shape=shapes, in_specs=places, out_specs=[vmem...  15.4 us
    ppermute x5, starting transfers between devices, both(): lax.ppermute(upward, 'expert', up_pairs)  9.62 us
    ppermute x4, starting transfers between devices, shifted(): return lax.ppermute(part, ('section', 'expert'), moves)  9.18 us
    ppermute x4, waiting for transfers between devices, shifted(): return lax.ppermute(part, ('section', 'expert'), moves)  4.52 us
    ppermute x5, waiting for transfers between devices, both(): lax.ppermute(upward, 'expert', up_pairs)  3.94 us
    ppermute x5, starting transfers between devices, both(): lax.ppermute(downward, 'expert', down_pairs)  1.72 us
    ppermute x1, starting transfers between devices, shards(): below = lax.ppermute(below, 'expert', up_pairs)  1.63 us
  transfers between devices with their start and end apart: 18, of which 7 were waited for; matrix products, arithmetic and copies ran while one was open for 0% of the time, Pallas kernels for 26%

profile of v4, /device:TPU:0, one launch (start us, length us, event | category | flops | bytes accessed | tf_op | source)
XLA Modules:
  0.0 48.5 jit_solution(16038659379715793972)
XLA Ops:
  0.7 1.8 %pack.1.refs_2_ = bf16[32,3200]{1,0:T(8,128)(2,1)} custom-call(bf16[32,1024]{1,0:T(8,128)(2,1)} %bitcast.20, s32[8,32]{1,0:T(8,128)} %bitcast.26, f32[8,32]{1,0:T(8,128)} %bitcast.27, bf16[32,1024]{1,0:T(8,128)(2,1)} %bitcast.22, s32[8,32]{1,0:T(8,128)} %bitcast.28, f32[8,32]{1,0:T(8,128)} %bitcast.29, bf16[32,1024]{1,0:T(8,128)(2,1)} %bitcast.24, ...), custom_call_target="tpu_custom_call" | custom-call | bytes 409600 | tf_op jit(solution)/shard_map/pack/pallas_call | solution.py:26
  2.5 3.0 %collective-permute-start = (bf16[32,3200]{1,0:T(8,128)(2,1)}, bf16[32,3200]{1,0:T(8,128)(2,1)S(1)}, u32[]{:S(2)}, u32[]{:S(2)}) collective-permute-start(bf16[32,3200]{1,0:T(8,128)(2,1)} %pack.1.refs_2_), channel_id=1, source_target_pairs={{0,4},{1,5},{4,8},{5,9},{8,12},{9,13},{12,14},{13,15},{14,10},{15,... | collective-permute-start | bytes 614408 | tf_op jit(solution)/shard_map/ppermute | solution.py:177
  6.0 2.3 %hold.1 = (bf16[1024,512]{1,0:T(8,128)(2,1)S(1)}, bf16[1024,512]{1,0:T(8,128)(2,1)S(1)}, bf16[512,1024]{1,0:T(8,128)(2,1)S(1)}, bf16[32,1024]{1,0:T(8,128)(2,1)S...) custom-call(bf16[1024,512]{1,0:T(8,128)(2,1)} %bitcast.31, ...), custom_call_target="tpu_custom_call" | custom-call | flops 20000000000 | bytes 9830400 | tf_op jit(solution)/shard_map/hold/pallas_call | solution.py:26
  8.4 2.3 %collective-permute-done.refs_0_ = bf16[32,3200]{1,0:T(8,128)(2,1)S(1)} collective-permute-done((bf16[32,3200]{1,0:T(8,128)(2,1)}, bf16[32,3200]{1,0:T(8,128)(2,1)S(1)}, u32[]{:S(2)}, u32[]{:S(2)}) %collective-permute-start) | collective-permute-done | bytes 204832 | tf_op jit(solution)/shard_map/ppermute | solution.py:177
  10.7 1.8 %collective-permute-start.6 = (bf16[32,3200]{1,0:T(8,128)(2,1)S(1)}, bf16[32,3200]{1,0:T(8,128)(2,1)S(1)}, u32[]{:S(2)}, u32[]{:S(2)}) collective-permute-start(bf16[32,3200]{1,0:T(8,128)(2,1)S(1)} %collective-permute-done.refs_0_), channel_id=1, source_target_pairs={{0,4},{1,5},{4,8},{5,9},{8,12},{9,13},{12,14},{13,15},{14,10},{15,... | collective-permute-start | bytes 614408 | tf_op jit(solution)/shard_map/ppermute | solution.py:177
  12.8 2.8 %expert.4 = (f32[96,2048]{1,0:T(8,128)S(1)}, bf16[512,1024]{1,0:T(8,128)(2,1)S(1)}, bf16[512,1024]{1,0:T(8,128)(2,1)S(1)}, bf16[1024,512]{1,0:T(8,128)(2,1)S(1)}) custom-call(bf16[32,3200]{1,0:T(8,128)(2,1)S(1)} %collective-permute-done.refs_0_, bf16[32,3200]{1,0:T(8,128)(2,1)S(1)} %collective-permute-done.1.refs_1_, bf16[32,3200]{1,0:T(8,128)(2,1)S(1)} %copy-done, ...), custom_call_target="tpu_custom_call" | custom-call | flops 1610612736 | bytes 13987840 | tf_op jit(solution)/shard_map/expert/pallas_call | solution.py:26
  15.6 1.4 %collective-permute-done.6.refs_0_ = bf16[32,3200]{1,0:T(8,128)(2,1)S(1)} collective-permute-done((bf16[32,3200]{1,0:T(8,128)(2,1)S(1)}, bf16[32,3200]{1,0:T(8,128)(2,1)S(1)}, u32[]{:S(2)}, u32[]{:S(2)}) %collective-permute-start.6) | collective-permute-done | bytes 204832 | tf_op jit(solution)/shard_map/ppermute | solution.py:177
  17.0 1.5 %collective-permute-start.7 = (bf16[32,3200]{1,0:T(8,128)(2,1)S(1)}, bf16[32,3200]{1,0:T(8,128)(2,1)S(1)}, u32[]{:S(2)}, u32[]{:S(2)}) collective-permute-start(bf16[32,3200]{1,0:T(8,128)(2,1)S(1)} %collective-permute-done.6.refs_0_), channel_id=1, source_target_pairs={{0,4},{1,5},{4,8},{5,9},{8,12},{9,13},{12,14},{13,15},{14,10},{15,... | collective-permute-start | bytes 614408 | tf_op jit(solution)/shard_map/ppermute | solution.py:177
  18.5 0.6 %collective-permute-start.10 = (bf16[32,3200]{1,0:T(8,128)(2,1)S(1)}, bf16[32,3200]{1,0:T(8,128)(2,1)S(1)}, u32[]{:S(2)}, u32[]{:S(2)}) collective-permute-start(bf16[32,3200]{1,0:T(8,128)(2,1)S(1)} %collective-permute-done.8.refs_1_), channel_id=1, source_target_pairs={{0,2},{1,3},{4,0},{5,1},{8,4},{9,5},{12,8},{13,9},{14,12},{15,13},... | collective-permute-start | bytes 614408 | tf_op jit(solution)/shard_map/ppermute | solution.py:178
  19.1 1.5 %collective-permute-start.5 = (bf16[32,5120]{1,0:T(8,128)(2,1)S(1)}, bf16[32,5120]{1,0:T(8,128)(2,1)S(1)}, u32[]{:S(2)}, u32[]{:S(2)}) collective-permute-start(bf16[32,5120]{1,0:T(8,128)(2,1)S(1)} %constant_dynamic-update-slice_fusion), channel_id=1, source_target_pairs={{0,16},{1,17},{2,18},{3,19},{4,20},{5,21},{6,22},{7,23},{8,24},{9,... | collective-permute-start | bytes 983048 | tf_op jit(solution)/shard_map/ppermute | solution.py:188
  20.6 2.5 %expert.5 = f32[64,2048]{1,0:T(8,128)S(1)} custom-call(bf16[32,3200]{1,0:T(8,128)(2,1)S(1)} %collective-permute-done.6.refs_0_, bf16[32,3200]{1,0:T(8,128)(2,1)S(1)} %collective-permute-done.8.refs_1_, bf16[1024,512]{1,0:T(8,128)(2,1)S(1)} %get-tuple-element.41.refs_3_.refs_2_.refs_1_, bf16[1024,512]{1,0:T(8,128)(2,1)S(1)} %get-tuple-element.42.refs_4_.refs_3_.refs_2_, ...), custom_call_target="tpu_custom_call" | custom-call | flops 1073741824 | bytes 13520896 | tf_op jit(solution)/shard_map/expert/pallas_call | solution.py:26
  23.2 1.6 %collective-permute-start.9 = (bf16[32,3200]{1,0:T(8,128)(2,1)S(1)}, bf16[32,3200]{1,0:T(8,128)(2,1)S(1)}, u32[]{:S(2)}, u32[]{:S(2)}) collective-permute-start(bf16[32,3200]{1,0:T(8,128)(2,1)S(1)} %collective-permute-done.7.refs_0_), channel_id=1, source_target_pairs={{0,4},{1,5},{4,8},{5,9},{8,12},{9,13},{12,14},{13,15},{14,10},{15,... | collective-permute-start | bytes 614408 | tf_op jit(solution)/shard_map/ppermute | solution.py:257
  24.8 2.6 %expert.6 = f32[64,2048]{1,0:T(8,128)S(1)} custom-call(bf16[32,3200]{1,0:T(8,128)(2,1)S(1)} %collective-permute-done.7.refs_0_, bf16[32,3200]{1,0:T(8,128)(2,1)S(1)} %collective-permute-done.10.refs_1_, bf16[1024,512]{1,0:T(8,128)(2,1)S(1)} %get-tuple-element.41.refs_3_.refs_2_.refs_1_, bf16[1024,512]{1,0:T(8,128)(2,1)S(1)} %get-tuple-element.42.refs_4_.refs_3_.refs_2_, ...), custom_call_target="tpu_custom_call" | custom-call | flops 1073741824 | bytes 13520896 | tf_op jit(solution)/shard_map/expert/pallas_call | solution.py:26
  27.4 1.6 %collective-permute-start.12 = (bf16[32,2048]{1,0:T(8,128)(2,1)S(1)}, bf16[32,2048]{1,0:T(8,128)(2,1)S(1)}, u32[]{:S(2)}, u32[]{:S(2)}) collective-permute-start(bf16[32,2048]{1,0:T(8,128)(2,1)S(1)} %get-tuple-element.60), channel_id=1, source_target_pairs={{0,4},{1,5},{4,8},{5,9},{8,12},{9,13},{12,14},{13,15},{14,10},{15,... | collective-permute-start | bytes 393224 | tf_op jit(solution)/shard_map/ppermute | solution.py:177
  29.5 0.9 %collective-permute-done.9.refs_0_ = bf16[32,3200]{1,0:T(8,128)(2,1)S(1)} collective-permute-done((bf16[32,3200]{1,0:T(8,128)(2,1)S(1)}, bf16[32,3200]{1,0:T(8,128)(2,1)S(1)}, u32[]{:S(2)}, u32[]{:S(2)}) %collective-permute-start.9) | collective-permute-done | bytes 204832 | tf_op jit(solution)/shard_map/ppermute | solution.py:257
  30.4 2.6 %expert.7 = bf16[32,2048]{1,0:T(8,128)(2,1)S(1)} custom-call(bf16[32,3200]{1,0:T(8,128)(2,1)S(1)} %collective-permute-done.9.refs_0_, bf16[1024,512]{1,0:T(8,128)(2,1)S(1)} %get-tuple-element.41.refs_3_.refs_2_.refs_1_, bf16[1024,512]{1,0:T(8,128)(2,1)S(1)} %get-tuple-element.42.refs_4_.refs_3_.refs_2_, ...), custom_call_target="tpu_custom_call" | custom-call | flops 536870912 | bytes 12922880 | tf_op jit(solution)/shard_map/expert/pallas_call | solution.py:26
  33.0 1.6 %collective-permute-start.14 = (bf16[32,2048]{1,0:T(8,128)(2,1)S(1)}, bf16[32,2048]{1,0:T(8,128)(2,1)S(1)}, u32[]{:S(2)}, u32[]{:S(2)}) collective-permute-start(bf16[32,2048]{1,0:T(8,128)(2,1)S(1)} %fusion), channel_id=1, source_target_pairs={{0,4},{1,5},{4,8},{5,9},{8,12},{9,13},{12,14},{13,15},{14,10},{15,... | collective-permute-start | bytes 393224 | tf_op jit(solution)/shard_map/ppermute | solution.py:177
  35.2 4.5 %collective-permute-start.13 = (bf16[32,2048]{1,0:T(8,128)(2,1)S(1)}, bf16[32,2048]{1,0:T(8,128)(2,1)S(1)}, u32[]{:S(2)}, u32[]{:S(2)}) collective-permute-start(bf16[32,2048]{1,0:T(8,128)(2,1)S(1)} %expert.7), channel_id=1, source_target_pairs={{0,30},{1,31},{4,26},{5,27},{8,22},{9,23},{12,18},{13,19},{14,16},... | collective-permute-start | bytes 393224 | tf_op jit(solution)/shard_map/ppermute | solution.py:188
  40.0 1.8 %collective-permute-start.15 = (bf16[32,2048]{1,0:T(8,128)(2,1)S(1)}, bf16[32,2048]{1,0:T(8,128)(2,1)S(1)}, u32[]{:S(2)}, u32[]{:S(2)}) collective-permute-start(bf16[32,2048]{1,0:T(8,128)(2,1)S(1)} %add_convert_fusion.1), channel_id=1, source_target_pairs={{0,20},{1,21},{4,24},{5,25},{8,28},{9,29},{12,30},{13,31},{14,26},... | collective-permute-start | bytes 393224 | tf_op jit(solution)/shard_map/ppermute | solution.py:188
  41.8 1.4 %collective-permute-start.17 = (bf16[32,2048]{1,0:T(8,128)(2,1)S(1)}, bf16[32,2048]{1,0:T(8,128)(2,1)S(1)}, u32[]{:S(2)}, u32[]{:S(2)}) collective-permute-start(bf16[32,2048]{1,0:T(8,128)(2,1)S(1)} %add_convert_fusion), channel_id=1, source_target_pairs={{0,18},{1,19},{4,16},{5,17},{8,20},{9,21},{12,24},{13,25},{14,28},... | collective-permute-start | bytes 393224 | tf_op jit(solution)/shard_map/ppermute | solution.py:188
  43.2 0.7 %collective-permute-done.13.far = bf16[32,2048]{1,0:T(8,128)(2,1)S(1)} collective-permute-done((bf16[32,2048]{1,0:T(8,128)(2,1)S(1)}, bf16[32,2048]{1,0:T(8,128)(2,1)S(1)}, u32[]{:S(2)}, u32[]{:S(2)}) %collective-permute-start.13) | collective-permute-done | bytes 131104 | tf_op jit(solution)/shard_map/ppermute | solution.py:188
  43.9 2.0 %collective-permute-done.15.below = bf16[32,2048]{1,0:T(8,128)(2,1)S(1)} collective-permute-done((bf16[32,2048]{1,0:T(8,128)(2,1)S(1)}, bf16[32,2048]{1,0:T(8,128)(2,1)S(1)}, u32[]{:S(2)}, u32[]{:S(2)}) %collective-permute-start.15) | collective-permute-done | bytes 131104 | tf_op jit(solution)/shard_map/ppermute | solution.py:188
  45.9 1.8 %collective-permute-done.17.above = bf16[32,2048]{1,0:T(8,128)(2,1)S(1)} collective-permute-done((bf16[32,2048]{1,0:T(8,128)(2,1)S(1)}, bf16[32,2048]{1,0:T(8,128)(2,1)S(1)}, u32[]{:S(2)}, u32[]{:S(2)}) %collective-permute-start.17) | collective-permute-done | bytes 131104 | tf_op jit(solution)/shard_map/ppermute | solution.py:188
  47.7 0.8 %finish.1 = (bf16[32,1024]{1,0:T(8,128)(2,1)}, bf16[32,1024]{1,0:T(8,128)(2,1)}) custom-call(bf16[32,5120]{1,0:T(8,128)(2,1)S(1)} %collective-permute-done.5.home, bf16[32,2048]{1,0:T(8,128)(2,1)S(1)} %collective-permute-done.13.far, bf16[32,2048]{1,0:T(8,128)(2,1)S(1)} %collective-permute-done.15.below, bf16[32,2048]{1,0:T(8,128)(2,1)S(1)} %collective-permute-done.17.above), custom_call_target="tpu_custom_call" | custom-call | bytes 851968 | tf_op jit(solution)/shard_map/finish/pallas_call | solution.py:26
  (41 shorter events, 2.2 us)
Async XLA Ops:
  0.6 5.4 %copy-start.2 = (bf16[1,32,1024]{2,1,0:T(8,128)(2,1)S(1)}, bf16[1,32,1024]{2,1,0:T(8,128)(2,1)}, u32[]{:S(2)}) copy-start(bf16[1,32,1024]{2,1,0:T(8,128)(2,1)} %param.11) | copy-start | bytes 196612
  0.6 5.4 %copy-start.3 = (bf16[1,32,1024]{2,1,0:T(8,128)(2,1)S(1)}, bf16[1,32,1024]{2,1,0:T(8,128)(2,1)}, u32[]{:S(2)}) copy-start(bf16[1,32,1024]{2,1,0:T(8,128)(2,1)} %param.14) | copy-start | bytes 196612
  0.7 5.4 %copy-start.4 = (bf16[1,32,1024]{2,1,0:T(8,128)(2,1)S(1)}, bf16[1,32,1024]{2,1,0:T(8,128)(2,1)}, u32[]{:S(2)}) copy-start(bf16[1,32,1024]{2,1,0:T(8,128)(2,1)} %param.17) | copy-start | bytes 196612
  2.5 8.2 %collective-permute-start = (bf16[32,3200]{1,0:T(8,128)(2,1)}, bf16[32,3200]{1,0:T(8,128)(2,1)S(1)}, u32[]{:S(2)}, u32[]{:S(2)}) collective-permute-start(bf16[32,3200]{1,0:T(8,128)(2,1)} %pack.1.refs_2_), channel_id=1, source_target_pairs={{0,4},{1,5},{4,8},{5,9},{8,12},{9,13},{12,14},{13,15},{14,10},{15,... | collective-permute-start | bytes 614408 | tf_op jit(solution)/shard_map/ppermute | solution.py:177
  5.5 7.0 %collective-permute-start.1 = (bf16[32,3200]{1,0:T(8,128)(2,1)}, bf16[32,3200]{1,0:T(8,128)(2,1)S(1)}, u32[]{:S(2)}, u32[]{:S(2)}) collective-permute-start(bf16[32,3200]{1,0:T(8,128)(2,1)} %pack.1.refs_2_), channel_id=1, source_target_pairs={{0,2},{1,3},{4,0},{5,1},{8,4},{9,5},{12,8},{13,9},{14,12},{15,13},... | collective-permute-start | bytes 614408 | tf_op jit(solution)/shard_map/ppermute | solution.py:178
  5.5 7.2 %collective-permute-start.2 = (bf16[1024,512]{1,0:T(8,128)(2,1)}, bf16[1024,512]{1,0:T(8,128)(2,1)S(1)}, u32[]{:S(2)}, u32[]{:S(2)}) collective-permute-start(bf16[1024,512]{1,0:T(8,128)(2,1)} %bitcast.30), channel_id=1, source_target_pairs={{0,1},{1,0},{2,3},{3,2},{4,5},{5,4},{6,7},{7,6},{8,9},{9,8},{10,11... | collective-permute-start | bytes 3145736 | tf_op jit(solution)/shard_map/ppermute | solution.py:227
  5.5 7.2 %collective-permute-start.3 = (bf16[1024,512]{1,0:T(8,128)(2,1)}, bf16[1024,512]{1,0:T(8,128)(2,1)S(1)}, u32[]{:S(2)}, u32[]{:S(2)}) collective-permute-start(bf16[1024,512]{1,0:T(8,128)(2,1)} %bitcast.32), channel_id=1, source_target_pairs={{0,1},{1,0},{2,3},{3,2},{4,5},{5,4},{6,7},{7,6},{8,9},{9,8},{10,11... | collective-permute-start | bytes 3145736 | tf_op jit(solution)/shard_map/ppermute | solution.py:227
  6.0 6.7 %copy-start = (bf16[32,3200]{1,0:T(8,128)(2,1)S(1)}, bf16[32,3200]{1,0:T(8,128)(2,1)}, u32[]{:S(2)}) copy-start(bf16[32,3200]{1,0:T(8,128)(2,1)} %pack.1.refs_2_) | copy-start | bytes 614404
  6.0 6.7 %collective-permute-start.4 = (bf16[512,1024]{1,0:T(8,128)(2,1)}, bf16[512,1024]{1,0:T(8,128)(2,1)S(1)}, u32[]{:S(2)}, u32[]{:S(2)}) collective-permute-start(bf16[512,1024]{1,0:T(8,128)(2,1)} %bitcast.34), channel_id=1, source_target_pairs={{0,1},{1,0},{2,3},{3,2},{4,5},{5,4},{6,7},{7,6},{8,9},{9,8},{10,11... | collective-permute-start | bytes 3145736 | tf_op jit(solution)/shard_map/ppermute | solution.py:227
  10.7 2.1 %copy-start.1 = (f32[1,1024]{1,0:T(1,128)S(1)}, f32[1,1024]{1,0:T(1,128)}, u32[]{:S(2)}) copy-start(f32[1,1024]{1,0:T(1,128)} %refs_13_.1) | copy-start | bytes 12292
  10.7 6.3 %collective-permute-start.6 = (bf16[32,3200]{1,0:T(8,128)(2,1)S(1)}, bf16[32,3200]{1,0:T(8,128)(2,1)S(1)}, u32[]{:S(2)}, u32[]{:S(2)}) collective-permute-start(bf16[32,3200]{1,0:T(8,128)(2,1)S(1)} %collective-permute-done.refs_0_), channel_id=1, source_target_pairs={{0,4},{1,5},{4,8},{5,9},{8,12},{9,13},{12,14},{13,15},{14,10},{15,... | collective-permute-start | bytes 614408 | tf_op jit(solution)/shard_map/ppermute | solution.py:177
  12.5 6.0 %collective-permute-start.8 = (bf16[32,3200]{1,0:T(8,128)(2,1)S(1)}, bf16[32,3200]{1,0:T(8,128)(2,1)S(1)}, u32[]{:S(2)}, u32[]{:S(2)}) collective-permute-start(bf16[32,3200]{1,0:T(8,128)(2,1)S(1)} %collective-permute-done.1.refs_1_), channel_id=1, source_target_pairs={{0,2},{1,3},{4,0},{5,1},{8,4},{9,5},{12,8},{13,9},{14,12},{15,13},... | collective-permute-start | bytes 614408 | tf_op jit(solution)/shard_map/ppermute | solution.py:178
  17.0 6.2 %collective-permute-start.7 = (bf16[32,3200]{1,0:T(8,128)(2,1)S(1)}, bf16[32,3200]{1,0:T(8,128)(2,1)S(1)}, u32[]{:S(2)}, u32[]{:S(2)}) collective-permute-start(bf16[32,3200]{1,0:T(8,128)(2,1)S(1)} %collective-permute-done.6.refs_0_), channel_id=1, source_target_pairs={{0,4},{1,5},{4,8},{5,9},{8,12},{9,13},{12,14},{13,15},{14,10},{15,... | collective-permute-start | bytes 614408 | tf_op jit(solution)/shard_map/ppermute | solution.py:177
  18.5 6.3 %collective-permute-start.10 = (bf16[32,3200]{1,0:T(8,128)(2,1)S(1)}, bf16[32,3200]{1,0:T(8,128)(2,1)S(1)}, u32[]{:S(2)}, u32[]{:S(2)}) collective-permute-start(bf16[32,3200]{1,0:T(8,128)(2,1)S(1)} %collective-permute-done.8.refs_1_), channel_id=1, source_target_pairs={{0,2},{1,3},{4,0},{5,1},{8,4},{9,5},{12,8},{13,9},{14,12},{15,13},... | collective-permute-start | bytes 614408 | tf_op jit(solution)/shard_map/ppermute | solution.py:178
  19.1 8.3 %collective-permute-start.5 = (bf16[32,5120]{1,0:T(8,128)(2,1)S(1)}, bf16[32,5120]{1,0:T(8,128)(2,1)S(1)}, u32[]{:S(2)}, u32[]{:S(2)}) collective-permute-start(bf16[32,5120]{1,0:T(8,128)(2,1)S(1)} %constant_dynamic-update-slice_fusion), channel_id=1, source_target_pairs={{0,16},{1,17},{2,18},{3,19},{4,20},{5,21},{6,22},{7,23},{8,24},{9,... | collective-permute-start | bytes 983048 | tf_op jit(solution)/shard_map/ppermute | solution.py:188
  23.2 7.2 %collective-permute-start.9 = (bf16[32,3200]{1,0:T(8,128)(2,1)S(1)}, bf16[32,3200]{1,0:T(8,128)(2,1)S(1)}, u32[]{:S(2)}, u32[]{:S(2)}) collective-permute-start(bf16[32,3200]{1,0:T(8,128)(2,1)S(1)} %collective-permute-done.7.refs_0_), channel_id=1, source_target_pairs={{0,4},{1,5},{4,8},{5,9},{8,12},{9,13},{12,14},{13,15},{14,10},{15,... | collective-permute-start | bytes 614408 | tf_op jit(solution)/shard_map/ppermute | solution.py:257
  27.4 5.6 %collective-permute-start.12 = (bf16[32,2048]{1,0:T(8,128)(2,1)S(1)}, bf16[32,2048]{1,0:T(8,128)(2,1)S(1)}, u32[]{:S(2)}, u32[]{:S(2)}) collective-permute-start(bf16[32,2048]{1,0:T(8,128)(2,1)S(1)} %get-tuple-element.60), channel_id=1, source_target_pairs={{0,4},{1,5},{4,8},{5,9},{8,12},{9,13},{12,14},{13,15},{14,10},{15,... | collective-permute-start | bytes 393224 | tf_op jit(solution)/shard_map/ppermute | solution.py:177
  29.1 5.6 %collective-permute-start.11 = (bf16[32,2048]{1,0:T(8,128)(2,1)S(1)}, bf16[32,2048]{1,0:T(8,128)(2,1)S(1)}, u32[]{:S(2)}, u32[]{:S(2)}) collective-permute-start(bf16[32,2048]{1,0:T(8,128)(2,1)S(1)} %get-tuple-element.68), channel_id=1, source_target_pairs={{0,2},{1,3},{4,0},{5,1},{8,4},{9,5},{12,8},{13,9},{14,12},{15,13},... | collective-permute-start | bytes 393224 | tf_op jit(solution)/shard_map/ppermute | solution.py:178
  33.0 6.9 %collective-permute-start.14 = (bf16[32,2048]{1,0:T(8,128)(2,1)S(1)}, bf16[32,2048]{1,0:T(8,128)(2,1)S(1)}, u32[]{:S(2)}, u32[]{:S(2)}) collective-permute-start(bf16[32,2048]{1,0:T(8,128)(2,1)S(1)} %fusion), channel_id=1, source_target_pairs={{0,4},{1,5},{4,8},{5,9},{8,12},{9,13},{12,14},{13,15},{14,10},{15,... | collective-permute-start | bytes 393224 | tf_op jit(solution)/shard_map/ppermute | solution.py:177
  34.7 7.1 %collective-permute-start.16 = (bf16[32,2048]{1,0:T(8,128)(2,1)S(1)}, bf16[32,2048]{1,0:T(8,128)(2,1)S(1)}, u32[]{:S(2)}, u32[]{:S(2)}) collective-permute-start(bf16[32,2048]{1,0:T(8,128)(2,1)S(1)} %fusion.1), channel_id=1, source_target_pairs={{0,2},{1,3},{4,0},{5,1},{8,4},{9,5},{12,8},{13,9},{14,12},{15,13},... | collective-permute-start | bytes 393224 | tf_op jit(solution)/shard_map/ppermute | solution.py:178
  35.2 8.7 %collective-permute-start.13 = (bf16[32,2048]{1,0:T(8,128)(2,1)S(1)}, bf16[32,2048]{1,0:T(8,128)(2,1)S(1)}, u32[]{:S(2)}, u32[]{:S(2)}) collective-permute-start(bf16[32,2048]{1,0:T(8,128)(2,1)S(1)} %expert.7), channel_id=1, source_target_pairs={{0,30},{1,31},{4,26},{5,27},{8,22},{9,23},{12,18},{13,19},{14,16},... | collective-permute-start | bytes 393224 | tf_op jit(solution)/shard_map/ppermute | solution.py:188
  40.0 5.9 %collective-permute-start.15 = (bf16[32,2048]{1,0:T(8,128)(2,1)S(1)}, bf16[32,2048]{1,0:T(8,128)(2,1)S(1)}, u32[]{:S(2)}, u32[]{:S(2)}) collective-permute-start(bf16[32,2048]{1,0:T(8,128)(2,1)S(1)} %add_convert_fusion.1), channel_id=1, source_target_pairs={{0,20},{1,21},{4,24},{5,25},{8,28},{9,29},{12,30},{13,31},{14,26},... | collective-permute-start | bytes 393224 | tf_op jit(solution)/shard_map/ppermute | solution.py:188
  41.8 5.9 %collective-permute-start.17 = (bf16[32,2048]{1,0:T(8,128)(2,1)S(1)}, bf16[32,2048]{1,0:T(8,128)(2,1)S(1)}, u32[]{:S(2)}, u32[]{:S(2)}) collective-permute-start(bf16[32,2048]{1,0:T(8,128)(2,1)S(1)} %add_convert_fusion), channel_id=1, source_target_pairs={{0,18},{1,19},{4,16},{5,17},{8,20},{9,21},{12,24},{13,25},{14,28},... | collective-permute-start | bytes 393224 | tf_op jit(solution)/shard_map/ppermute | solution.py:188

commit v5 on v4

--- a/solution.py
+++ b/solution.py
@@ -239,7 +239,7 @@
             *parts,
             *held,
             norm_gain,
-            flops=2 * 2 * rows * 8 * weights[0].size,
+            flops=(1 if first else 4) * rows * 8 * weights[0].size,
         )
         held.extend(new)
         return result
@@ -255,7 +255,8 @@
             below, above = both(below, above)
         else:
             below = lax.ppermute(below, "expert", up_pairs)
-        results.append(expert_of(*mine, *([message] if step == 1 else [])))
+        dtype = BF16 if step == reach - 1 else F32
+        results.append(expert_of(*mine, *([message] if step == 1 else []), dtype=dtype))
         if step == 1:
             home = results[0][2 * tokens :].astype(BF16)
             home = [home[:, :width], rows, home[:, width:], rear, cotangent]

time: 48.7 us -> 48.7 us (level)
  no operation moved by 1% of the time
where the time goes in v5:
time: 48.7 us; the launch traced here: 48.5 us
  starting transfers between devices  22.6 us (46%)
  Pallas kernels  15.4 us (32%)
  waiting for transfers between devices  9.48 us (19%)
  between operations  0.81 us (2%)
    pallas_call x7, Pallas kernels, call(): pl.pallas_call(kernel, out_shape=shapes, in_specs=places, out_specs=[vmem...  15.4 us
    ppermute x5, starting transfers between devices, both(): lax.ppermute(upward, 'expert', up_pairs)  9.62 us
    ppermute x4, starting transfers between devices, shifted(): return lax.ppermute(part, ('section', 'expert'), moves)  9.09 us
    ppermute x4, waiting for transfers between devices, shifted(): return lax.ppermute(part, ('section', 'expert'), moves)  4.58 us
    ppermute x5, waiting for transfers between devices, both(): lax.ppermute(upward, 'expert', up_pairs)  3.98 us
    ppermute x5, starting transfers between devices, both(): lax.ppermute(downward, 'expert', down_pairs)  1.72 us
    ppermute x1, starting transfers between devices, shards(): below = lax.ppermute(below, 'expert', up_pairs)  1.63 us
  transfers between devices with their start and end apart: 18, of which 7 were waited for; matrix products, arithmetic and copies ran while one was open for 0% of the time, Pallas kernels for 26%

profile of v5, /device:TPU:0, one launch (start us, length us, event | category | flops | bytes accessed | tf_op | source)
XLA Modules:
  0.0 48.5 jit_solution(14749993404969609301)
XLA Ops:
  0.7 1.8 %pack.1.refs_2_ = bf16[32,3200]{1,0:T(8,128)(2,1)} custom-call(bf16[32,1024]{1,0:T(8,128)(2,1)} %bitcast.20, s32[8,32]{1,0:T(8,128)} %bitcast.26, f32[8,32]{1,0:T(8,128)} %bitcast.27, bf16[32,1024]{1,0:T(8,128)(2,1)} %bitcast.22, s32[8,32]{1,0:T(8,128)} %bitcast.28, f32[8,32]{1,0:T(8,128)} %bitcast.29, bf16[32,1024]{1,0:T(8,128)(2,1)} %bitcast.24, ...), custom_call_target="tpu_custom_call" | custom-call | bytes 409600 | tf_op jit(solution)/shard_map/pack/pallas_call | solution.py:26
  2.5 3.0 %collective-permute-start = (bf16[32,3200]{1,0:T(8,128)(2,1)}, bf16[32,3200]{1,0:T(8,128)(2,1)S(1)}, u32[]{:S(2)}, u32[]{:S(2)}) collective-permute-start(bf16[32,3200]{1,0:T(8,128)(2,1)} %pack.1.refs_2_), channel_id=1, source_target_pairs={{0,4},{1,5},{4,8},{5,9},{8,12},{9,13},{12,14},{13,15},{14,10},{15,... | collective-permute-start | bytes 614408 | tf_op jit(solution)/shard_map/ppermute | solution.py:177
  6.0 2.3 %hold.1 = (bf16[1024,512]{1,0:T(8,128)(2,1)S(1)}, bf16[1024,512]{1,0:T(8,128)(2,1)S(1)}, bf16[512,1024]{1,0:T(8,128)(2,1)S(1)}, bf16[32,1024]{1,0:T(8,128)(2,1)S...) custom-call(bf16[1024,512]{1,0:T(8,128)(2,1)} %bitcast.31, ...), custom_call_target="tpu_custom_call" | custom-call | flops 20000000000 | bytes 9830400 | tf_op jit(solution)/shard_map/hold/pallas_call | solution.py:26
  8.4 2.3 %collective-permute-done.refs_0_ = bf16[32,3200]{1,0:T(8,128)(2,1)S(1)} collective-permute-done((bf16[32,3200]{1,0:T(8,128)(2,1)}, bf16[32,3200]{1,0:T(8,128)(2,1)S(1)}, u32[]{:S(2)}, u32[]{:S(2)}) %collective-permute-start) | collective-permute-done | bytes 204832 | tf_op jit(solution)/shard_map/ppermute | solution.py:177
  10.7 1.8 %collective-permute-start.6 = (bf16[32,3200]{1,0:T(8,128)(2,1)S(1)}, bf16[32,3200]{1,0:T(8,128)(2,1)S(1)}, u32[]{:S(2)}, u32[]{:S(2)}) collective-permute-start(bf16[32,3200]{1,0:T(8,128)(2,1)S(1)} %collective-permute-done.refs_0_), channel_id=1, source_target_pairs={{0,4},{1,5},{4,8},{5,9},{8,12},{9,13},{12,14},{13,15},{14,10},{15,... | collective-permute-start | bytes 614408 | tf_op jit(solution)/shard_map/ppermute | solution.py:177
  12.8 2.8 %expert.4 = (f32[96,2048]{1,0:T(8,128)S(1)}, bf16[512,1024]{1,0:T(8,128)(2,1)S(1)}, bf16[512,1024]{1,0:T(8,128)(2,1)S(1)}, bf16[1024,512]{1,0:T(8,128)(2,1)S(1)}) custom-call(bf16[32,3200]{1,0:T(8,128)(2,1)S(1)} %collective-permute-done.refs_0_, bf16[32,3200]{1,0:T(8,128)(2,1)S(1)} %collective-permute-done.1.refs_1_, bf16[32,3200]{1,0:T(8,128)(2,1)S(1)} %copy-done, ...), custom_call_target="tpu_custom_call" | custom-call | flops 402653184 | bytes 13987840 | tf_op jit(solution)/shard_map/expert/pallas_call | solution.py:26
  15.6 1.4 %collective-permute-done.6.refs_0_ = bf16[32,3200]{1,0:T(8,128)(2,1)S(1)} collective-permute-done((bf16[32,3200]{1,0:T(8,128)(2,1)S(1)}, bf16[32,3200]{1,0:T(8,128)(2,1)S(1)}, u32[]{:S(2)}, u32[]{:S(2)}) %collective-permute-start.6) | collective-permute-done | bytes 204832 | tf_op jit(solution)/shard_map/ppermute | solution.py:177
  17.0 1.5 %collective-permute-start.7 = (bf16[32,3200]{1,0:T(8,128)(2,1)S(1)}, bf16[32,3200]{1,0:T(8,128)(2,1)S(1)}, u32[]{:S(2)}, u32[]{:S(2)}) collective-permute-start(bf16[32,3200]{1,0:T(8,128)(2,1)S(1)} %collective-permute-done.6.refs_0_), channel_id=1, source_target_pairs={{0,4},{1,5},{4,8},{5,9},{8,12},{9,13},{12,14},{13,15},{14,10},{15,... | collective-permute-start | bytes 614408 | tf_op jit(solution)/shard_map/ppermute | solution.py:177
  18.5 0.6 %collective-permute-start.10 = (bf16[32,3200]{1,0:T(8,128)(2,1)S(1)}, bf16[32,3200]{1,0:T(8,128)(2,1)S(1)}, u32[]{:S(2)}, u32[]{:S(2)}) collective-permute-start(bf16[32,3200]{1,0:T(8,128)(2,1)S(1)} %collective-permute-done.8.refs_1_), channel_id=1, source_target_pairs={{0,2},{1,3},{4,0},{5,1},{8,4},{9,5},{12,8},{13,9},{14,12},{15,13},... | collective-permute-start | bytes 614408 | tf_op jit(solution)/shard_map/ppermute | solution.py:178
  19.1 1.5 %collective-permute-start.5 = (bf16[32,5120]{1,0:T(8,128)(2,1)S(1)}, bf16[32,5120]{1,0:T(8,128)(2,1)S(1)}, u32[]{:S(2)}, u32[]{:S(2)}) collective-permute-start(bf16[32,5120]{1,0:T(8,128)(2,1)S(1)} %constant_dynamic-update-slice_fusion), channel_id=1, source_target_pairs={{0,16},{1,17},{2,18},{3,19},{4,20},{5,21},{6,22},{7,23},{8,24},{9,... | collective-permute-start | bytes 983048 | tf_op jit(solution)/shard_map/ppermute | solution.py:188
  20.6 2.5 %expert.5 = f32[64,2048]{1,0:T(8,128)S(1)} custom-call(bf16[32,3200]{1,0:T(8,128)(2,1)S(1)} %collective-permute-done.6.refs_0_, bf16[32,3200]{1,0:T(8,128)(2,1)S(1)} %collective-permute-done.8.refs_1_, bf16[1024,512]{1,0:T(8,128)(2,1)S(1)} %get-tuple-element.41.refs_3_.refs_2_.refs_1_, bf16[1024,512]{1,0:T(8,128)(2,1)S(1)} %get-tuple-element.42.refs_4_.refs_3_.refs_2_, ...), custom_call_target="tpu_custom_call" | custom-call | flops 1073741824 | bytes 13520896 | tf_op jit(solution)/shard_map/expert/pallas_call | solution.py:26
  23.2 1.6 %collective-permute-start.9 = (bf16[32,3200]{1,0:T(8,128)(2,1)S(1)}, bf16[32,3200]{1,0:T(8,128)(2,1)S(1)}, u32[]{:S(2)}, u32[]{:S(2)}) collective-permute-start(bf16[32,3200]{1,0:T(8,128)(2,1)S(1)} %collective-permute-done.7.refs_0_), channel_id=1, source_target_pairs={{0,4},{1,5},{4,8},{5,9},{8,12},{9,13},{12,14},{13,15},{14,10},{15,... | collective-permute-start | bytes 614408 | tf_op jit(solution)/shard_map/ppermute | solution.py:257
  24.8 2.6 %expert.6 = bf16[64,2048]{1,0:T(8,128)(2,1)S(1)} custom-call(bf16[32,3200]{1,0:T(8,128)(2,1)S(1)} %collective-permute-done.7.refs_0_, bf16[32,3200]{1,0:T(8,128)(2,1)S(1)} %collective-permute-done.10.refs_1_, bf16[1024,512]{1,0:T(8,128)(2,1)S(1)} %get-tuple-element.41.refs_3_.refs_2_.refs_1_, ...), custom_call_target="tpu_custom_call" | custom-call | flops 1073741824 | bytes 13258752 | tf_op jit(solution)/shard_map/expert/pallas_call | solution.py:26
  27.4 1.6 %collective-permute-start.12 = (bf16[32,2048]{1,0:T(8,128)(2,1)S(1)}, bf16[32,2048]{1,0:T(8,128)(2,1)S(1)}, u32[]{:S(2)}, u32[]{:S(2)}) collective-permute-start(bf16[32,2048]{1,0:T(8,128)(2,1)S(1)} %get-tuple-element.60), channel_id=1, source_target_pairs={{0,4},{1,5},{4,8},{5,9},{8,12},{9,13},{12,14},{13,15},{14,10},{15,... | collective-permute-start | bytes 393224 | tf_op jit(solution)/shard_map/ppermute | solution.py:177
  29.5 0.9 %collective-permute-done.9.refs_0_ = bf16[32,3200]{1,0:T(8,128)(2,1)S(1)} collective-permute-done((bf16[32,3200]{1,0:T(8,128)(2,1)S(1)}, bf16[32,3200]{1,0:T(8,128)(2,1)S(1)}, u32[]{:S(2)}, u32[]{:S(2)}) %collective-permute-start.9) | collective-permute-done | bytes 204832 | tf_op jit(solution)/shard_map/ppermute | solution.py:257
  30.4 2.6 %expert.7 = bf16[32,2048]{1,0:T(8,128)(2,1)S(1)} custom-call(bf16[32,3200]{1,0:T(8,128)(2,1)S(1)} %collective-permute-done.9.refs_0_, bf16[1024,512]{1,0:T(8,128)(2,1)S(1)} %get-tuple-element.41.refs_3_.refs_2_.refs_1_, bf16[1024,512]{1,0:T(8,128)(2,1)S(1)} %get-tuple-element.42.refs_4_.refs_3_.refs_2_, ...), custom_call_target="tpu_custom_call" | custom-call | flops 536870912 | bytes 12922880 | tf_op jit(solution)/shard_map/expert/pallas_call | solution.py:26
  33.0 1.6 %collective-permute-start.14 = (bf16[32,2048]{1,0:T(8,128)(2,1)S(1)}, bf16[32,2048]{1,0:T(8,128)(2,1)S(1)}, u32[]{:S(2)}, u32[]{:S(2)}) collective-permute-start(bf16[32,2048]{1,0:T(8,128)(2,1)S(1)} %fusion), channel_id=1, source_target_pairs={{0,4},{1,5},{4,8},{5,9},{8,12},{9,13},{12,14},{13,15},{14,10},{15,... | collective-permute-start | bytes 393224 | tf_op jit(solution)/shard_map/ppermute | solution.py:177
  35.2 4.5 %collective-permute-start.13 = (bf16[32,2048]{1,0:T(8,128)(2,1)S(1)}, bf16[32,2048]{1,0:T(8,128)(2,1)S(1)}, u32[]{:S(2)}, u32[]{:S(2)}) collective-permute-start(bf16[32,2048]{1,0:T(8,128)(2,1)S(1)} %expert.7), channel_id=1, source_target_pairs={{0,30},{1,31},{4,26},{5,27},{8,22},{9,23},{12,18},{13,19},{14,16},... | collective-permute-start | bytes 393224 | tf_op jit(solution)/shard_map/ppermute | solution.py:188
  40.0 1.7 %collective-permute-start.15 = (bf16[32,2048]{1,0:T(8,128)(2,1)S(1)}, bf16[32,2048]{1,0:T(8,128)(2,1)S(1)}, u32[]{:S(2)}, u32[]{:S(2)}) collective-permute-start(bf16[32,2048]{1,0:T(8,128)(2,1)S(1)} %add_convert_fusion.1), channel_id=1, source_target_pairs={{0,20},{1,21},{4,24},{5,25},{8,28},{9,29},{12,30},{13,31},{14,26},... | collective-permute-start | bytes 393224 | tf_op jit(solution)/shard_map/ppermute | solution.py:188
  41.8 1.3 %collective-permute-start.17 = (bf16[32,2048]{1,0:T(8,128)(2,1)S(1)}, bf16[32,2048]{1,0:T(8,128)(2,1)S(1)}, u32[]{:S(2)}, u32[]{:S(2)}) collective-permute-start(bf16[32,2048]{1,0:T(8,128)(2,1)S(1)} %add_convert_fusion), channel_id=1, source_target_pairs={{0,18},{1,19},{4,16},{5,17},{8,20},{9,21},{12,24},{13,25},{14,28},... | collective-permute-start | bytes 393224 | tf_op jit(solution)/shard_map/ppermute | solution.py:188
  43.1 0.8 %collective-permute-done.13.far = bf16[32,2048]{1,0:T(8,128)(2,1)S(1)} collective-permute-done((bf16[32,2048]{1,0:T(8,128)(2,1)S(1)}, bf16[32,2048]{1,0:T(8,128)(2,1)S(1)}, u32[]{:S(2)}, u32[]{:S(2)}) %collective-permute-start.13) | collective-permute-done | bytes 131104 | tf_op jit(solution)/shard_map/ppermute | solution.py:188
  43.9 2.1 %collective-permute-done.15.below = bf16[32,2048]{1,0:T(8,128)(2,1)S(1)} collective-permute-done((bf16[32,2048]{1,0:T(8,128)(2,1)S(1)}, bf16[32,2048]{1,0:T(8,128)(2,1)S(1)}, u32[]{:S(2)}, u32[]{:S(2)}) %collective-permute-start.15) | collective-permute-done | bytes 131104 | tf_op jit(solution)/shard_map/ppermute | solution.py:188
  46.0 1.8 %collective-permute-done.17.above = bf16[32,2048]{1,0:T(8,128)(2,1)S(1)} collective-permute-done((bf16[32,2048]{1,0:T(8,128)(2,1)S(1)}, bf16[32,2048]{1,0:T(8,128)(2,1)S(1)}, u32[]{:S(2)}, u32[]{:S(2)}) %collective-permute-start.17) | collective-permute-done | bytes 131104 | tf_op jit(solution)/shard_map/ppermute | solution.py:188
  47.7 0.8 %finish.1 = (bf16[32,1024]{1,0:T(8,128)(2,1)}, bf16[32,1024]{1,0:T(8,128)(2,1)}) custom-call(bf16[32,5120]{1,0:T(8,128)(2,1)S(1)} %collective-permute-done.5.home, bf16[32,2048]{1,0:T(8,128)(2,1)S(1)} %collective-permute-done.13.far, bf16[32,2048]{1,0:T(8,128)(2,1)S(1)} %collective-permute-done.15.below, bf16[32,2048]{1,0:T(8,128)(2,1)S(1)} %collective-permute-done.17.above), custom_call_target="tpu_custom_call" | custom-call | bytes 851968 | tf_op jit(solution)/shard_map/finish/pallas_call | solution.py:26
  (40 shorter events, 2.2 us)
Async XLA Ops:
  0.6 5.4 %copy-start.2 = (bf16[1,32,1024]{2,1,0:T(8,128)(2,1)S(1)}, bf16[1,32,1024]{2,1,0:T(8,128)(2,1)}, u32[]{:S(2)}) copy-start(bf16[1,32,1024]{2,1,0:T(8,128)(2,1)} %param.11) | copy-start | bytes 196612
  0.6 5.4 %copy-start.3 = (bf16[1,32,1024]{2,1,0:T(8,128)(2,1)S(1)}, bf16[1,32,1024]{2,1,0:T(8,128)(2,1)}, u32[]{:S(2)}) copy-start(bf16[1,32,1024]{2,1,0:T(8,128)(2,1)} %param.14) | copy-start | bytes 196612
  0.7 5.4 %copy-start.4 = (bf16[1,32,1024]{2,1,0:T(8,128)(2,1)S(1)}, bf16[1,32,1024]{2,1,0:T(8,128)(2,1)}, u32[]{:S(2)}) copy-start(bf16[1,32,1024]{2,1,0:T(8,128)(2,1)} %param.17) | copy-start | bytes 196612
  2.5 8.2 %collective-permute-start = (bf16[32,3200]{1,0:T(8,128)(2,1)}, bf16[32,3200]{1,0:T(8,128)(2,1)S(1)}, u32[]{:S(2)}, u32[]{:S(2)}) collective-permute-start(bf16[32,3200]{1,0:T(8,128)(2,1)} %pack.1.refs_2_), channel_id=1, source_target_pairs={{0,4},{1,5},{4,8},{5,9},{8,12},{9,13},{12,14},{13,15},{14,10},{15,... | collective-permute-start | bytes 614408 | tf_op jit(solution)/shard_map/ppermute | solution.py:177
  5.5 7.0 %collective-permute-start.1 = (bf16[32,3200]{1,0:T(8,128)(2,1)}, bf16[32,3200]{1,0:T(8,128)(2,1)S(1)}, u32[]{:S(2)}, u32[]{:S(2)}) collective-permute-start(bf16[32,3200]{1,0:T(8,128)(2,1)} %pack.1.refs_2_), channel_id=1, source_target_pairs={{0,2},{1,3},{4,0},{5,1},{8,4},{9,5},{12,8},{13,9},{14,12},{15,13},... | collective-permute-start | bytes 614408 | tf_op jit(solution)/shard_map/ppermute | solution.py:178
  5.5 7.2 %collective-permute-start.2 = (bf16[1024,512]{1,0:T(8,128)(2,1)}, bf16[1024,512]{1,0:T(8,128)(2,1)S(1)}, u32[]{:S(2)}, u32[]{:S(2)}) collective-permute-start(bf16[1024,512]{1,0:T(8,128)(2,1)} %bitcast.30), channel_id=1, source_target_pairs={{0,1},{1,0},{2,3},{3,2},{4,5},{5,4},{6,7},{7,6},{8,9},{9,8},{10,11... | collective-permute-start | bytes 3145736 | tf_op jit(solution)/shard_map/ppermute | solution.py:227
  5.5 7.2 %collective-permute-start.3 = (bf16[1024,512]{1,0:T(8,128)(2,1)}, bf16[1024,512]{1,0:T(8,128)(2,1)S(1)}, u32[]{:S(2)}, u32[]{:S(2)}) collective-permute-start(bf16[1024,512]{1,0:T(8,128)(2,1)} %bitcast.32), channel_id=1, source_target_pairs={{0,1},{1,0},{2,3},{3,2},{4,5},{5,4},{6,7},{7,6},{8,9},{9,8},{10,11... | collective-permute-start | bytes 3145736 | tf_op jit(solution)/shard_map/ppermute | solution.py:227
  6.0 6.7 %copy-start = (bf16[32,3200]{1,0:T(8,128)(2,1)S(1)}, bf16[32,3200]{1,0:T(8,128)(2,1)}, u32[]{:S(2)}) copy-start(bf16[32,3200]{1,0:T(8,128)(2,1)} %pack.1.refs_2_) | copy-start | bytes 614404
  6.0 6.7 %collective-permute-start.4 = (bf16[512,1024]{1,0:T(8,128)(2,1)}, bf16[512,1024]{1,0:T(8,128)(2,1)S(1)}, u32[]{:S(2)}, u32[]{:S(2)}) collective-permute-start(bf16[512,1024]{1,0:T(8,128)(2,1)} %bitcast.34), channel_id=1, source_target_pairs={{0,1},{1,0},{2,3},{3,2},{4,5},{5,4},{6,7},{7,6},{8,9},{9,8},{10,11... | collective-permute-start | bytes 3145736 | tf_op jit(solution)/shard_map/ppermute | solution.py:227
  10.7 2.1 %copy-start.1 = (f32[1,1024]{1,0:T(1,128)S(1)}, f32[1,1024]{1,0:T(1,128)}, u32[]{:S(2)}) copy-start(f32[1,1024]{1,0:T(1,128)} %refs_13_.1) | copy-start | bytes 12292
  10.7 6.3 %collective-permute-start.6 = (bf16[32,3200]{1,0:T(8,128)(2,1)S(1)}, bf16[32,3200]{1,0:T(8,128)(2,1)S(1)}, u32[]{:S(2)}, u32[]{:S(2)}) collective-permute-start(bf16[32,3200]{1,0:T(8,128)(2,1)S(1)} %collective-permute-done.refs_0_), channel_id=1, source_target_pairs={{0,4},{1,5},{4,8},{5,9},{8,12},{9,13},{12,14},{13,15},{14,10},{15,... | collective-permute-start | bytes 614408 | tf_op jit(solution)/shard_map/ppermute | solution.py:177
  12.5 6.0 %collective-permute-start.8 = (bf16[32,3200]{1,0:T(8,128)(2,1)S(1)}, bf16[32,3200]{1,0:T(8,128)(2,1)S(1)}, u32[]{:S(2)}, u32[]{:S(2)}) collective-permute-start(bf16[32,3200]{1,0:T(8,128)(2,1)S(1)} %collective-permute-done.1.refs_1_), channel_id=1, source_target_pairs={{0,2},{1,3},{4,0},{5,1},{8,4},{9,5},{12,8},{13,9},{14,12},{15,13},... | collective-permute-start | bytes 614408 | tf_op jit(solution)/shard_map/ppermute | solution.py:178
  17.0 6.2 %collective-permute-start.7 = (bf16[32,3200]{1,0:T(8,128)(2,1)S(1)}, bf16[32,3200]{1,0:T(8,128)(2,1)S(1)}, u32[]{:S(2)}, u32[]{:S(2)}) collective-permute-start(bf16[32,3200]{1,0:T(8,128)(2,1)S(1)} %collective-permute-done.6.refs_0_), channel_id=1, source_target_pairs={{0,4},{1,5},{4,8},{5,9},{8,12},{9,13},{12,14},{13,15},{14,10},{15,... | collective-permute-start | bytes 614408 | tf_op jit(solution)/shard_map/ppermute | solution.py:177
  18.5 6.3 %collective-permute-start.10 = (bf16[32,3200]{1,0:T(8,128)(2,1)S(1)}, bf16[32,3200]{1,0:T(8,128)(2,1)S(1)}, u32[]{:S(2)}, u32[]{:S(2)}) collective-permute-start(bf16[32,3200]{1,0:T(8,128)(2,1)S(1)} %collective-permute-done.8.refs_1_), channel_id=1, source_target_pairs={{0,2},{1,3},{4,0},{5,1},{8,4},{9,5},{12,8},{13,9},{14,12},{15,13},... | collective-permute-start | bytes 614408 | tf_op jit(solution)/shard_map/ppermute | solution.py:178
  19.1 8.3 %collective-permute-start.5 = (bf16[32,5120]{1,0:T(8,128)(2,1)S(1)}, bf16[32,5120]{1,0:T(8,128)(2,1)S(1)}, u32[]{:S(2)}, u32[]{:S(2)}) collective-permute-start(bf16[32,5120]{1,0:T(8,128)(2,1)S(1)} %constant_dynamic-update-slice_fusion), channel_id=1, source_target_pairs={{0,16},{1,17},{2,18},{3,19},{4,20},{5,21},{6,22},{7,23},{8,24},{9,... | collective-permute-start | bytes 983048 | tf_op jit(solution)/shard_map/ppermute | solution.py:188
  23.2 7.2 %collective-permute-start.9 = (bf16[32,3200]{1,0:T(8,128)(2,1)S(1)}, bf16[32,3200]{1,0:T(8,128)(2,1)S(1)}, u32[]{:S(2)}, u32[]{:S(2)}) collective-permute-start(bf16[32,3200]{1,0:T(8,128)(2,1)S(1)} %collective-permute-done.7.refs_0_), channel_id=1, source_target_pairs={{0,4},{1,5},{4,8},{5,9},{8,12},{9,13},{12,14},{13,15},{14,10},{15,... | collective-permute-start | bytes 614408 | tf_op jit(solution)/shard_map/ppermute | solution.py:257
  27.4 5.6 %collective-permute-start.12 = (bf16[32,2048]{1,0:T(8,128)(2,1)S(1)}, bf16[32,2048]{1,0:T(8,128)(2,1)S(1)}, u32[]{:S(2)}, u32[]{:S(2)}) collective-permute-start(bf16[32,2048]{1,0:T(8,128)(2,1)S(1)} %get-tuple-element.60), channel_id=1, source_target_pairs={{0,4},{1,5},{4,8},{5,9},{8,12},{9,13},{12,14},{13,15},{14,10},{15,... | collective-permute-start | bytes 393224 | tf_op jit(solution)/shard_map/ppermute | solution.py:177
  29.0 5.6 %collective-permute-start.11 = (bf16[32,2048]{1,0:T(8,128)(2,1)S(1)}, bf16[32,2048]{1,0:T(8,128)(2,1)S(1)}, u32[]{:S(2)}, u32[]{:S(2)}) collective-permute-start(bf16[32,2048]{1,0:T(8,128)(2,1)S(1)} %get-tuple-element.68), channel_id=1, source_target_pairs={{0,2},{1,3},{4,0},{5,1},{8,4},{9,5},{12,8},{13,9},{14,12},{15,13},... | collective-permute-start | bytes 393224 | tf_op jit(solution)/shard_map/ppermute | solution.py:178
  33.0 7.0 %collective-permute-start.14 = (bf16[32,2048]{1,0:T(8,128)(2,1)S(1)}, bf16[32,2048]{1,0:T(8,128)(2,1)S(1)}, u32[]{:S(2)}, u32[]{:S(2)}) collective-permute-start(bf16[32,2048]{1,0:T(8,128)(2,1)S(1)} %fusion), channel_id=1, source_target_pairs={{0,4},{1,5},{4,8},{5,9},{8,12},{9,13},{12,14},{13,15},{14,10},{15,... | collective-permute-start | bytes 393224 | tf_op jit(solution)/shard_map/ppermute | solution.py:177
  34.7 7.1 %collective-permute-start.16 = (bf16[32,2048]{1,0:T(8,128)(2,1)S(1)}, bf16[32,2048]{1,0:T(8,128)(2,1)S(1)}, u32[]{:S(2)}, u32[]{:S(2)}) collective-permute-start(bf16[32,2048]{1,0:T(8,128)(2,1)S(1)} %fusion.1), channel_id=1, source_target_pairs={{0,2},{1,3},{4,0},{5,1},{8,4},{9,5},{12,8},{13,9},{14,12},{15,13},... | collective-permute-start | bytes 393224 | tf_op jit(solution)/shard_map/ppermute | solution.py:178
  35.2 8.7 %collective-permute-start.13 = (bf16[32,2048]{1,0:T(8,128)(2,1)S(1)}, bf16[32,2048]{1,0:T(8,128)(2,1)S(1)}, u32[]{:S(2)}, u32[]{:S(2)}) collective-permute-start(bf16[32,2048]{1,0:T(8,128)(2,1)S(1)} %expert.7), channel_id=1, source_target_pairs={{0,30},{1,31},{4,26},{5,27},{8,22},{9,23},{12,18},{13,19},{14,16},... | collective-permute-start | bytes 393224 | tf_op jit(solution)/shard_map/ppermute | solution.py:188
  40.0 5.9 %collective-permute-start.15 = (bf16[32,2048]{1,0:T(8,128)(2,1)S(1)}, bf16[32,2048]{1,0:T(8,128)(2,1)S(1)}, u32[]{:S(2)}, u32[]{:S(2)}) collective-permute-start(bf16[32,2048]{1,0:T(8,128)(2,1)S(1)} %add_convert_fusion.1), channel_id=1, source_target_pairs={{0,20},{1,21},{4,24},{5,25},{8,28},{9,29},{12,30},{13,31},{14,26},... | collective-permute-start | bytes 393224 | tf_op jit(solution)/shard_map/ppermute | solution.py:188
  41.8 5.9 %collective-permute-start.17 = (bf16[32,2048]{1,0:T(8,128)(2,1)S(1)}, bf16[32,2048]{1,0:T(8,128)(2,1)S(1)}, u32[]{:S(2)}, u32[]{:S(2)}) collective-permute-start(bf16[32,2048]{1,0:T(8,128)(2,1)S(1)} %add_convert_fusion), channel_id=1, source_target_pairs={{0,18},{1,19},{4,16},{5,17},{8,20},{9,21},{12,24},{13,25},{14,28},... | collective-permute-start | bytes 393224 | tf_op jit(solution)/shard_map/ppermute | solution.py:188
